TPU v7x, 32 devices: a whole 2x2x4 slice. The times are simulated.
32 devices in a mesh: dp: 8 (over y, x, core), fsdp: 4 (over z).
Axes of the slice: x: 2, y: 2, z: 4, core: 2. Of those that a mesh axis runs over, the one named last changes fastest.
Arguments:
- layer_input: bfloat16 [32, 1024, 1024], P(('dp', 'fsdp')), may hold values from -6 to 6
- qkv_weight: bfloat16 [1024, 3072], P('fsdp'), may hold values from -0.1875 to 0.1875
- query_value_bias: bfloat16 [2, 1024], P(None, 'fsdp'), may hold values from -1.796875 to 1.796875
- out_weight: bfloat16 [1024, 1024], P('fsdp'), may hold values from -0.1875 to 0.1875
- out_bias: bfloat16 [1024], P('fsdp'), may hold values from -3 to 3
- up_weight: bfloat16 [1024, 4096], P('fsdp'), may hold values from -0.1875 to 0.1875
- up_bias: bfloat16 [4096], P('fsdp'), may hold values from -3 to 3
- down_weight: bfloat16 [4096, 1024], P('fsdp'), may hold values from -0.09375 to 0.09375
- down_bias: bfloat16 [1024], P('fsdp'), may hold values from -3 to 3
- norm_gain: bfloat16 [4, 1024], P(None, 'fsdp'), may hold values from 0.5 to 1.5
- norm_shift: bfloat16 [4, 1024], P(None, 'fsdp'), may hold values from -1.1953125 to 1.1953125
- doc_lengths: int32 [32, 8], P(('dp', 'fsdp')), may hold values from 0 to 1024, as said below
- cotangent: bfloat16 [32, 1024, 1024], P(('dp', 'fsdp')), may hold values from -6 to 6
Outputs:
- layer_out: bfloat16 [32, 1024, 1024], P(('dp', 'fsdp'))
- grad_input: float32 [32, 1024, 1024], P(('dp', 'fsdp'))
- qkv_grad: float32 [1024, 3072], P('fsdp')
- query_value_grad: float32 [2, 1024], P(None, 'fsdp')
- out_weight_grad: float32 [1024, 1024], P('fsdp')
- out_bias_grad: float32 [1024], P('fsdp')
- up_weight_grad: float32 [1024, 4096], P('fsdp')
- up_bias_grad: float32 [4096], P('fsdp')
- down_weight_grad: float32 [4096, 1024], P('fsdp')
- down_bias_grad: float32 [1024], P('fsdp')
- gain_grad: float32 [4, 1024], P(None, 'fsdp')
- shift_grad: float32 [4, 1024], P(None, 'fsdp')
Inputs may be any that keep to these rules, and one draw needn't show every extreme that they name: `doc_lengths`: each row's lengths sum to between 512 and 1024; a zero marks an unused slot; in every draw some row holds a single document of 1024 tokens.
All inputs are finite; a program needn't handle non-finite values.
Results may differ from a plain program's by a relative error of at most 0.012.
Values may be sent and summed in bfloat16 or wider, within the bound.
No kernel may reach another device: no remote copies, remote signals or barrier semaphores. Data moves between devices by JAX's collectives and lax.ppermute only.
A program may use at most 256 MiB of HBM per device.

v0:
```python
import math

import jax
import jax.numpy as jnp
from jax import lax
from jax.sharding import PartitionSpec as P

HEADS = 16
HEAD_DIM = 64


relax_alpha = 32.0
norm_eps = 1e-05


def normalize(values, gain, shift):
    centre = values - jnp.mean(values, axis=-1, keepdims=True)
    spread = jnp.mean(centre * centre, axis=-1, keepdims=True)
    return centre * lax.rsqrt(spread + norm_eps) * gain + shift


def gelu_tanh(values):
    return jax.nn.gelu(values, approximate=True)


def document_ids(lengths, length):
    doc_ends = jnp.cumsum(lengths)
    positions = jnp.arange(length, dtype=jnp.int32)
    doc_index = jnp.sum((positions[:, None] >= doc_ends[None, :]).astype(jnp.int32), axis=1)
    return (doc_index, positions < doc_ends[-1])


def split_heads(tensor, groups):
    length, head_count, head_size = tensor.shape
    return tensor.reshape(length, groups, head_count // groups, head_size).transpose(1, 0, 2, 3)


def merge_heads(tensor):
    groups, length, group_heads, head_size = tensor.shape
    return tensor.transpose(1, 0, 2, 3).reshape(length, groups * group_heads * head_size)


def block_scores(query_block, offset, keys, doc_index):
    block_rows = query_block.shape[0]
    raw_scores = jnp.einsum("qhd,khd->hqk", query_block, keys, preferred_element_type=jnp.float32)
    query_pos = offset + jnp.arange(block_rows, dtype=jnp.int32)
    key_pos = jnp.arange(keys.shape[0], dtype=jnp.int32)
    query_docs = lax.dynamic_slice_in_dim(doc_index, offset, block_rows)
    allowed = (key_pos[None, :] <= query_pos[:, None]) & (query_docs[:, None] == doc_index[None, :])
    score_scale = 1.0 / (relax_alpha * math.sqrt(query_block.shape[-1]))
    return jnp.where(allowed[None], raw_scores * score_scale, -1000000000.0)


def layout(length, head_count):
    groups = head_count // min(4, head_count)
    block_rows = min(512, length)
    block_count = length // block_rows
    offsets = jnp.arange(block_count, dtype=jnp.int32) * block_rows
    return (groups, block_rows, block_count, offsets)


def attend_row(queries, keys, values, doc_index):
    length, head_count, head_size = queries.shape
    groups, block_rows, block_count, offsets = layout(length, head_count)

    def one_group(element):
        group_q, group_k, group_v = element

        def one_block(entry):
            query_block, offset = entry
            scores = block_scores(query_block, offset, group_k, doc_index)
            row_top = jnp.max(scores, axis=-1)
            exp_scores = jnp.exp(relax_alpha * (scores - row_top[..., None]))
            row_total = jnp.sum(exp_scores, axis=-1)
            attn_probs = exp_scores / row_total[..., None]
            result = jnp.einsum(
                "hqk,khd->qhd",
                attn_probs.astype(jnp.bfloat16),
                group_v,
                preferred_element_type=jnp.float32,
            )
            return (result, row_top, row_total)

        query_blocks = group_q.reshape(block_count, block_rows, group_q.shape[1], head_size)
        return lax.map(one_block, (query_blocks, offsets))

    result, row_top, row_total = lax.map(
        one_group,
        (split_heads(queries, groups), split_heads(keys, groups), split_heads(values, groups)),
    )
    result = result.reshape(groups, length, head_count // groups, head_size)
    return (merge_heads(result), row_top, row_total)


def attend_row_back(queries, keys, values, doc_index, grad_rows, top_rows, total_rows):
    length, head_count, head_size = queries.shape
    groups, block_rows, block_count, offsets = layout(length, head_count)
    grad_scale = relax_alpha / (relax_alpha * math.sqrt(head_size))

    def one_group(element):
        group_q, group_k, group_v, group_grad, group_top, group_total = element
        group_heads = group_q.shape[1]

        def one_block(running, entry):
            grad_keys, grad_values = running
            query_block, grad_block, offset, block_top, block_total = entry
            scores = block_scores(query_block, offset, group_k, doc_index)
            attn_probs = (
                jnp.exp(relax_alpha * (scores - block_top[..., None])) / block_total[..., None]
            )
            grad_values = grad_values + jnp.einsum(
                "hqk,qhd->khd",
                attn_probs.astype(jnp.bfloat16),
                grad_block,
                preferred_element_type=jnp.float32,
            )
            grad_probs = jnp.einsum(
                "qhd,khd->hqk", grad_block, group_v, preferred_element_type=jnp.float32
            )
            inner = jnp.sum(attn_probs * grad_probs, axis=-1, keepdims=True)
            grad_scores = (grad_scale * attn_probs * (grad_probs - inner)).astype(jnp.bfloat16)
            grad_query = jnp.einsum(
                "hqk,khd->qhd", grad_scores, group_k, preferred_element_type=jnp.float32
            )
            grad_keys = grad_keys + jnp.einsum(
                "hqk,qhd->khd", grad_scores, query_block, preferred_element_type=jnp.float32
            )
            return ((grad_keys, grad_values), grad_query)

        blank_grad = jnp.zeros(group_k.shape, jnp.float32)
        query_blocks = group_q.reshape(block_count, block_rows, group_heads, head_size)
        grad_blocks = group_grad.reshape(block_count, block_rows, group_heads, head_size)
        (grad_keys, grad_values), grad_query = lax.scan(
            one_block,
            (blank_grad, blank_grad),
            (query_blocks, grad_blocks, offsets, group_top, group_total),
        )
        return (grad_query.reshape(length, group_heads, head_size), grad_keys, grad_values)

    grad_query, grad_keys, grad_values = lax.map(
        one_group,
        (
            split_heads(queries, groups),
            split_heads(keys, groups),
            split_heads(values, groups),
            split_heads(grad_rows, groups),
            top_rows,
            total_rows,
        ),
    )
    return (merge_heads(grad_query), merge_heads(grad_keys), merge_heads(grad_values))


def regroup(grad_arr, axis_dim, outer_count, inner_count):
    leading = jnp.moveaxis(grad_arr, axis_dim, 0)
    full_shape = leading.shape
    blocks = leading.reshape(
        (outer_count, inner_count, full_shape[0] // (outer_count * inner_count)) + full_shape[1:]
    )
    swapped = jnp.swapaxes(blocks, 0, 1).reshape(full_shape)
    return jnp.moveaxis(swapped, 0, axis_dim)


def on_device(
    layer_input,
    qkv_weight,
    query_value_bias,
    out_weight,
    out_bias,
    up_weight,
    up_bias,
    down_weight,
    down_bias,
    norm_gain,
    norm_shift,
    doc_lengths,
    cotangent,
):
    gathered = (
        lax.all_gather(qkv_weight, "fsdp", axis=0, tiled=True),
        lax.all_gather(query_value_bias, "fsdp", axis=1, tiled=True),
        lax.all_gather(out_weight, "fsdp", axis=0, tiled=True),
        lax.all_gather(out_bias, "fsdp", axis=0, tiled=True),
        lax.all_gather(up_weight, "fsdp", axis=0, tiled=True),
        lax.all_gather(up_bias, "fsdp", axis=0, tiled=True),
        lax.all_gather(down_weight, "fsdp", axis=0, tiled=True),
        lax.all_gather(down_bias, "fsdp", axis=0, tiled=True),
        lax.all_gather(norm_gain, "fsdp", axis=1, tiled=True),
        lax.all_gather(norm_shift, "fsdp", axis=1, tiled=True),
    )
    (
        all_qkv,
        all_qv_bias,
        all_out,
        all_out_bias,
        all_up,
        all_up_bias,
        all_down,
        all_down_bias,
        all_gain,
        all_shift,
    ) = gathered
    row_count, length, model_width = layer_input.shape
    tokens = row_count * length
    gains = all_gain.astype(jnp.float32)
    shifts = all_shift.astype(jnp.float32)
    doc_index, live_mask = jax.vmap(lambda lengths: document_ids(lengths, length))(doc_lengths)
    resid_in = layer_input.reshape(tokens, model_width).astype(jnp.float32)
    normed_one = normalize(resid_in, gains[0], shifts[0]).astype(jnp.bfloat16)
    qkv_shift = jnp.concatenate(
        [
            all_qv_bias[0].astype(jnp.float32),
            jnp.zeros((model_width,), jnp.float32),
            all_qv_bias[1].astype(jnp.float32),
        ]
    )
    packed = (jnp.dot(normed_one, all_qkv, preferred_element_type=jnp.float32) + qkv_shift).astype(
        jnp.bfloat16
    )
    packed_rows = packed.reshape(row_count, length, 3, HEADS, HEAD_DIM)

    def forward_row(element):
        pieces, row_docs = element
        return attend_row(pieces[:, 0], pieces[:, 1], pieces[:, 2], row_docs)

    attended, row_top, row_total = lax.map(forward_row, (packed_rows, doc_index))
    attended = attended.reshape(tokens, model_width).astype(jnp.bfloat16)
    mixed_pre = jnp.dot(
        attended, all_out, preferred_element_type=jnp.float32
    ) + all_out_bias.astype(jnp.float32)
    resid_mid = resid_in + normalize(mixed_pre, gains[1], shifts[1])
    normed_two = normalize(resid_mid, gains[2], shifts[2]).astype(jnp.bfloat16)
    hidden_pre = jnp.dot(
        normed_two, all_up, preferred_element_type=jnp.float32
    ) + all_up_bias.astype(jnp.float32)
    hidden_act = gelu_tanh(hidden_pre).astype(jnp.bfloat16)
    ffn_pre = jnp.dot(
        hidden_act, all_down, preferred_element_type=jnp.float32
    ) + all_down_bias.astype(jnp.float32)
    layer_out = (
        (resid_mid + normalize(ffn_pre, gains[3], shifts[3]))
        .astype(jnp.bfloat16)
        .reshape(row_count, length, model_width)
    )
    again = (
        lax.all_gather(qkv_weight, "fsdp", axis=0, tiled=True),
        lax.all_gather(out_weight, "fsdp", axis=0, tiled=True),
        lax.all_gather(up_weight, "fsdp", axis=0, tiled=True),
        lax.all_gather(down_weight, "fsdp", axis=0, tiled=True),
        lax.all_gather(norm_gain, "fsdp", axis=1, tiled=True),
    )
    back_qkv, back_out, back_up, back_down = (again[0], again[1], again[2], again[3])
    back_gain = again[4].astype(jnp.float32)
    out_grad = cotangent.reshape(tokens, model_width).astype(jnp.float32) * live_mask.reshape(
        tokens, 1
    ).astype(jnp.float32)
    _, norm_back = jax.vjp(normalize, ffn_pre, back_gain[3], shifts[3])
    grad_ffn, gain_three, shift_three = norm_back(out_grad)
    grad_ffn = grad_ffn.astype(jnp.bfloat16)
    down_weight_grad = jnp.einsum(
        "nf,nd->fd", hidden_act, grad_ffn, preferred_element_type=jnp.float32
    )
    down_bias_grad = jnp.sum(grad_ffn.astype(jnp.float32), axis=0)
    grad_act = jnp.einsum("nd,fd->nf", grad_ffn, back_down, preferred_element_type=jnp.float32)
    _, gelu_back = jax.vjp(gelu_tanh, hidden_pre)
    grad_hidden = gelu_back(grad_act)[0].astype(jnp.bfloat16)
    up_weight_grad = jnp.einsum(
        "nd,nf->df", normed_two, grad_hidden, preferred_element_type=jnp.float32
    )
    up_bias_grad = jnp.sum(grad_hidden.astype(jnp.float32), axis=0)
    grad_normed = jnp.einsum("nf,df->nd", grad_hidden, back_up, preferred_element_type=jnp.float32)
    _, norm_back = jax.vjp(normalize, resid_mid, back_gain[2], shifts[2])
    grad_mid, gain_two, shift_two = norm_back(grad_normed)
    grad_mid = grad_mid + out_grad
    _, norm_back = jax.vjp(normalize, mixed_pre, back_gain[1], shifts[1])
    grad_mixed, gain_one, shift_one = norm_back(grad_mid)
    grad_mixed = grad_mixed.astype(jnp.bfloat16)
    out_weight_grad = jnp.einsum(
        "nd,ne->de", attended, grad_mixed, preferred_element_type=jnp.float32
    )
    out_bias_grad = jnp.sum(grad_mixed.astype(jnp.float32), axis=0)
    grad_attended = jnp.einsum(
        "ne,de->nd", grad_mixed, back_out, preferred_element_type=jnp.float32
    ).astype(jnp.bfloat16)

    def backward_row(element):
        pieces, row_docs, grad_rows, top_rows, total_rows = element
        return attend_row_back(
            pieces[:, 0], pieces[:, 1], pieces[:, 2], row_docs, grad_rows, top_rows, total_rows
        )

    grad_query, grad_keys, grad_values = lax.map(
        backward_row,
        (
            packed_rows,
            doc_index,
            grad_attended.reshape(row_count, length, HEADS, HEAD_DIM),
            row_top,
            row_total,
        ),
    )
    grad_packed = (
        jnp.concatenate([grad_query, grad_keys, grad_values], axis=-1)
        .reshape(tokens, 3 * model_width)
        .astype(jnp.bfloat16)
    )
    qkv_grad = jnp.einsum("nd,ne->de", normed_one, grad_packed, preferred_element_type=jnp.float32)
    packed_sums = jnp.sum(grad_packed.astype(jnp.float32), axis=0)
    query_value_grad = jnp.stack([packed_sums[:model_width], packed_sums[2 * model_width :]])
    grad_normed_one = jnp.einsum(
        "ne,de->nd", grad_packed, back_qkv, preferred_element_type=jnp.float32
    )
    _, norm_back = jax.vjp(normalize, resid_in, back_gain[0], shifts[0])
    grad_first, gain_zero, shift_zero = norm_back(grad_normed_one)
    grad_input = (grad_mid + grad_first).reshape(row_count, length, model_width)
    gain_grad = jnp.stack([gain_zero, gain_one, gain_two, gain_three])
    shift_grad = jnp.stack([shift_zero, shift_one, shift_two, shift_three])
    local_grads = (
        qkv_grad,
        query_value_grad,
        out_weight_grad,
        out_bias_grad,
        up_weight_grad,
        up_bias_grad,
        down_weight_grad,
        down_bias_grad,
        gain_grad,
        shift_grad,
    )
    grad_dims = (0, 1, 0, 0, 0, 0, 0, 0, 1, 1)
    outer_count = lax.axis_size("fsdp")
    inner_count = lax.axis_size("dp")
    moved = [
        regroup(grad_arr, grad_dim, outer_count, inner_count)
        for grad_arr, grad_dim in zip(local_grads, grad_dims)
    ]
    pieces = (
        lax.psum_scatter(moved[0], ("dp", "fsdp"), scatter_dimension=0, tiled=True),
        lax.psum_scatter(moved[1], ("dp", "fsdp"), scatter_dimension=1, tiled=True),
        lax.psum_scatter(moved[2], ("dp", "fsdp"), scatter_dimension=0, tiled=True),
        lax.psum_scatter(moved[3], ("dp", "fsdp"), scatter_dimension=0, tiled=True),
        lax.psum_scatter(moved[4], ("dp", "fsdp"), scatter_dimension=0, tiled=True),
        lax.psum_scatter(moved[5], ("dp", "fsdp"), scatter_dimension=0, tiled=True),
        lax.psum_scatter(moved[6], ("dp", "fsdp"), scatter_dimension=0, tiled=True),
        lax.psum_scatter(moved[7], ("dp", "fsdp"), scatter_dimension=0, tiled=True),
        lax.psum_scatter(moved[8], ("dp", "fsdp"), scatter_dimension=1, tiled=True),
        lax.psum_scatter(moved[9], ("dp", "fsdp"), scatter_dimension=1, tiled=True),
    )
    summed = (
        lax.all_gather(pieces[0].astype(jnp.bfloat16), "dp", axis=0, tiled=True).astype(
            jnp.float32
        ),
        lax.all_gather(pieces[1].astype(jnp.bfloat16), "dp", axis=1, tiled=True).astype(
            jnp.float32
        ),
        lax.all_gather(pieces[2].astype(jnp.bfloat16), "dp", axis=0, tiled=True).astype(
            jnp.float32
        ),
        lax.all_gather(pieces[3].astype(jnp.bfloat16), "dp", axis=0, tiled=True).astype(
            jnp.float32
        ),
        lax.all_gather(pieces[4].astype(jnp.bfloat16), "dp", axis=0, tiled=True).astype(
            jnp.float32
        ),
        lax.all_gather(pieces[5].astype(jnp.bfloat16), "dp", axis=0, tiled=True).astype(
            jnp.float32
        ),
        lax.all_gather(pieces[6].astype(jnp.bfloat16), "dp", axis=0, tiled=True).astype(
            jnp.float32
        ),
        lax.all_gather(pieces[7].astype(jnp.bfloat16), "dp", axis=0, tiled=True).astype(
            jnp.float32
        ),
        lax.all_gather(pieces[8].astype(jnp.bfloat16), "dp", axis=1, tiled=True).astype(
            jnp.float32
        ),
        lax.all_gather(pieces[9].astype(jnp.bfloat16), "dp", axis=1, tiled=True).astype(
            jnp.float32
        ),
    )
    return (
        layer_out,
        grad_input,
        summed[0],
        summed[1],
        summed[2],
        summed[3],
        summed[4],
        summed[5],
        summed[6],
        summed[7],
        summed[8],
        summed[9],
    )


def solution(mesh):
    placed = (
        P(("dp", "fsdp"), None, None),
        P("fsdp", None),
        P(None, "fsdp"),
        P("fsdp", None),
        P("fsdp"),
        P("fsdp", None),
        P("fsdp"),
        P("fsdp", None),
        P("fsdp"),
        P(None, "fsdp"),
        P(None, "fsdp"),
        P(("dp", "fsdp"), None),
        P(("dp", "fsdp"), None, None),
    )
    return jax.shard_map(
        on_device,
        mesh=mesh,
        in_specs=placed,
        out_specs=(
            P(("dp", "fsdp"), None, None),
            P(("dp", "fsdp"), None, None),
            P("fsdp", None),
            P(None, "fsdp"),
            P("fsdp", None),
            P("fsdp"),
            P("fsdp", None),
            P("fsdp"),
            P("fsdp", None),
            P("fsdp"),
            P(None, "fsdp"),
            P(None, "fsdp"),
        ),
        check_vma=False,
    )
```

profile of v0, /device:TPU:0, one launch (start us, length us, event | category | flops | bytes accessed | tf_op | source)
XLA Modules:
  0.0 2356.3 jit_solution(13020822991524247044)
XLA Ops:
  14.1 13.7 all_gather.65
  28.4 16.4 all_gather.66
  45.3 7.9 all_gather.68
  54.1 14.7 all-gather
  69.4 17.5 all_gather.72
  87.5 8.3 all-gather.1
  103.7 24.3 %all-gather.14.cloned.1.call-done = bf16[1024,3072]{1,0:T(8,128)(2,1)} async-done(((bf16[256,3072]{1,0:T(8,128)(2,1)}), bf16[1024,3072]{1,0:T(8,128)(2,1)}) %all-gather.14.cloned.1.call-update) | async-done | bytes 6291472 | tf_op jit(solution)/shard_map/all_gather | solution.py:180
  128.0 11.4 add_convert_fusion
  139.5 8.6 copy.180
  153.9 109.8 %while.84 = (s32[]{:T(128)}, bf16[4,2,512,4,64]{2,4,3,1,0:T(8,128)(2,1)}, f32[4,2,4,512]{3,2,1,0:T(4,128)S(1)}, f32[4,2,4,512]{3,2,1,0:T(4,128)S(1)}, bf16[4,102...) while((s32[]{:T(128)}, ...), condition=%wide.region_9.10_spmd.clone, body=%wide.region_4.9_spmd.clone.sunk | while | flops 567800320 | bytes 35543988 | solution.py:87
  156.8 23.6 %while.87 = (s32[]{:T(128)}, bf16[2,512,4,64]{1,3,2,0:T(8,128)(2,1)S(1)}, f32[2,4,512]{2,1,0:T(4,128)S(1)}, f32[2,4,512]{2,1,0:T(4,128)S(1)}, s32[2]{0:T(128)S(1...) while((s32[]{:T(128)}, ...), condition=%wide.region_8.8_spmd, body=%wide.region_5.7_spmd.sunk | while | flops 567800320 | bytes 29186232 | solution.py:85
  184.4 23.6 %while.87 = (s32[]{:T(128)}, bf16[2,512,4,64]{1,3,2,0:T(8,128)(2,1)S(1)}, f32[2,4,512]{2,1,0:T(4,128)S(1)}, f32[2,4,512]{2,1,0:T(4,128)S(1)}, s32[2]{0:T(128)S(1...) while((s32[]{:T(128)}, ...), condition=%wide.region_8.8_spmd, body=%wide.region_5.7_spmd.sunk | while | flops 567800320 | bytes 29186232 | solution.py:85
  211.7 23.6 %while.87 = (s32[]{:T(128)}, bf16[2,512,4,64]{1,3,2,0:T(8,128)(2,1)S(1)}, f32[2,4,512]{2,1,0:T(4,128)S(1)}, f32[2,4,512]{2,1,0:T(4,128)S(1)}, s32[2]{0:T(128)S(1...) while((s32[]{:T(128)}, ...), condition=%wide.region_8.8_spmd, body=%wide.region_5.7_spmd.sunk | while | flops 567800320 | bytes 29186232 | solution.py:85
  239.1 23.6 %while.87 = (s32[]{:T(128)}, bf16[2,512,4,64]{1,3,2,0:T(8,128)(2,1)S(1)}, f32[2,4,512]{2,1,0:T(4,128)S(1)}, f32[2,4,512]{2,1,0:T(4,128)S(1)}, s32[2]{0:T(128)S(1...) while((s32[]{:T(128)}, ...), condition=%wide.region_8.8_spmd, body=%wide.region_5.7_spmd.sunk | while | flops 567800320 | bytes 29186232 | solution.py:85
  277.6 46.3 %all-gather.18.cloned.1.call-done = bf16[1024,4096]{1,0:T(8,128)(2,1)} async-done(((bf16[256,4096]{1,0:T(8,128)(2,1)}), bf16[1024,4096]{1,0:T(8,128)(2,1)}) %all-gather.18.cloned.1.call-update) | async-done | bytes 8388624 | tf_op jit(solution)/shard_map/all_gather | solution.py:184
  323.9 22.1 multiply_convert_fusion.1
  346.0 127.2 %all-gather.20.cloned.1.call-done = bf16[4096,1024]{1,0:T(8,128)(2,1)} async-done(((bf16[1024,1024]{1,0:T(8,128)(2,1)}), bf16[4096,1024]{1,0:T(8,128)(2,1)}) %all-gather.20.cloned.1.call-update) | async-done | bytes 8388624 | tf_op jit(solution)/shard_map/all_gather | solution.py:186
  473.2 14.4 add_reduce_fusion
  497.3 26.9 %convert_reduce_fusion = (f32[4096]{0:T(1024)}, bf16[1024,4096]{1,0:T(8,128)(2,1)}) fusion(f32[1024,4096]{1,0:T(8,128)} %get-tuple-element.772, f32[4096]{0:T(1024)S(1)} %copy-done.49, bf16[1024,1024]{0,1:T(8,128)(2,1)} %get-tuple-element.729, bf16[4096,1024]{1,0:T(8,128)(2,1)} %all-gather.20.cloned.1.call-done), kind=kOutput, calls=%fused_computation.77 | convolution fusion | flops 8686399488 | bytes 35684352 | tf_op jit(solution)/shard_map/nd,fd->nf/dot_general | solution.py:264
  524.2 15.8 fusion.98
  566.0 226.4 %while.86 = (s32[]{:T(128)}, bf16[4,1024,4,64]{1,3,2,0:T(8,128)(2,1)}, bf16[4,1024,4,64]{1,3,2,0:T(8,128)(2,1)}, bf16[4,1024,4,64]{1,3,2,0:T(8,128)(2,1)}, bf16[...) while((s32[]{:T(128)}, ...), condition=%wide.region_26.27_spmd.clone, body=%wide.region_22.26_spmd.clone.sunk | while | flops 1369963008 | bytes 177357520 | solution.py:140
  573.3 46.3 %while.88 = (s32[]{:T(128)}, f32[1024,4,64]{0,2,1:T(8,128)S(1)}, f32[1024,4,64]{0,2,1:T(8,128)S(1)}, bf16[2,512,4,64]{1,3,2,0:T(8,128)(2,1)}, bf16[2,512,4,64]{1...) while((s32[]{:T(128)}, f32[1024,4,64]{0,2,1:T(8,128)S(1)}, ...), condition=%wide.region_25.25_spmd.clone, body=%wide.region_23.24_spmd.clone.sunk | while | flops 1369963008 | bytes 159464816 | solution.py:133
  629.8 46.2 %while.88 = (s32[]{:T(128)}, f32[1024,4,64]{0,2,1:T(8,128)S(1)}, f32[1024,4,64]{0,2,1:T(8,128)S(1)}, bf16[2,512,4,64]{1,3,2,0:T(8,128)(2,1)}, bf16[2,512,4,64]{1...) while((s32[]{:T(128)}, f32[1024,4,64]{0,2,1:T(8,128)S(1)}, ...), condition=%wide.region_25.25_spmd.clone, body=%wide.region_23.24_spmd.clone.sunk | while | flops 1369963008 | bytes 159464816 | solution.py:133
  686.3 46.2 %while.88 = (s32[]{:T(128)}, f32[1024,4,64]{0,2,1:T(8,128)S(1)}, f32[1024,4,64]{0,2,1:T(8,128)S(1)}, bf16[2,512,4,64]{1,3,2,0:T(8,128)(2,1)}, bf16[2,512,4,64]{1...) while((s32[]{:T(128)}, f32[1024,4,64]{0,2,1:T(8,128)S(1)}, ...), condition=%wide.region_25.25_spmd.clone, body=%wide.region_23.24_spmd.clone.sunk | while | flops 1369963008 | bytes 159464816 | solution.py:133
  742.8 46.2 %while.88 = (s32[]{:T(128)}, f32[1024,4,64]{0,2,1:T(8,128)S(1)}, f32[1024,4,64]{0,2,1:T(8,128)S(1)}, bf16[2,512,4,64]{1,3,2,0:T(8,128)(2,1)}, bf16[2,512,4,64]{1...) while((s32[]{:T(128)}, f32[1024,4,64]{0,2,1:T(8,128)S(1)}, ...), condition=%wide.region_25.25_spmd.clone, body=%wide.region_23.24_spmd.clone.sunk | while | flops 1369963008 | bytes 159464816 | solution.py:133
  803.4 14.0 convolution_bitcast_fusion.2
  817.4 10.7 copy.191
  828.8 13.0 fusion.87
  850.1 11.8 fusion.100
  870.2 12.0 fusion.99
  909.6 72.2 %reduce-scatter.14.cloned.1.call-done = f32[32,3072]{1,0:T(8,128)} async-done(((f32[1024,3072]{1,0:T(8,128)}), f32[32,3072]{1,0:T(8,128)}) %reduce-scatter.14.cloned.1.call-update) | async-done | bytes 393232 | tf_op jit(solution)/shard_map/reduce_scatter | solution.py:338
  983.6 363.8 %reduce-scatter.18.cloned.1.call-done = f32[32,4096]{1,0:T(8,128)} async-done(((f32[1024,4096]{1,0:T(8,128)}), f32[32,4096]{1,0:T(8,128)}) %reduce-scatter.18.cloned.1.call-update) | async-done | bytes 524304 | tf_op jit(solution)/shard_map/reduce_scatter | solution.py:342
  1349.3 362.7 %reduce-scatter.20.cloned.1.call-done = f32[128,1024]{1,0:T(8,128)} async-done(((f32[4096,1024]{1,0:T(8,128)}), f32[128,1024]{1,0:T(8,128)}) %reduce-scatter.20.cloned.1.call-update) | async-done | bytes 524304 | tf_op jit(solution)/shard_map/reduce_scatter | solution.py:344
  1715.4 38.5 %all-reduce.5 = (bf16[1024]{0:T(1024)(128)(2,1)S(1)}, bf16[4096]{0:T(1024)(128)(2,1)S(1)}, bf16[1024]{0:T(1024)(128)(2,1)S(1)}) all-reduce(f32[1024]{0:T(1024)S(1)} %reshape.481, f32[4096]{0:T(1024)S(1)} %bitcast.429, f32[1024]{0:T(1024)S(1)} %reshape.489), channel_id=5, replica_groups=mesh['dp'=8,'fsdp'=4] {'dp','fsdp'}, use_global_device_ids=true, to_apply=%region_34.35.clone | all-reduce | flops 6144 | bytes 36864
  1754.0 9.5 all-gather.3
  1764.6 13.7 all-reduce.6
  1779.4 6.8 add_bitcast_fusion
  1794.3 52.7 %reduce-scatter.22.cloned.1.call-done = f32[32,2]{1,0:T(8,128)} async-done(((f32[1024,2]{1,0:T(8,128)}), f32[32,2]{1,0:T(8,128)}) %reduce-scatter.22.cloned.1.call-update) | async-done | bytes 272
  1847.8 7.9 all-gather.2
  1856.4 123.5 %reduce-scatter.26.cloned.1.call-done = f32[32,4]{1,0:T(8,128)} async-done(((f32[1024,4]{1,0:T(8,128)}), f32[32,4]{1,0:T(8,128)}) %reduce-scatter.26.cloned.1.call-update) | async-done | bytes 528
  1980.7 7.9 all-gather.5
  1989.2 123.8 %reduce-scatter.24.cloned.1.call-done = f32[32,4]{1,0:T(8,128)} async-done(((f32[1024,4]{1,0:T(8,128)}), f32[32,4]{1,0:T(8,128)}) %reduce-scatter.24.cloned.1.call-update) | async-done | bytes 528
  2113.8 7.9 all-gather.4
  2122.4 137.8 %reduce-scatter.16.cloned.1.call-done = f32[32,1024]{1,0:T(8,128)} async-done(((f32[1024,1024]{1,0:T(8,128)}), f32[32,1024]{1,0:T(8,128)}) %reduce-scatter.16.cloned.1.call-update) | async-done | bytes 131088 | tf_op jit(solution)/shard_map/reduce_scatter | solution.py:340
  2261.1 9.0 all_gather.77
  2271.2 14.8 all-gather.22.cloned.1.call-done
  2289.4 26.4 %all-gather.24.cloned.1.call-done = bf16[256,4096]{1,0:T(8,128)(2,1)} async-done(((bf16[32,4096]{1,0:T(8,128)(2,1)}), bf16[256,4096]{1,0:T(8,128)(2,1)}) %all-gather.24.cloned.1.call-update) | async-done | bytes 2097168 | tf_op jit(solution)/shard_map/all_gather | solution.py:362
  2319.9 25.6 %all-gather.26.cloned.1.call-done = bf16[1024,1024]{1,0:T(8,128)(2,1)} async-done(((bf16[128,1024]{1,0:T(8,128)(2,1)}), bf16[1024,1024]{1,0:T(8,128)(2,1)}) %all-gather.26.cloned.1.call-update) | async-done | bytes 2097168 | tf_op jit(solution)/shard_map/all_gather | solution.py:368
  (627 shorter events, 464.5 us)
Async XLA Ops:
  7.2 120.9 %all-gather.14.cloned.1.call-start = ((), (), s32[]{:S(2)}) async-start(), calls=%async_computation.7 | async-start | bytes 7864320 | tf_op jit(solution)/shard_map/all_gather | solution.py:180
  7.9 257.7 %all-gather.16.cloned.1.call-start = ((), (), s32[]{:S(2)}) async-start(), calls=%async_computation.8 | async-start | bytes 2621440 | tf_op jit(solution)/shard_map/all_gather | solution.py:182
  8.7 315.2 %all-gather.18.cloned.1.call-start = ((), (), s32[]{:S(2)}) async-start(), calls=%async_computation.9 | async-start | bytes 10485760 | tf_op jit(solution)/shard_map/all_gather | solution.py:184
  9.4 463.8 %all-gather.20.cloned.1.call-start = ((), (), s32[]{:S(2)}) async-start(), calls=%async_computation.10 | async-start | bytes 10485760 | tf_op jit(solution)/shard_map/all_gather | solution.py:186
  10.0 971.9 %reduce-scatter.14.cloned.1.call-start = ((), (), s32[]{:S(2)}) async-start(), calls=%async_computation.11 | async-start | bytes 12976128 | tf_op jit(solution)/shard_map/reduce_scatter | solution.py:338
  10.1 18.3 copy-start.59
  10.1 35.2 %copy-start.61 = (bf16[2,256]{1,0:T(2,128)(2,1)S(1)}, bf16[2,256]{1,0:T(2,128)(2,1)}, u32[]{:S(2)}) copy-start(bf16[2,256]{1,0:T(2,128)(2,1)} %param.23) | copy-start | bytes 3076
  10.1 43.1 %copy-start.63 = (s32[1,8]{1,0:T(1,128)S(1)}, s32[1,8]{1,0:T(1,128)}, u32[]{:S(2)}) copy-start(s32[1,8]{1,0:T(1,128)} %param.32) | copy-start | bytes 100
  10.1 44.0 %copy-start.64 = (bf16[256]{0:T(256)(128)(2,1)S(1)}, bf16[256]{0:T(256)(128)(2,1)}, u32[]{:S(2)}) copy-start(bf16[256]{0:T(256)(128)(2,1)} %param.25) | copy-start | bytes 1540
  10.1 59.2 %copy-start.60 = (bf16[1024]{0:T(1024)(128)(2,1)S(1)}, bf16[1024]{0:T(1024)(128)(2,1)}, u32[]{:S(2)}) copy-start(bf16[1024]{0:T(1024)(128)(2,1)} %param.27) | copy-start | bytes 6148
  10.1 77.3 %copy-start.65 = (bf16[256]{0:T(256)(128)(2,1)S(1)}, bf16[256]{0:T(256)(128)(2,1)}, u32[]{:S(2)}) copy-start(bf16[256]{0:T(256)(128)(2,1)} %param.29) | copy-start | bytes 1540
  13.0 88.5 %copy-start.8 = (bf16[1,1024,1024]{1,2,0:T(8,128)(2,1)}, bf16[1,1024,1024]{1,2,0:T(8,128)(2,1)S(1)}, u32[]{:S(2)}) copy-start(bf16[1,1024,1024]{1,2,0:T(8,128)(2,1)S(1)} %copy.179) | copy-start | bytes 6291460
  13.4 90.3 %copy-start.25 = (f32[1024]{0:T(1024)}, f32[1024]{0:T(1024)S(1)}, u32[]{:S(2)}) copy-start(f32[1024]{0:T(1024)S(1)} %broadcast_multiply_fusion.3) | copy-start | bytes 12292
  14.1 89.6 %copy-start.42 = (f32[1024]{0:T(1024)}, f32[1024]{0:T(1024)S(1)}, u32[]{:S(2)}) copy-start(f32[1024]{0:T(1024)S(1)} %fusion.63) | copy-start | bytes 12292
  14.1 89.6 %copy-start.36 = (f32[1024]{0:T(1024)}, f32[1024]{0:T(1024)S(1)}, u32[]{:S(2)}) copy-start(f32[1024]{0:T(1024)S(1)} %fusion.78) | copy-start | bytes 12292
  28.4 75.3 %copy-start.30 = (f32[1,1024]{1,0:T(1,128)}, f32[1,1024]{1,0:T(1,128)S(1)}, u32[]{:S(2)}) copy-start(f32[1,1024]{1,0:T(1,128)S(1)} %get-tuple-element.760) | copy-start | bytes 12292
  275.0 48.8 %copy-start.33 = (f32[1,1024]{1,0:T(1,128)S(1)}, f32[1,1024]{1,0:T(1,128)}, u32[]{:S(2)}) copy-start(f32[1,1024]{1,0:T(1,128)} %get-tuple-element.758) | copy-start | bytes 12292
  275.1 48.8 %copy-start.49 = (f32[4096]{0:T(1024)S(1)}, f32[4096]{0:T(1024)}, u32[]{:S(2)}) copy-start(f32[4096]{0:T(1024)} %convert_element_type.204) | copy-start | bytes 49156
  275.1 48.8 %copy-start.55 = (f32[1,1024]{1,0:T(1,128)S(1)}, f32[1,1024]{1,0:T(1,128)}, u32[]{:S(2)}) copy-start(f32[1,1024]{1,0:T(1,128)} %get-tuple-element.762) | copy-start | bytes 12292
  275.1 278.9 %copy-start.27 = (f32[1024]{0:T(1024)}, f32[1024]{0:T(1024)S(1)}, u32[]{:S(2)}) copy-start(f32[1024]{0:T(1024)S(1)} %broadcast_multiply_fusion.1) | copy-start | bytes 12292
  277.5 276.5 %copy-start.40 = (f32[1024]{0:T(1024)}, f32[1024]{0:T(1024)S(1)}, u32[]{:S(2)}) copy-start(f32[1024]{0:T(1024)S(1)} %fusion.80) | copy-start | bytes 12292
  323.9 149.3 %copy-start.38 = (f32[4,1,256]{2,1,0:T(1,128)S(1)}, f32[4,1,256]{2,1,0:T(1,128)}, u32[]{:S(2)}) copy-start(f32[4,1,256]{2,1,0:T(1,128)} %convert_element_type.244) | copy-start | bytes 12292
  473.2 14.4 copy-start.15
  473.2 14.4 copy-start.32
  473.2 14.4 copy-start.39
  545.4 5.9 copy-start.14
  588.0 7.4 copy-start.2
  611.1 7.4 copy-start.2
  644.5 7.4 copy-start.2
  667.6 7.4 copy-start.2
  701.0 7.4 copy-start.2
  724.2 7.4 copy-start.2
  757.5 7.4 copy-start.2
  780.6 7.4 copy-start.2
  828.1 519.3 %reduce-scatter.18.cloned.1.call-start = ((), (), s32[]{:S(2)}) async-start(), calls=%async_computation.14 | async-start | bytes 17301504 | tf_op jit(solution)/shard_map/reduce_scatter | solution.py:342
  848.5 863.5 %reduce-scatter.20.cloned.1.call-start = ((), (), s32[]{:S(2)}) async-start(), calls=%async_computation.16 | async-start | bytes 17301504 | tf_op jit(solution)/shard_map/reduce_scatter | solution.py:344
  868.5 978.5 %reduce-scatter.22.cloned.1.call-start = ((), (), s32[]{:S(2)}) async-start(), calls=%async_computation.18 | async-start | bytes 540672
  887.9 5.8 copy-start.31
  899.4 1080.5 %reduce-scatter.26.cloned.1.call-start = ((), (), s32[]{:S(2)}) async-start(), calls=%async_computation.20 | async-start | bytes 540672
  900.8 1212.2 %reduce-scatter.24.cloned.1.call-start = ((), (), s32[]{:S(2)}) async-start(), calls=%async_computation.19 | async-start | bytes 540672
  902.4 1357.8 %reduce-scatter.16.cloned.1.call-start = ((), (), s32[]{:S(2)}) async-start(), calls=%async_computation.13 | async-start | bytes 4325376 | tf_op jit(solution)/shard_map/reduce_scatter | solution.py:340
  909.5 804.3 %copy-start.66 = (u32[32]{0:T(128)S(1)}, u32[32]{0:T(128)}, u32[]{:S(2)}) copy-start(u32[32]{0:T(128)} %constant.175) | copy-start | bytes 388
  909.5 805.6 %copy-start.45 = (f32[1024]{0:T(1024)S(1)}, f32[1024]{0:T(1024)}, u32[]{:S(2)}) copy-start(f32[1024]{0:T(1024)} %get-tuple-element.732) | copy-start | bytes 12292
  909.5 805.7 %copy-start.50 = (f32[4096]{0:T(1024)S(1)}, f32[4096]{0:T(1024)}, u32[]{:S(2)}) copy-start(f32[4096]{0:T(1024)} %get-tuple-element.730) | copy-start | bytes 49156
  909.5 805.7 %copy-start.53 = (f32[1024]{0:T(1024)S(1)}, f32[1024]{0:T(1024)}, u32[]{:S(2)}) copy-start(f32[1024]{0:T(1024)} %get-tuple-element.728) | copy-start | bytes 12292
  909.5 1376.4 %all-gather.22.cloned.1.call-start = ((), (), s32[]{:S(2)}) async-start(), calls=%async_computation.12 | async-start | bytes 1769472 | tf_op jit(solution)/shard_map/all_gather | solution.py:350
  983.6 1332.2 %all-gather.24.cloned.1.call-start = ((), (), s32[]{:S(2)}) async-start(), calls=%async_computation.15 | async-start | bytes 2359296 | tf_op jit(solution)/shard_map/all_gather | solution.py:362
  1349.2 996.2 %all-gather.26.cloned.1.call-start = ((), (), s32[]{:S(2)}) async-start(), calls=%async_computation.17 | async-start | bytes 2359296 | tf_op jit(solution)/shard_map/all_gather | solution.py:368
  (71 other events, 193.3 us)
Sparse Core Ops, SparseCore 0:
  9.6 118.4 all-gather.13
  129.6 44.1 all-gather.15
  175.4 148.4 all-gather.17
  325.3 147.8 all-gather.19
  828.2 153.5 reduce-scatter.13
  984.1 363.2 reduce-scatter.17
  1349.8 362.1 reduce-scatter.19
  1714.9 132.0 reduce-scatter.21
  1849.2 130.6 reduce-scatter.25
  1982.6 130.3 reduce-scatter.23
  2115.8 144.2 reduce-scatter.15
  2261.9 23.9 all-gather.21
  2287.9 27.8 all-gather.23
  2317.5 27.8 all-gather.25
where the time goes:
time: 2360 us
  waiting for transfers between devices  1500 us (64%)
  matrix products  301 us (13%)
  local copies, waits for them, and re-layouts  197 us (8%)
  blocking collectives  173 us (7%)
  other arithmetic  130 us (6%)
  loops' own time  34.7 us (1%)
    reduce_scatter x1, waiting for transfers between devices, on_device(): lax.psum_scatter(moved[4], ('dp', 'fsdp'), scatter_dimension=0, tiled=True)  364 us
    reduce_scatter x1, waiting for transfers between devices, on_device(): lax.psum_scatter(moved[6], ('dp', 'fsdp'), scatter_dimension=0, tiled=True)  363 us
    unnamed x17, waiting for transfers between devices  303 us
    reduce_scatter x1, waiting for transfers between devices, on_device(): lax.psum_scatter(moved[2], ('dp', 'fsdp'), scatter_dimension=0, tiled=True)  138 us
    all_gather x1, waiting for transfers between devices, on_device(): lax.all_gather(down_weight, 'fsdp', axis=0, tiled=True)  127 us
    reduce_scatter x1, waiting for transfers between devices, on_device(): lax.psum_scatter(moved[0], ('dp', 'fsdp'), scatter_dimension=0, tiled=True)  72.2 us
    unnamed x2, blocking collectives  52.1 us
  transfers between devices with their start and end apart: 14, of which 13 were waited for; matrix products, arithmetic and copies ran while one was open for 12% of the time, Pallas kernels for 0%

commit v1 on v0

v1 whole, which is shorter than its diff:
```python
import functools
import math

import jax
import jax.numpy as jnp
from jax import lax
from jax.experimental import pallas as pl
from jax.experimental.pallas import tpu as pltpu
from jax.sharding import PartitionSpec as P

F32 = jnp.float32
BF = jnp.bfloat16
SDS = jax.ShapeDtypeStruct
HEAD_DIM = 64
PAIR = 2 * HEAD_DIM
EPS = 1e-05
MASKED = -1e30
QUERY_SCALE = math.log2(math.e) / math.sqrt(HEAD_DIM)
GRAD_SCALE = 1.0 / math.sqrt(HEAD_DIM)
BLOCK = 256
GELU_A = math.sqrt(2.0 / math.pi)
GELU_B = 0.044715 * GELU_A


def params(**more):
    return pltpu.CompilerParams(vmem_limit_bytes=60 * 1024 * 1024, **more)


def cost(flops, nbytes, trans=0):
    return pl.CostEstimate(flops=int(flops), bytes_accessed=int(nbytes), transcendentals=int(trans))


def dot_nn(a, b):
    return lax.dot_general(a, b, (((1,), (0,)), ((), ())), preferred_element_type=F32)


def dot_nt(a, b):
    return lax.dot_general(a, b, (((1,), (1,)), ((), ())), preferred_element_type=F32)


def dot_tn(a, b):
    return lax.dot_general(a, b, (((0,), (0,)), ((), ())), preferred_element_type=F32)


def centred(values):
    centre = values - jnp.mean(values, axis=-1, keepdims=True)
    rstd = lax.rsqrt(jnp.mean(centre * centre, axis=-1, keepdims=True) + EPS)
    return centre * rstd, rstd


def norm_back(grad, vhat, rstd, gain):
    e = grad * gain
    mean_e = jnp.mean(e, axis=-1, keepdims=True)
    mean_ev = jnp.mean(e * vhat, axis=-1, keepdims=True)
    return (e - mean_e - vhat * mean_ev) * rstd


def col_sum(values):
    return jnp.sum(values, axis=0, keepdims=True)


def qkv_kernel(x_ref, w_ref, bias_ref, gain_ref, shift_ref, normed_ref, packed_ref):
    step = pl.program_id(0)

    @pl.when(step == 0)
    def _():
        vhat, _ = centred(x_ref[...].astype(F32))
        normed_ref[...] = (vhat * gain_ref[...] + shift_ref[...]).astype(BF)

    out = dot_nn(normed_ref[...], w_ref[...]) + bias_ref[...]
    is_query = step < pl.num_programs(0) // 3
    packed_ref[...] = (out * jnp.where(is_query, QUERY_SCALE, 1.0)).astype(BF)


def qkv_forward(x, weight, bias, gain, shift):
    tokens, width = x.shape
    cols = weight.shape[1]
    bn = width // 2
    row = pl.BlockSpec((1, width), lambda j: (0, 0))
    full = pl.BlockSpec((tokens, width), lambda j: (0, 0))
    return pl.pallas_call(
        qkv_kernel,
        grid=(cols // bn,),
        in_specs=[
            full,
            pl.BlockSpec((width, bn), lambda j: (0, j)),
            pl.BlockSpec((1, bn), lambda j: (0, j)),
            row,
            row,
        ],
        out_specs=(full, pl.BlockSpec((tokens, bn), lambda j: (0, j))),
        out_shape=(SDS((tokens, width), BF), SDS((tokens, cols), BF)),
        compiler_params=params(),
        cost_estimate=cost(2 * tokens * width * cols, 2 * width * cols + 2 * tokens * cols),
        name="qkv_forward",
    )(x, weight, bias, gain, shift)


def out_kernel(att_ref, x_ref, w_ref, bias_ref, gain_ref, shift_ref, mixed_ref, mid_ref, two_ref):
    mixed = dot_nn(att_ref[...], w_ref[...]) + bias_ref[...]
    mixed_ref[...] = mixed
    vhat, _ = centred(mixed)
    mid = x_ref[...].astype(F32) + vhat * gain_ref[1:2, :] + shift_ref[1:2, :]
    mid_ref[...] = mid
    vhat, _ = centred(mid)
    two_ref[...] = (vhat * gain_ref[2:3, :] + shift_ref[2:3, :]).astype(BF)


def out_forward(attended, x, weight, bias, gain, shift):
    tokens, width = x.shape
    tok = pl.BlockSpec((BLOCK, width), lambda i: (i, 0))

    def whole(arr):
        return pl.BlockSpec(arr.shape, lambda i: (0, 0))

    return pl.pallas_call(
        out_kernel,
        grid=(tokens // BLOCK,),
        in_specs=[tok, tok, whole(weight), whole(bias), whole(gain), whole(shift)],
        out_specs=(tok, tok, tok),
        out_shape=(SDS((tokens, width), F32), SDS((tokens, width), F32), SDS((tokens, width), BF)),
        compiler_params=params(),
        cost_estimate=cost(2 * tokens * width * width, 16 * tokens * width),
        name="out_forward",
    )(attended, x, weight, bias, gain, shift)


def up_kernel(two_ref, w_ref, bias_ref, act_ref, slope_ref):
    a = dot_nn(two_ref[...], w_ref[...]) + bias_ref[...]
    sq = a * a
    t = jnp.tanh(a * (sq * GELU_B + GELU_A))
    half = 0.5 * t + 0.5
    act = a * half
    act_ref[...] = act.astype(BF)
    slope = half + act * ((1.0 - half) * (sq * (6.0 * GELU_B) + 2.0 * GELU_A))
    slope_ref[...] = slope.astype(BF)


def up_forward(two, weight, bias):
    tokens, width = two.shape
    cols = weight.shape[1]
    bn = 512
    blk = pl.BlockSpec((tokens, bn), lambda j: (0, j))
    return pl.pallas_call(
        up_kernel,
        grid=(cols // bn,),
        in_specs=[
            pl.BlockSpec((tokens, width), lambda j: (0, 0)),
            pl.BlockSpec((width, bn), lambda j: (0, j)),
            pl.BlockSpec((1, bn), lambda j: (0, j)),
        ],
        out_specs=(blk, blk),
        out_shape=(SDS((tokens, cols), BF), SDS((tokens, cols), BF)),
        compiler_params=params(),
        cost_estimate=cost(2 * tokens * width * cols, 2 * width * cols + 4 * tokens * cols),
        name="up_forward",
    )(two, weight, bias)


def down_kernel(
    act_ref, w_ref, bias_ref, mid_ref, cot_ref, live_ref, gain_ref, shift_ref, out_ref, grad_ref, sums_ref
):
    @pl.when(pl.program_id(0) == 0)
    def _():
        sums_ref[...] = jnp.zeros_like(sums_ref)

    ffn = dot_nn(act_ref[...], w_ref[...]) + bias_ref[...]
    vhat, rstd = centred(ffn)
    gain = gain_ref[3:4, :]
    out_ref[...] = (mid_ref[...] + vhat * gain + shift_ref[3:4, :]).astype(BF)
    grad = cot_ref[...].astype(F32) * live_ref[...]
    low = norm_back(grad, vhat, rstd, gain).astype(BF)
    grad_ref[...] = low
    sums_ref[0:1, :] += col_sum(grad * vhat)
    sums_ref[1:2, :] += col_sum(grad)
    sums_ref[2:3, :] += col_sum(low.astype(F32))


def down_forward(act, weight, bias, mid, cot, live, gain, shift):
    tokens, width = mid.shape
    cols = act.shape[1]
    tok = pl.BlockSpec((BLOCK, width), lambda i: (i, 0))

    def whole(arr):
        return pl.BlockSpec(arr.shape, lambda i: (0, 0))

    return pl.pallas_call(
        down_kernel,
        grid=(tokens // BLOCK,),
        in_specs=[
            pl.BlockSpec((BLOCK, cols), lambda i: (i, 0)),
            whole(weight),
            whole(bias),
            tok,
            tok,
            pl.BlockSpec((BLOCK, 1), lambda i: (i, 0)),
            whole(gain),
            whole(shift),
        ],
        out_specs=(tok, tok, pl.BlockSpec((8, width), lambda i: (0, 0))),
        out_shape=(SDS((tokens, width), BF), SDS((tokens, width), BF), SDS((8, width), F32)),
        compiler_params=params(),
        cost_estimate=cost(2 * tokens * width * cols, 2 * width * cols + 2 * tokens * cols),
        name="down_forward",
    )(act, weight, bias, mid, cot, live, gain, shift)


def hidden_kernel(grad_ref, w_ref, slope_ref, out_ref, sum_ref):
    low = (dot_nt(grad_ref[...], w_ref[...]) * slope_ref[...].astype(F32)).astype(BF)
    out_ref[...] = low
    sum_ref[...] = col_sum(low.astype(F32))


def hidden_backward(grad, weight, slope):
    tokens, width = grad.shape
    cols = weight.shape[0]
    bn = 512
    blk = pl.BlockSpec((tokens, bn), lambda j: (0, j))
    return pl.pallas_call(
        hidden_kernel,
        grid=(cols // bn,),
        in_specs=[
            pl.BlockSpec((tokens, width), lambda j: (0, 0)),
            pl.BlockSpec((bn, width), lambda j: (j, 0)),
            blk,
        ],
        out_specs=(blk, pl.BlockSpec((1, bn), lambda j: (0, j))),
        out_shape=(SDS((tokens, cols), BF), SDS((1, cols), F32)),
        compiler_params=params(),
        cost_estimate=cost(2 * tokens * width * cols, 2 * width * cols + 4 * tokens * cols),
        name="hidden_backward",
    )(grad, weight, slope)


def mid_kernel(
    gh_ref, up_ref, out_w_ref, mid_ref, mixed_ref, cot_ref, live_ref, gain_ref,
    gmid_ref, gmix_ref, gatt_ref, sums_ref,
):
    @pl.when(pl.program_id(0) == 0)
    def _():
        sums_ref[...] = jnp.zeros_like(sums_ref)

    grad = dot_nt(gh_ref[...], up_ref[...])
    vhat, rstd = centred(mid_ref[...])
    sums_ref[0:1, :] += col_sum(grad * vhat)
    sums_ref[1:2, :] += col_sum(grad)
    gmid = cot_ref[...].astype(F32) * live_ref[...] + norm_back(grad, vhat, rstd, gain_ref[2:3, :])
    gmid_ref[...] = gmid
    vhat, rstd = centred(mixed_ref[...])
    sums_ref[2:3, :] += col_sum(gmid * vhat)
    sums_ref[3:4, :] += col_sum(gmid)
    low = norm_back(gmid, vhat, rstd, gain_ref[1:2, :]).astype(BF)
    gmix_ref[...] = low
    sums_ref[4:5, :] += col_sum(low.astype(F32))
    gatt_ref[...] = dot_nt(low, out_w_ref[...]).astype(BF)


def mid_backward(gh, up, out_w, mid, mixed, cot, live, gain):
    tokens, width = mid.shape
    cols = gh.shape[1]
    tok = pl.BlockSpec((BLOCK, width), lambda i: (i, 0))

    def whole(arr):
        return pl.BlockSpec(arr.shape, lambda i: (0, 0))

    return pl.pallas_call(
        mid_kernel,
        grid=(tokens // BLOCK,),
        in_specs=[
            pl.BlockSpec((BLOCK, cols), lambda i: (i, 0)),
            whole(up),
            whole(out_w),
            tok,
            tok,
            tok,
            pl.BlockSpec((BLOCK, 1), lambda i: (i, 0)),
            whole(gain),
        ],
        out_specs=(tok, tok, tok, pl.BlockSpec((8, width), lambda i: (0, 0))),
        out_shape=(
            SDS((tokens, width), F32),
            SDS((tokens, width), BF),
            SDS((tokens, width), BF),
            SDS((8, width), F32),
        ),
        compiler_params=params(),
        cost_estimate=cost(2 * tokens * width * (cols + width), 2 * width * cols + 2 * tokens * cols),
        name="mid_backward",
    )(gh, up, out_w, mid, mixed, cot, live, gain)


def input_kernel(n_grads, *refs):
    grad_refs, (w_ref, x_ref, gmid_ref, gain_ref, out_ref, sums_ref) = refs[:n_grads], refs[n_grads:]

    @pl.when(pl.program_id(0) == 0)
    def _():
        sums_ref[...] = jnp.zeros_like(sums_ref)

    grads = jnp.concatenate([ref[...] for ref in grad_refs], axis=1)
    grad = dot_nt(grads, w_ref[...])
    vhat, rstd = centred(x_ref[...].astype(F32))
    sums_ref[0:1, :] += col_sum(grad * vhat)
    sums_ref[1:2, :] += col_sum(grad)
    out_ref[...] = gmid_ref[...] + norm_back(grad, vhat, rstd, gain_ref[0:1, :])


def input_backward(grads, weight, x, gmid, gain):
    tokens, width = x.shape
    tok = pl.BlockSpec((BLOCK, width), lambda i: (i, 0))

    def whole(arr):
        return pl.BlockSpec(arr.shape, lambda i: (0, 0))

    return pl.pallas_call(
        functools.partial(input_kernel, len(grads)),
        grid=(tokens // BLOCK,),
        in_specs=[pl.BlockSpec((BLOCK, g.shape[1]), lambda i: (i, 0)) for g in grads]
        + [whole(weight), tok, tok, whole(gain)],
        out_specs=(tok, pl.BlockSpec((8, width), lambda i: (0, 0))),
        out_shape=(SDS((tokens, width), F32), SDS((8, width), F32)),
        compiler_params=params(),
        cost_estimate=cost(6 * tokens * width * width, 6 * width * width + 14 * tokens * width),
        name="input_backward",
    )(*grads, weight, x, gmid, gain)


def fill_bias(bias, start_ref):
    length = bias.shape[0]
    for j in range(length // BLOCK):
        key = lax.broadcasted_iota(jnp.int32, (BLOCK, length), 0) + j * BLOCK
        query = lax.broadcasted_iota(jnp.int32, (BLOCK, length), 1)
        allowed = (key <= query) & (key >= start_ref[...])
        bias[j * BLOCK : (j + 1) * BLOCK, :] = jnp.where(allowed, 0.0, MASKED)


def one_head(low, arr, head):
    zero = jnp.zeros_like(arr)
    return jnp.where(low, arr, zero) if head == 0 else jnp.where(low, zero, arr)


def attend_kernel(q_ref, k_ref, v_ref, start_ref, out_ref, lse_ref, bias):
    length = q_ref.shape[0]

    @pl.when(pl.program_id(0) == 0)
    def _():
        fill_bias(bias, start_ref)

    low = lax.broadcasted_iota(jnp.int32, (1, PAIR), 1) < HEAD_DIM
    low_rows = lax.broadcasted_iota(jnp.int32, (PAIR, 1), 0) < HEAD_DIM
    keys = k_ref[...]
    values = jnp.concatenate([v_ref[...], jnp.ones((length, PAIR), BF)], axis=1)
    for i in range(length // BLOCK):
        reach = (i + 1) * BLOCK
        sl = slice(i * BLOCK, reach)
        queries = q_ref[sl, :]
        parts = []
        for head in range(2):
            scores = dot_nt(keys[:reach], one_head(low, queries, head)) + bias[:reach, sl]
            top = jnp.max(scores, axis=0, keepdims=True)
            probs = jnp.exp2(scores - top).astype(BF)
            mixed = dot_tn(values[:reach], probs)
            total = mixed[PAIR : PAIR + 1]
            parts.append(mixed[:PAIR] / total)
            lse_ref[0, head : head + 1, sl] = top + jnp.log2(total)
        out_ref[sl, :] = jnp.where(low_rows, parts[0], parts[1]).T.astype(BF)


def attend(packed, start_row):
    length = packed.shape[0]
    pairs = packed.shape[1] // (3 * PAIR)

    def blk(offset):
        return pl.BlockSpec((length, PAIR), lambda h: (0, offset + h))

    return pl.pallas_call(
        attend_kernel,
        grid=(pairs,),
        in_specs=[blk(0), blk(pairs), blk(2 * pairs), pl.BlockSpec((1, length), lambda h: (0, 0))],
        out_specs=(blk(0), pl.BlockSpec((1, 2, length), lambda h: (h, 0, 0))),
        out_shape=(SDS((length, PAIR * pairs), BF), SDS((pairs, 2, length), F32)),
        scratch_shapes=[pltpu.VMEM((length, length), F32)],
        compiler_params=params(),
        cost_estimate=cost(8 * pairs * length * length * PAIR, 8 * length * pairs * PAIR),
        name="attend",
    )(packed, packed, packed, start_row)


def attend_back_kernel(
    q_ref, k_ref, v_ref, g_ref, o_ref, lse_ref, start_ref, gq_ref, gk_ref, gv_ref, sq_ref, sv_ref, bias, acc
):
    length = q_ref.shape[0]

    @pl.when(pl.program_id(0) == 0)
    def _():
        fill_bias(bias, start_ref)

    low = lax.broadcasted_iota(jnp.int32, (1, PAIR), 1) < HEAD_DIM
    queries, grads = q_ref[...], g_ref[...]
    q_of = [one_head(low, queries, head) for head in range(2)]
    g_of = [one_head(low, grads, head) for head in range(2)]
    inner = (grads.astype(F32) * o_ref[...].astype(F32)).T
    inner_of = [col_sum(inner[:HEAD_DIM]), col_sum(inner[HEAD_DIM:])]
    sum_v = jnp.zeros((1, PAIR), F32)
    for j in range(length // BLOCK):
        first = j * BLOCK
        sl = slice(first, first + BLOCK)
        keys, values = k_ref[sl, :], v_ref[sl, :]
        gk = gv = gq = 0.0
        for head in range(2):
            scores = dot_nt(keys, q_of[head][first:]) + bias[sl, first:]
            probs = jnp.exp2(scores - lse_ref[0, head : head + 1, first:])
            gprobs = dot_nt(values, g_of[head][first:])
            gscores = (probs * (gprobs - inner_of[head][:, first:]) * GRAD_SCALE).astype(BF)
            gv = gv + dot_nn(probs.astype(BF), g_of[head][first:])
            gk = gk + dot_nn(gscores, q_of[head][first:])
            gq = gq + dot_tn(gscores, one_head(low, keys, head))
        low_v = gv.astype(BF)
        gv_ref[sl, :] = low_v
        gk_ref[sl, :] = (gk * (1.0 / QUERY_SCALE)).astype(BF)
        sum_v = sum_v + col_sum(low_v.astype(F32))
        if j == 0:
            acc[...] = gq
        else:
            acc[first:, :] += gq
    low_q = acc[...].astype(BF)
    gq_ref[...] = low_q
    sq_ref[...] = col_sum(low_q.astype(F32))
    sv_ref[...] = sum_v


def attend_back(packed, grads, attended, lse, start_row, part, parts):
    length = packed.shape[0]
    total = packed.shape[1] // (3 * PAIR)
    pairs = total // parts
    skip = part * pairs

    def blk(offset):
        return pl.BlockSpec((length, PAIR), lambda h: (0, offset + h))

    row = pl.BlockSpec((1, PAIR), lambda h: (0, h))
    grad = SDS((length, PAIR * pairs), BF)
    sums = SDS((1, PAIR * pairs), F32)
    return pl.pallas_call(
        attend_back_kernel,
        grid=(pairs,),
        in_specs=[
            blk(skip),
            blk(total + skip),
            blk(2 * total + skip),
            blk(skip),
            blk(skip),
            pl.BlockSpec((1, 2, length), lambda h: (skip + h, 0, 0)),
            pl.BlockSpec((1, length), lambda h: (0, 0)),
        ],
        out_specs=(blk(0), blk(0), blk(0), row, row),
        out_shape=(grad, grad, grad, sums, sums),
        scratch_shapes=[pltpu.VMEM((length, length), F32), pltpu.VMEM((length, PAIR), F32)],
        compiler_params=params(),
        cost_estimate=cost(20 * pairs * length * length * PAIR, 16 * length * pairs * PAIR),
        name="attend_back",
    )(packed, packed, packed, grads, attended, lse, start_row)


def swap(arr, axis, mask):
    size = lax.axis_size(axis)
    return lax.ppermute(arr, axis, [(i, i ^ mask) for i in range(size)])


def after(first, then):
    return lax.optimization_barrier((first, then))


def shard_swaps(piece):
    return [swap(piece, "fsdp", k) for k in range(1, lax.axis_size("fsdp"))]


def plane_swaps(got, order):
    first, second = order
    own = jnp.stack(got)
    two = jnp.concatenate([own, swap(own, "dp", first)])
    four = swap(two, "dp", second)
    return [
        ((0, first), two),
        ((second, second ^ first), four),
        ((1, 1 ^ first), swap(two, "dp", 1)),
        ((1 ^ second, 1 ^ second ^ first), swap(four, "dp", 1)),
    ]


def place_kernel(layout, masks, shards, n_own, idx_ref, *refs):
    n_out = len(layout)
    owns = refs[:n_own]
    slots = refs[n_own : n_own + len(masks)]
    outs = refs[n_own + len(masks) : -1]
    sems = refs[-1]
    dp, z = idx_ref[0], idx_ref[1]
    copies = []

    def start(src, dst):
        copy = pltpu.make_async_copy(src, dst, sems.at[len(copies)])
        copy.start()
        copies.append(copy)

    for o in range(n_out):
        rows = owns[o].shape[0]
        start(owns[o], outs[o].at[pl.ds(pl.multiple_of(z * rows, rows), rows), :])
    for pair, ref in zip(masks, slots):
        for which, mask in enumerate(pair):
            for k in range(1, shards):
                at = which * (shards - 1) + k - 1
                for o, (c0, c1) in enumerate(layout):
                    shard_rows = owns[o].shape[0]
                    rows = ref.shape[1]
                    dst = pl.multiple_of((z ^ k) * shard_rows + (dp ^ mask) * rows, rows)
                    src = ref.at[at] if n_out == 1 else ref.at[at, :, c0:c1]
                    start(src, outs[o].at[pl.ds(dst, rows), :])
    for copy in copies:
        copy.wait()


def place(idx, owns, flow, layout, shards):
    masks = [m for m, _ in flow]
    slots = [a for _, a in flow]
    any_spec = pl.BlockSpec(memory_space=pl.ANY)
    n_copies = len(owns) * (1 + 2 * (shards - 1) * len(slots))
    outs = tuple(SDS((o.shape[0] * shards, o.shape[1]), BF) for o in owns)
    nbytes = sum(2 * 2 * math.prod(o.shape) for o in outs)
    return pl.pallas_call(
        functools.partial(place_kernel, layout, masks, shards, len(owns)),
        in_specs=[pl.BlockSpec(memory_space=pltpu.SMEM)] + [any_spec] * (len(owns) + len(slots)),
        out_specs=(pl.BlockSpec(memory_space=pltpu.VMEM),) * len(owns),
        out_shape=outs,
        scratch_shapes=[pltpu.SemaphoreType.DMA((n_copies,))],
        compiler_params=params(),
        cost_estimate=cost(0, nbytes),
        name="place",
    )(idx, *owns, *slots)


def split_down(refs, zz):
    (wide,) = refs
    rows, cols = wide.shape[0] // 4, wide.shape[1] // 2
    part = wide[zz * rows : (zz + 1) * rows]
    return part[:, :cols], part[:, cols:]


def split_up(refs, zz):
    (wide,) = refs
    rows = wide.shape[0] // 8
    return wide[2 * zz * rows : (2 * zz + 1) * rows], wide[(2 * zz + 1) * rows : (2 * zz + 2) * rows]


def split_rows(refs, zz):
    rows = refs[0].shape[0] // 4
    return (jnp.concatenate([r[zz * rows : (zz + 1) * rows] for r in refs], axis=1),)


def grad_kernel(keep, groups, split, first, idx_ref, *refs):
    step = pl.program_id(0)
    z = idx_ref[1]
    at, dots = 0, []
    for n_left, n_right in groups:
        left = [r[...] for r in refs[at : at + n_left]]
        right = [r[...] for r in refs[at + n_left : at + n_left + n_right]]
        at += n_left + n_right
        left = left[0] if n_left == 1 else jnp.concatenate(left, axis=1)
        right = right[0] if n_right == 1 else jnp.concatenate(right, axis=1)
        dots.append(dot_tn(left, right))
    rest = refs[at:]
    if not keep:
        for zz in range(4):
            for f, part in enumerate(split(dots, zz)):
                rest[0][0, zz ^ z, f] = part.astype(BF)
        return
    got_ref, outs = rest[0], rest[1:]
    for dst in range(4):

        @pl.when(step == dst)
        def _():
            for zz in range(4):
                slot = zz ^ z
                for f, part in enumerate(split(dots, zz)):
                    bit = dst // 2 if first[f] == 4 else dst % 2
                    low = (part + got_ref[0, slot, f].astype(F32)).astype(BF)
                    outs[2 * f + bit][0, slot] = low


def grad_call(name, idx, specs, args, groups, split, first, piece, flops, got=None):
    keep = got is not None
    flows, rows, cols = piece
    block = pl.BlockSpec((1, 4) + piece, lambda i, idx: (i, 0, 0, 0, 0))
    half = (1, 4, rows, cols)
    if keep:
        maps = {
            4: (lambda i, idx: (jnp.minimum(i, 1), 0, 0, 0), lambda i, idx: (jnp.maximum(i - 2, 0), 0, 0, 0)),
            2: (lambda i, idx: (i // 2, 0, 0, 0), lambda i, idx: (i // 2, 0, 0, 0)),
        }
        specs = specs + [block]
        args = args + [got]
        out_specs = tuple(pl.BlockSpec(half, m) for mask in first for m in maps[mask])
        out_shape = (SDS((2, 4, rows, cols), BF),) * (2 * flows)
    else:
        out_specs = block
        out_shape = SDS((4, 4) + piece, BF)
    return pl.pallas_call(
        functools.partial(grad_kernel, keep, groups, split, first),
        grid_spec=pltpu.PrefetchScalarGridSpec(
            num_scalar_prefetch=1, grid=(4,), in_specs=specs, out_specs=out_specs
        ),
        out_shape=out_shape,
        compiler_params=params(),
        cost_estimate=cost(flops, flops // 400),
        name=name + ("_keep" if keep else "_send"),
    )(idx, *args)


def chip_of(i, idx):
    return (idx[0] // 2) ^ (3 - i)


def core_of(keep, idx):
    return idx[0] & 1 if keep else (idx[0] & 1) ^ 1


def grad_down(idx, act, grad, got=None):
    tokens, width = grad.shape
    keep = got is not None
    rows = act.shape[1] // 32

    def block(zz):
        return pl.BlockSpec(
            (tokens, rows), lambda i, idx: (0, zz * 8 + chip_of(i, idx) * 2 + core_of(keep, idx))
        )

    specs = [block(0), block(1), block(2), block(3), pl.BlockSpec((tokens, width), lambda i, idx: (0, 0))]
    args = [act, act, act, act, grad]
    flops = act.shape[1] * width * tokens
    piece = (2, rows, width // 2)
    return grad_call(
        "grad_down", idx, specs, args, [(4, 1)], split_down, (4, 2), piece, flops, got
    )


def grad_up(idx, two, grad, got=None):
    tokens, width = two.shape
    keep = got is not None
    cols = grad.shape[1] // 8
    specs = [
        pl.BlockSpec((tokens, width), lambda i, idx: (0, 0)),
        pl.BlockSpec((tokens, cols), lambda i, idx: (0, chip_of(i, idx) * 2 + core_of(keep, idx))),
    ]
    flops = grad.shape[1] * width * tokens
    piece = (2, width // 8, cols)
    return grad_call("grad_up", idx, specs, [two, grad], [(1, 1)], split_up, (4, 2), piece, flops, got)


def grad_heads(idx, first, one, gq, gk, gv, att=None, gmix=None, got=None):
    tokens, width = one.shape
    keep = got is not None
    rows = width // 8

    def left(zz):
        return pl.BlockSpec((tokens, rows), lambda i, idx: (0, zz * 2 + core_of(keep, idx)))

    def right(cols):
        return pl.BlockSpec((tokens, cols), lambda i, idx: (0, chip_of(i, idx)))

    lefts = [left(0), left(1), left(2), left(3)]
    specs, args, groups = lefts + [right(PAIR)] * 3, [one] * 4 + [gq, gk, gv], [(4, 3)]
    cols = 3 * PAIR
    if att is not None:
        specs, args, groups = specs + lefts + [right(width // 4)], args + [att] * 4 + [gmix], groups + [(4, 1)]
        cols += width // 4
    piece = (1, rows, cols)
    flops = 4 * tokens * width * cols
    return grad_call("grad_heads", idx, specs, args, groups, split_rows, (first,), piece, flops, got)


def add_low(a, b):
    return (a.astype(F32) + b.astype(F32)).astype(BF)


def add_wide(a, b):
    return a.astype(F32) + b.astype(F32)


def plane_first(parts, first):
    return [swap(parts[2 * f], "dp", mask) for f, mask in enumerate(first)]


def plane_second(parts, got, first):
    send = [add_low(parts[2 * f + 1][0], got[f][0]) for f in range(len(first))]
    keep = [add_low(parts[2 * f + 1][1], got[f][1]) for f in range(len(first))]
    return keep, [swap(s, "dp", 6 - mask) for s, mask in zip(send, first)]


def across(keep, got):
    both = jnp.stack([add_wide(k, g) for k, g in zip(keep, got)], axis=1)
    back = swap(both[1::2].astype(BF), "fsdp", 1)
    both = add_wide(both[0::2], back)
    back = swap(both[1].astype(BF), "fsdp", 2)
    return add_low(both[0], back)


def spread(piece, first):
    second = 6 - first
    two = jnp.stack([piece, swap(piece, "dp", first)])
    four = swap(two, "dp", second)
    return [
        ((0, first), two),
        ((second, 6), four),
        ((1, 1 ^ first), swap(two, "dp", 1)),
        ((1 ^ second, 7), swap(four, "dp", 1)),
    ]


def place_down(dp, piece, outs):
    (out,) = outs
    rows, cols = piece.shape[1], piece.shape[2]
    at = pl.ds(pl.multiple_of(dp * rows, rows), rows)
    out[at, :cols] = piece[0].astype(F32)
    out[at, cols:] = piece[1].astype(F32)


def place_up(dp, piece, outs):
    (out,) = outs
    rows, cols = piece.shape[1], piece.shape[2]
    at = pl.ds(pl.multiple_of(dp * cols, cols), cols)
    out[:rows, at] = piece[0].astype(F32)
    out[rows:, at] = piece[1].astype(F32)


def place_heads(half, dp, piece, outs):
    rows = piece.shape[1]
    chip, core = dp // 2, dp % 2
    at_rows = pl.ds(pl.multiple_of(core * rows, rows), rows)
    width = outs[0].shape[1] // 3
    for part in range(3):
        at = pl.multiple_of(part * width + half * (width // 2) + chip * PAIR, PAIR)
        outs[0][at_rows, pl.ds(at, PAIR)] = piece[0, :, part * PAIR : (part + 1) * PAIR].astype(F32)
    if half == 0:
        cols = width // 4
        at = pl.multiple_of(chip * cols, cols)
        outs[1][at_rows, pl.ds(at, cols)] = piece[0, :, 3 * PAIR :].astype(F32)


def finish_kernel(placers, masks, idx_ref, *refs):
    n_in = sum(len(m) for m in masks)
    ins, outs = list(refs[:n_in]), refs[n_in:]
    for placer, pairs in zip(placers, masks):
        for pair in pairs:
            ref = ins.pop(0)
            for which, mask in enumerate(pair):
                placer(idx_ref[0] ^ mask, ref[which], outs)


def finish(name, idx, placers, pieces, shapes):
    masks = [[m for m, _ in p] for p in pieces]
    arrays = [a for p in pieces for _, a in p]
    vmem = pl.BlockSpec(memory_space=pltpu.VMEM)
    return pl.pallas_call(
        functools.partial(finish_kernel, placers, masks),
        in_specs=[pl.BlockSpec(memory_space=pltpu.SMEM)] + [vmem] * len(arrays),
        out_specs=(vmem,) * len(shapes),
        out_shape=tuple(SDS(s, F32) for s in shapes),
        compiler_params=params(),
        cost_estimate=cost(0, sum(6 * math.prod(s) for s in shapes)),
        name=name,
    )(idx, *arrays)


def segment_starts(lengths, length):
    ends = jnp.cumsum(lengths)
    positions = jnp.arange(length, dtype=jnp.int32)
    begun = jnp.where(ends[None, :] <= positions[:, None], ends[None, :], 0)
    return jnp.max(begun, axis=1).astype(jnp.int32), positions < ends[-1]


def eighth(shard):
    rows = shard.shape[0] // 8
    return lax.dynamic_slice_in_dim(shard, lax.axis_index("dp") * rows, rows, axis=0)


SMALL_ROWS = 16


def pack_small(qv_bias, out_bias, up_bias, down_bias, gain, shift):
    flat = [a.reshape(-1) for a in (qv_bias, out_bias, up_bias, down_bias, gain, shift)]
    return jnp.concatenate(flat)


def unpack_small(shards):
    count, total = shards.shape
    unit = total // SMALL_ROWS
    sizes = ((2, unit), (1, unit), (1, 4 * unit), (1, unit), (4, unit), (4, unit))
    out, at = [], 0
    for lead, cols in sizes:
        block = shards[:, at : at + lead * cols].reshape(count, lead, cols)
        out.append(jnp.swapaxes(block, 0, 1).reshape(lead, count * cols))
        at += lead * cols
    return out


def by_shard(rows, count):
    flat = []
    for arr in rows:
        lead, cols = arr.shape
        flat.append(
            jnp.swapaxes(arr.reshape(lead, count, cols // count), 0, 1).reshape(count, -1)
        )
    return jnp.concatenate(flat, axis=1)


def gather_small(own, got):
    z = lax.axis_index("fsdp")
    slots = jnp.stack([own] + got)
    low, high = z % 2, z // 2
    slots = jnp.where(low == 0, slots, slots[jnp.array([1, 0, 3, 2])])
    return jnp.where(high == 0, slots, slots[jnp.array([2, 3, 0, 1])])


def on_device(
    layer_input,
    qkv_weight,
    query_value_bias,
    out_weight,
    out_bias,
    up_weight,
    up_bias,
    down_weight,
    down_bias,
    norm_gain,
    norm_shift,
    doc_lengths,
    cotangent,
):
    _, tokens, width = layer_input.shape
    shards = lax.axis_size("fsdp")
    halves = shards == 4 and lax.axis_size("dp") == 8
    idx = jnp.stack([lax.axis_index("dp"), lax.axis_index("fsdp")]).astype(jnp.int32)
    x = layer_input[0]
    cot = cotangent[0]
    start, live = segment_starts(doc_lengths[0], tokens)
    start_row = start[None, :]
    live_col = live.astype(F32)[:, None]
    small_own = pack_small(query_value_bias, out_bias, up_bias, down_bias, norm_gain, norm_shift)
    if halves:
        piece = eighth(qkv_weight)
        cols = piece.shape[1]
        extra = small_own.reshape(piece.shape[0], -1)
        got_q = shard_swaps(jnp.concatenate([piece, extra], axis=1))
        piece_u = jnp.concatenate([eighth(out_weight), eighth(up_weight)], axis=1)
        got_q, piece_u = after(got_q, piece_u)
        small = gather_small(small_own, [g[:, cols:].reshape(-1) for g in got_q])
        flow_q = plane_swaps([g[:, :cols] for g in got_q], (4, 2))
        got_u = shard_swaps(piece_u)
        got_u, piece_d = after(got_u, eighth(down_weight))
        got_d = shard_swaps(piece_d)
        (w_qkv,) = place(idx, [qkv_weight], flow_q, [(0, cols)], shards)
        flow_u = plane_swaps(got_u, (4, 2))
        w_out, w_up = place(
            idx, [out_weight, up_weight], flow_u, [(0, width), (width, piece_u.shape[1])], shards
        )
        flow_d = plane_swaps(got_d, (2, 4))
        (w_down,) = place(idx, [down_weight], flow_d, [(0, width)], shards)
    else:
        small = lax.all_gather(small_own, "fsdp", axis=0)
        w_qkv = lax.all_gather(qkv_weight, "fsdp", axis=0, tiled=True)
        w_out = lax.all_gather(out_weight, "fsdp", axis=0, tiled=True)
        w_up = lax.all_gather(up_weight, "fsdp", axis=0, tiled=True)
        w_down = lax.all_gather(down_weight, "fsdp", axis=0, tiled=True)
    qv_b, out_b, up_b, down_b, gain, shift = unpack_small(small.astype(F32))
    qkv_b = jnp.concatenate([qv_b[0:1], jnp.zeros((1, width), F32), qv_b[1:2]], axis=1)

    normed_one, packed = qkv_forward(x, w_qkv, qkv_b, gain[0:1], shift[0:1])
    attended, lse = attend(packed, start_row)
    mixed, mid, two = out_forward(attended, x, w_out, out_b, gain, shift)
    act, slope = up_forward(two, w_up, up_b)
    layer_out, gffn, sums3 = down_forward(act, w_down, down_b, mid, cot, live_col, gain, shift)

    both = (4, 2)
    if halves:
        send = grad_down(idx, act, gffn)
        got_down = swap(send, "dp", 1)
        _, gffn = after(send, gffn)
    ghid, up_sum = hidden_backward(gffn, w_down, slope)
    if halves:
        got_down, act, ghid = lax.optimization_barrier((got_down, act, ghid))
        down_parts = grad_down(idx, act, gffn, got_down)
        down_got = plane_first(down_parts, both)
        down_parts, ghid = after(down_parts, ghid)
        send = grad_up(idx, two, ghid)
        got_up = swap(send, "dp", 1)
        _, ghid = after(send, ghid)
    gmid, gmix, gatt, sums21 = mid_backward(ghid, w_up, w_out, mid, mixed, cot, live_col, gain)
    if halves:
        down_got, gatt = after(down_got, gatt)
        down_keep, down_got = plane_second(down_parts, down_got, both)
        got_up, ghid = after(got_up, ghid)
        up_parts = grad_up(idx, two, ghid, got_up)
        up_got = plane_first(up_parts, both)
        up_parts, down_keep, gatt = lax.optimization_barrier((up_parts, down_keep, gatt))
    gq0, gk0, gv0, sq0, sv0 = attend_back(packed, gatt, attended, lse, start_row, 0, 2)
    if halves:
        send = grad_heads(idx, 4, normed_one, gq0, gk0, gv0, attended, gmix)
        got_heads = swap(send, "dp", 1)
        up_got, down_got, send, gatt = lax.optimization_barrier((up_got, down_got, send, gatt))
        up_keep, up_got = plane_second(up_parts, up_got, both)
        down_piece = across(down_keep, down_got)
    gq1, gk1, gv1, sq1, sv1 = attend_back(packed, gatt, attended, lse, start_row, 1, 2)
    if halves:
        got_heads, gq1 = after(got_heads, gq1)
        heads_parts = grad_heads(idx, 4, normed_one, gq0, gk0, gv0, attended, gmix, got_heads)
        heads_got = plane_first(heads_parts, (4,))
        send = grad_heads(idx, 2, normed_one, gq1, gk1, gv1)
        got_last = swap(send, "dp", 1)
        up_piece = across(up_keep, up_got)
        down_all = spread(down_piece, 4)
        last_parts = grad_heads(idx, 2, normed_one, gq1, gk1, gv1, got=got_last)
        last_got = plane_first(last_parts, (2,))
        last_parts, gq1 = after(last_parts, gq1)
    grad_input, sums0 = input_backward([gq0, gq1, gk0, gk1, gv0, gv1], w_qkv, x, gmid, gain)
    small_grads = by_shard(
        [
            jnp.concatenate([jnp.concatenate([sq0, sq1], axis=1), jnp.concatenate([sv0, sv1], axis=1)]),
            sums21[4:5],
            up_sum,
            sums3[2:3],
            jnp.concatenate([sums0[0:1], sums21[2:3], sums21[0:1], sums3[0:1]]),
            jnp.concatenate([sums0[1:2], sums21[3:4], sums21[1:2], sums3[1:2]]),
        ],
        shards,
    )
    if halves:
        heads_keep, heads_got = plane_second(heads_parts, heads_got, (4,))
        up_all = spread(up_piece, 2)
        last_keep, last_got = plane_second(last_parts, last_got, (2,))
        heads_piece = across(heads_keep, heads_got)
        last_piece = across(last_keep, last_got)
        tail = small_grads.reshape(-1, width // 8)
        for mask in (1, 2, 4):
            tail = tail + swap(tail, "dp", mask)
        for mask in (1, 2):
            tail = tail + swap(tail, "fsdp", mask)
        small_sum = lax.dynamic_index_in_dim(
            tail.reshape(small_grads.shape), lax.axis_index("fsdp"), 0, keepdims=False
        )
        heads_all = spread(heads_piece, 4)
        last_all = spread(last_piece, 2)
        (down_grad,) = finish("finish_down", idx, [place_down], [down_all], [down_weight.shape])
        (up_grad,) = finish("finish_up", idx, [place_up], [up_all], [up_weight.shape])
        qkv_grad, out_grad = finish(
            "finish_heads",
            idx,
            [functools.partial(place_heads, 0), functools.partial(place_heads, 1)],
            [heads_all, last_all],
            [qkv_weight.shape, out_weight.shape],
        )
    else:
        gpacked = jnp.concatenate([gq0, gq1, gk0, gk1, gv0, gv1], axis=1)

        def reduced(left, right):
            grad = dot_tn(left, right)
            return lax.psum(lax.psum_scatter(grad, "fsdp", scatter_dimension=0, tiled=True), "dp")

        qkv_grad = reduced(normed_one, gpacked)
        out_grad = reduced(attended, gmix)
        up_grad = reduced(two, ghid)
        down_grad = reduced(act, gffn)
        small_sum = lax.dynamic_index_in_dim(
            lax.psum(small_grads, ("dp", "fsdp")), lax.axis_index("fsdp"), 0, keepdims=False
        )
    qv_g, outb_g, upb_g, downb_g, gain_g, shift_g = unpack_small(small_sum[None])
    return (
        layer_out[None],
        grad_input[None],
        qkv_grad,
        qv_g,
        out_grad,
        outb_g[0],
        up_grad,
        upb_g[0],
        down_grad,
        downb_g[0],
        gain_g,
        shift_g,
    )


def solution(mesh):
    rows = P(("dp", "fsdp"), None, None)
    split = P("fsdp", None)
    placed = (
        rows,
        split,
        P(None, "fsdp"),
        split,
        P("fsdp"),
        split,
        P("fsdp"),
        split,
        P("fsdp"),
        P(None, "fsdp"),
        P(None, "fsdp"),
        P(("dp", "fsdp"), None),
        rows,
    )
    return jax.shard_map(
        on_device,
        mesh=mesh,
        in_specs=placed,
        out_specs=(
            rows,
            rows,
            split,
            P(None, "fsdp"),
            split,
            P("fsdp"),
            split,
            P("fsdp"),
            split,
            P("fsdp"),
            P(None, "fsdp"),
            P(None, "fsdp"),
        ),
        check_vma=False,
    )
```

time: 2360 us -> 628 us (0.27)
  waiting for transfers between devices: 1500 us -> 226 us
  matrix products: 301 us -> 0 us
  Pallas kernels: 0 us -> 279 us
  blocking collectives: 173 us -> 0 us
  local copies, waits for them, and re-layouts: 197 us -> 30.4 us
  other arithmetic: 130 us -> 24.8 us
  starting transfers between devices: 0.82 us -> 55.9 us
  loops' own time: 34.7 us -> 0 us
    reduce_scatter x4 -> x0, waiting for transfers between devices: 937 us -> none  [the longest x1 364 us: on_device(): lax.psum_scatter(moved[4], ('dp', 'fsdp'), scatter_dimension=0, tiled=True)]
    unnamed x17 -> x0, waiting for transfers between devices: 303 us -> none
    dot_general x68 -> x0, matrix products: 301 us -> none  [the longest x16 43.8 us: block_scores(): jnp.einsum('qhd,khd->hqk', query_block, keys, preferred_element_type=jnp....]
    pallas_call x0 -> x24, Pallas kernels: none -> 279 us  [the longest x8 72.7 us: grad_call(): pl.pallas_call(functools.partial(grad_kernel, keep, groups, split, first)...]
    all_gather x7 -> x0, waiting for transfers between devices: 265 us -> none  [the longest x1 127 us: on_device(): lax.all_gather(down_weight, 'fsdp', axis=0, tiled=True)]
    ppermute x0 -> x66, waiting for transfers between devices: none -> 226 us  [swap(): return lax.ppermute(arr, axis, [(i, i ^ mask) for i in range(size)])]
    all_gather x11 -> x0, blocking collectives: 121 us -> none  [the longest x1 17.5 us: on_device(): lax.all_gather(up_bias, 'fsdp', axis=0, tiled=True)]
    reduce_sum x25 -> x0, other arithmetic: 58.3 us -> none  [the longest x7 21.6 us: normalize(): return centre * lax.rsqrt(spread + norm_eps) * gain + shift]
  transfers between devices with their start and end apart: 14 -> 66, of which waited for: 13 -> 25; matrix products, arithmetic and copies ran while one was open for 12% -> 7% of each run, Pallas kernels for 0% -> 30%
where the time goes in v1:
time: 628 us; the launch traced here: 619 us
  Pallas kernels  279 us (44%)
  waiting for transfers between devices  226 us (36%)
  starting transfers between devices  55.9 us (9%)
  local copies, waits for them, and re-layouts  30.4 us (5%)
  other arithmetic  24.8 us (4%)
    ppermute x66, waiting for transfers between devices, swap(): return lax.ppermute(arr, axis, [(i, i ^ mask) for i in range(size)])  226 us
    pallas_call x8, Pallas kernels, grad_call(): pl.pallas_call(functools.partial(grad_kernel, keep, groups, split, first)...  72.7 us
    ppermute x66, starting transfers between devices, swap(): return lax.ppermute(arr, axis, [(i, i ^ mask) for i in range(size)])  55.9 us
    pallas_call x2, Pallas kernels, attend_back(): pl.pallas_call(attend_back_kernel, grid=(pairs,), in_specs=[blk(skip), bl...  35.9 us
    pallas_call x1, Pallas kernels, mid_backward(): pl.pallas_call(mid_kernel, grid=(tokens // BLOCK,), in_specs=[pl.BlockSpe...  23.7 us
    pallas_call x3, Pallas kernels, place(): pl.pallas_call(functools.partial(place_kernel, layout, masks, shards, len...  22.9 us
    pallas_call x1, Pallas kernels, up_forward(): pl.pallas_call(up_kernel, grid=(cols // bn,), in_specs=[pl.BlockSpec((tok...  20.8 us
    pallas_call x1, Pallas kernels, attend(): pl.pallas_call(attend_kernel, grid=(pairs,), in_specs=[blk(0), blk(pairs)...  20.1 us
  transfers between devices with their start and end apart: 66, of which 25 were waited for; matrix products, arithmetic and copies ran while one was open for 7% of the time, Pallas kernels for 30%

profile of v1, /device:TPU:0, one launch (start us, length us, event | category | flops | bytes accessed | tf_op | source)
XLA Modules:
  0.0 618.7 jit_solution(6719080349793177900)
XLA Ops:
  6.4 5.1 collective-permute-start.2
  20.5 8.5 %collective-permute-done.1 = bf16[32,3200]{1,0:T(8,128)(2,1)S(1)} collective-permute-done((bf16[32,3200]{1,0:T(8,128)(2,1)S(1)}, bf16[32,3200]{1,0:T(8,128)(2,1)S(1)}, u32[]{:S(2)}, u32[]{:S(2)}) %collective-permute-start.1) | collective-permute-done | bytes 204832 | tf_op jit(solution)/shard_map/ppermute | solution.py:466
  29.0 2.6 collective-permute-start.9
  35.8 5.8 collective-permute-done.9
  41.6 16.8 %collective-permute-done.8 = bf16[32,5120]{1,0:T(8,128)(2,1)S(1)} collective-permute-done((bf16[32,5120]{1,0:T(8,128)(2,1)S(1)}, bf16[32,5120]{1,0:T(8,128)(2,1)S(1)}, u32[]{:S(2)}, u32[]{:S(2)}) %collective-permute-start.8) | collective-permute-done | bytes 327712 | tf_op jit(solution)/shard_map/ppermute | solution.py:466
  60.1 2.7 collective-permute-start.14
  66.1 3.4 collective-permute-done.16
  69.5 10.8 %collective-permute-done.15 = bf16[128,1024]{1,0:T(8,128)(2,1)S(1)} collective-permute-done((bf16[128,1024]{1,0:T(8,128)(2,1)S(1)}, bf16[128,1024]{1,0:T(8,128)(2,1)S(1)}, u32[]{:S(2)}, u32[]{:S(2)}) %collective-permute-start.15) | collective-permute-done | bytes 262176 | tf_op jit(solution)/shard_map/ppermute | solution.py:466
  87.3 13.6 %collective-permute-done.17 = bf16[3,128,1024]{2,1,0:T(8,128)(2,1)S(1)} collective-permute-done((bf16[3,128,1024]{2,1,0:T(8,128)(2,1)S(1)}, bf16[3,128,1024]{2,1,0:T(8,128)(2,1)S(1)}, u32[]{:S(2)}, u32[]{:S(2)}) %collective-permute-start.17) | collective-permute-done | bytes 786464 | tf_op jit(solution)/shard_map/ppermute | solution.py:466
  102.8 23.3 %collective-permute-done.4.refs_2_ = bf16[6,32,3072]{2,1,0:T(8,128)(2,1)S(1)} collective-permute-done((bf16[6,32,3072]{2,1,0:T(8,128)(2,1)S(1)}, bf16[6,32,3072]{2,1,0:T(8,128)(2,1)S(1)}, u32[]{:S(2)}, u32[]{:S(2)}) %collective-permute-start.4) | collective-permute-done | bytes 1179680 | tf_op jit(solution)/shard_map/ppermute | solution.py:466
  127.3 37.7 %collective-permute-done.11.refs_3_ = bf16[6,32,5120]{2,1,0:T(8,128)(2,1)} collective-permute-done((bf16[6,32,5120]{2,1,0:T(8,128)(2,1)S(1)}, bf16[6,32,5120]{2,1,0:T(8,128)(2,1)}, u32[]{:S(2)}, u32[]{:S(2)}) %collective-permute-start.11) | collective-permute-done | bytes 1966112 | tf_op jit(solution)/shard_map/ppermute | solution.py:466
  170.2 6.2 %place.3.w_ref.refs_6_ = bf16[1024,3072]{1,0:T(8,128)(2,1)} custom-call(s32[2]{0:T(128)} %pad_add_fusion.idx_ref, bf16[256,3072]{1,0:T(8,128)(2,1)} %refs_0_.3, bf16[6,32,3072]{2,1,0:T(8,128)(2,1)} %copy-done.2, bf16[6,32,3072]{2,1,0:T(8,128)(2,1)} %copy-done.8, bf16[6,32,3072]{2,1,0:T(8,128)(2,1)} %copy-done.9, ...), custom_call_target="tpu_custom_call" | custom-call | bytes 12582912 | tf_op jit(solution)/shard_map/place/pallas_call | solution.py:528
  176.5 12.9 %qkv_forward.1 = (bf16[1024,1024]{1,0:T(8,128)(2,1)}, bf16[1024,3072]{1,0:T(8,128)(2,1)}) custom-call(bf16[1024,1024]{1,0:T(8,128)(2,1)} %bitcast.253, bf16[1024,3072]{1,0:T(8,128)(2,1)} %place.3.w_ref.refs_6_, f32[1,3072]{1,0:T(1,128)} %pad_maximum_fusion.17.bias_ref, f32[1,1024]{1,0:T(1,128)} %bitcast.241, f32[1,1024]{1,0:T(1,128)} %bitcast.242), custom_call_target="tpu_custom_call" | custom-call | flops 6442450944 | bytes 12582912 | tf_op jit(solution)/shard_map/qkv_forward/pallas_call | solution.py:81
  189.4 20.1 %attend.1 = (bf16[1024,1024]{1,0:T(8,128)(2,1)}, f32[8,2,1024]{2,1,0:T(2,128)}) custom-call(bf16[1024,3072]{1,0:T(8,128)(2,1)} %get-tuple-element.96.q_ref.k_ref.v_ref, bf16[1024,3072]{1,0:T(8,128)(2,1)} %get-tuple-element.96.q_ref.k_ref.v_ref, bf16[1024,3072]{1,0:T(8,128)(2,1)} %get-tuple-element.96.q_ref.k_ref.v_ref, s32[1,1024]{1,0:T(1,128)} %bitcast.236), custom_call_target="tpu_custom_call" | custom-call | flops 8589934592 | bytes 8388608 | tf_op jit(solution)/shard_map/attend/pallas_call | solution.py:375
  209.5 7.6 %place.5.w_ref = bf16[4096,1024]{1,0:T(8,128)(2,1)} custom-call(s32[2]{0:T(128)} %pad_add_fusion.idx_ref, bf16[1024,1024]{1,0:T(8,128)(2,1)} %refs_0_.5, bf16[6,128,1024]{2,1,0:T(8,128)(2,1)} %copy-done.1, bf16[6,128,1024]{2,1,0:T(8,128)(2,1)} %collective-permute-done.18.refs_2_, bf16[6,128,1024]{2,1,0:T(8,128)(2,1)} %collective-permute-done.19.refs_3_, ...), custom_call_target="tpu_custom_call" | custom-call | bytes 16777216 | tf_op jit(solution)/shard_map/place/pallas_call | solution.py:528
  217.1 9.1 %place.4 = (bf16[1024,1024]{1,0:T(8,128)(2,1)}, bf16[1024,4096]{1,0:T(8,128)(2,1)}) custom-call(s32[2]{0:T(128)} %pad_add_fusion.idx_ref, bf16[256,1024]{1,0:T(8,128)(2,1)} %refs_0_.4, bf16[256,4096]{1,0:T(8,128)(2,1)} %refs_1_.1, bf16[6,32,5120]{2,1,0:T(8,128)(2,1)} %copy-done, bf16[6,32,5120]{2,1,0:T(8,128)(2,1)} %collective-permute-done.11.refs_3_, ...), custom_call_target="tpu_custom_call" | custom-call | bytes 20971520 | tf_op jit(solution)/shard_map/place/pallas_call | solution.py:528
  226.2 8.5 %out_forward.1 = (f32[1024,1024]{1,0:T(8,128)}, f32[1024,1024]{1,0:T(8,128)}, bf16[1024,1024]{1,0:T(8,128)(2,1)}) custom-call(bf16[1024,1024]{1,0:T(8,128)(2,1)} %get-tuple-element.97.att_ref.o_ref.refs_7_.refs_8_.refs_9_.refs_10_, bf16[1024,1024]{1,0:T(8,128)(2,1)} %bitcast.254, bf16[1024,1024]{1,0:T(8,128)(2,1)} %get-tuple-element.102.w_ref.out_w_ref, ...), custom_call_target="tpu_custom_call" | custom-call | flops 2147483648 | bytes 16777216 | tf_op jit(solution)/shard_map/out_forward/pallas_call | solution.py:116
  234.7 20.8 %up_forward.1 = (bf16[1024,4096]{1,0:T(8,128)(2,1)}, bf16[1024,4096]{1,0:T(8,128)(2,1)}) custom-call(bf16[1024,1024]{1,0:T(8,128)(2,1)} %get-tuple-element.103.two_ref.refs_0_, bf16[1024,4096]{1,0:T(8,128)(2,1)} %get-tuple-element.104.w_ref.up_ref, f32[1,4096]{1,0:T(1,128)} %bitcast.229), custom_call_target="tpu_custom_call" | custom-call | flops 8589934592 | bytes 25165824 | tf_op jit(solution)/shard_map/up_forward/pallas_call | solution.py:144
  255.4 18.7 %down_forward.1 = (bf16[1024,1024]{1,0:T(8,128)(2,1)}, bf16[1024,1024]{1,0:T(8,128)(2,1)}, f32[8,1024]{1,0:T(8,128)}) custom-call(bf16[1024,4096]{1,0:T(8,128)(2,1)} %get-tuple-element.113.act_ref.refs_0_.refs_1_.refs_2_.refs_3_, bf16[4096,1024]{1,0:T(8,128)(2,1)} %place.5.w_ref, f32[1,1024]{1,0:T(1,128)} %bitcast.239, ...), custom_call_target="tpu_custom_call" | custom-call | flops 8589934592 | bytes 16777216 | tf_op jit(solution)/shard_map/down_forward/pallas_call | solution.py:187
  274.1 9.2 %grad_down_send.1 = bf16[4,4,2,128,512]{4,3,2,1,0:T(8,128)(2,1)} custom-call(s32[2]{0:T(128)} %pad_add_fusion.idx_ref, bf16[1024,4096]{1,0:T(8,128)(2,1)} %get-tuple-element.113.act_ref.refs_0_.refs_1_.refs_2_.refs_3_, bf16[1024,4096]{1,0:T(8,128)(2,1)} %get-tuple-element.113.act_ref.refs_0_.refs_1_.refs_2_.refs_3_, ...), custom_call_target="tpu_custom_call" | custom-call | flops 4294967296 | bytes 10737418 | tf_op jit(solution)/shard_map/grad_down_send/pallas_call | solution.py:605
  283.9 16.6 %hidden_backward.1 = (bf16[1024,4096]{1,0:T(8,128)(2,1)}, f32[1,4096]{1,0:T(1,128)}) custom-call(bf16[1024,1024]{1,0:T(8,128)(2,1)} %get-tuple-element.110.refs_4_.grad_ref, bf16[4096,1024]{1,0:T(8,128)(2,1)} %place.5.w_ref, bf16[1024,4096]{1,0:T(8,128)(2,1)} %get-tuple-element.111.slope_ref), custom_call_target="tpu_custom_call" | custom-call | flops 8589934592 | bytes 25165824 | tf_op jit(solution)/shard_map/hidden_backward/pallas_call | solution.py:219
  300.5 10.9 %grad_down_keep.1 = (bf16[2,4,128,512]{3,2,1,0:T(8,128)(2,1)}, bf16[2,4,128,512]{3,2,1,0:T(8,128)(2,1)}, bf16[2,4,128,512]{3,2,1,0:T(8,128)(2,1)}, bf16[2,4,128,512]{3,2,1,0:T(8,128)(2,1)}) custom-call(s32[2]{0:T(128)} %pad_add_fusion.idx_ref, bf16[1024,4096]{1,0:T(8,128)(2,1)} %get-tuple-element.113.act_ref.refs_0_.refs_1_.refs_2_.refs_3_, ...), custom_call_target="tpu_custom_call" | custom-call | flops 4294967296 | bytes 10737418 | tf_op jit(solution)/shard_map/grad_down_keep/pallas_call | solution.py:605
  311.4 9.3 %grad_up_send.1 = bf16[4,4,2,128,512]{4,3,2,1,0:T(8,128)(2,1)} custom-call(s32[2]{0:T(128)} %pad_add_fusion.idx_ref, bf16[1024,1024]{1,0:T(8,128)(2,1)} %get-tuple-element.103.two_ref.refs_0_, bf16[1024,4096]{1,0:T(8,128)(2,1)} %get-tuple-element.122.refs_1_.gh_ref), custom_call_target="tpu_custom_call" | custom-call | flops 4294967296 | bytes 10737418 | tf_op jit(solution)/shard_map/grad_up_send/pallas_call | solution.py:605
  325.9 23.7 %mid_backward.1 = (f32[1024,1024]{1,0:T(8,128)}, bf16[1024,1024]{1,0:T(8,128)(2,1)}, bf16[1024,1024]{1,0:T(8,128)(2,1)}, f32[8,1024]{1,0:T(8,128)}) custom-call(bf16[1024,4096]{1,0:T(8,128)(2,1)} %get-tuple-element.122.refs_1_.gh_ref, bf16[1024,4096]{1,0:T(8,128)(2,1)} %get-tuple-element.104.w_ref.up_ref, ...), custom_call_target="tpu_custom_call" | custom-call | flops 10737418240 | bytes 16777216 | tf_op jit(solution)/shard_map/mid_backward/pallas_call | solution.py:266
  356.1 10.8 %grad_up_keep.1 = (bf16[2,4,128,512]{3,2,1,0:T(8,128)(2,1)}, bf16[2,4,128,512]{3,2,1,0:T(8,128)(2,1)}, bf16[2,4,128,512]{3,2,1,0:T(8,128)(2,1)}, bf16[2,4,128,512]{3,2,1,0:T(8,128)(2,1)}) custom-call(s32[2]{0:T(128)} %pad_add_fusion.idx_ref, bf16[1024,1024]{1,0:T(8,128)(2,1)} %get-tuple-element.103.two_ref.refs_0_, ...), custom_call_target="tpu_custom_call" | custom-call | flops 4294967296 | bytes 10737418 | tf_op jit(solution)/shard_map/grad_up_keep/pallas_call | solution.py:605
  369.9 17.8 %attend_back.2 = (bf16[1024,512]{1,0:T(8,128)(2,1)}, bf16[1024,512]{1,0:T(8,128)(2,1)}, bf16[1024,512]{1,0:T(8,128)(2,1)}, f32[1,512]{1,0:T(1,128)}, f32[1,512]{1,0:T(1,128)}) custom-call(bf16[1024,3072]{1,0:T(8,128)(2,1)} %get-tuple-element.96.q_ref.k_ref.v_ref, bf16[1024,3072]{1,0:T(8,128)(2,1)} %get-tuple-element.96.q_ref.k_ref.v_ref, ...), custom_call_target="tpu_custom_call" | custom-call | flops 10737418240 | bytes 8388608 | tf_op jit(solution)/shard_map/attend_back/pallas_call | solution.py:443
  387.7 8.5 %grad_heads_send.2 = bf16[4,4,1,128,640]{4,3,2,1,0:T(8,128)(2,1)} custom-call(s32[2]{0:T(128)} %pad_add_fusion.idx_ref, bf16[1024,1024]{1,0:T(8,128)(2,1)} %get-tuple-element.138.refs_0_.refs_1_.refs_2_.refs_3_, bf16[1024,1024]{1,0:T(8,128)(2,1)} %get-tuple-element.138.refs_0_.refs_1_.refs_2_.refs_3_, ...), custom_call_target="tpu_custom_call" | custom-call | flops 2684354560 | bytes 6710886 | tf_op jit(solution)/shard_map/grad_heads_send/pallas_call | solution.py:605
  397.4 18.0 %attend_back.3 = (bf16[1024,512]{1,0:T(8,128)(2,1)}, bf16[1024,512]{1,0:T(8,128)(2,1)}, bf16[1024,512]{1,0:T(8,128)(2,1)}, f32[1,512]{1,0:T(1,128)}, f32[1,512]{1,0:T(1,128)}) custom-call(bf16[1024,3072]{1,0:T(8,128)(2,1)} %get-tuple-element.96.q_ref.k_ref.v_ref, bf16[1024,3072]{1,0:T(8,128)(2,1)} %get-tuple-element.96.q_ref.k_ref.v_ref, ...), custom_call_target="tpu_custom_call" | custom-call | flops 10737418240 | bytes 8388608 | tf_op jit(solution)/shard_map/attend_back/pallas_call | solution.py:443
  421.4 10.6 %collective-permute-done.53 = bf16[4,128,512]{2,1,0:T(8,128)(2,1)S(1)} collective-permute-done((bf16[4,128,512]{2,1,0:T(8,128)(2,1)S(1)}, bf16[4,128,512]{2,1,0:T(8,128)(2,1)S(1)}, u32[]{:S(2)}, u32[]{:S(2)}) %collective-permute-start.53) | collective-permute-done | bytes 524320 | tf_op jit(solution)/shard_map/ppermute | solution.py:466
  435.4 16.5 %collective-permute-done.54 = bf16[2,2,128,512]{3,2,1,0:T(8,128)(2,1)S(1)} collective-permute-done((bf16[2,2,128,512]{3,2,1,0:T(8,128)(2,1)S(1)}, bf16[2,2,128,512]{3,2,1,0:T(8,128)(2,1)S(1)}, u32[]{:S(2)}, u32[]{:S(2)}) %collective-permute-start.54) | collective-permute-done | bytes 524320 | tf_op jit(solution)/shard_map/ppermute | solution.py:466
  452.0 9.7 %grad_heads_keep.3 = (bf16[2,4,128,640]{3,2,1,0:T(8,128)(2,1)}, bf16[2,4,128,640]{3,2,1,0:T(8,128)(2,1)}) custom-call(s32[2]{0:T(128)} %pad_add_fusion.idx_ref, bf16[1024,1024]{1,0:T(8,128)(2,1)} %get-tuple-element.138.refs_0_.refs_1_.refs_2_.refs_3_, bf16[1024,1024]{1,0:T(8,128)(2,1)} %get-tuple-element.138.refs_0_.refs_1_.refs_2_.refs_3_, ...), custom_call_target="tpu_custom_call" | custom-call | flops 2684354560 | bytes 6710886 | tf_op jit(solution)/shard_map/grad_heads_keep/pallas_call | solution.py:605
  463.2 6.7 %grad_heads_send.3 = bf16[4,4,1,128,384]{4,3,2,1,0:T(8,128)(2,1)} custom-call(s32[2]{0:T(128)} %pad_add_fusion.idx_ref, bf16[1024,1024]{1,0:T(8,128)(2,1)} %get-tuple-element.138.refs_0_.refs_1_.refs_2_.refs_3_, bf16[1024,1024]{1,0:T(8,128)(2,1)} %get-tuple-element.138.refs_0_.refs_1_.refs_2_.refs_3_, ...), custom_call_target="tpu_custom_call" | custom-call | flops 1610612736 | bytes 4026531 | tf_op jit(solution)/shard_map/grad_heads_send/pallas_call | solution.py:605
  471.3 12.9 %collective-permute-done.55 = bf16[2,128,512]{2,1,0:T(8,128)(2,1)S(1)} collective-permute-done((bf16[2,128,512]{2,1,0:T(8,128)(2,1)S(1)}, bf16[2,128,512]{2,1,0:T(8,128)(2,1)S(1)}, u32[]{:S(2)}, u32[]{:S(2)}) %collective-permute-start.55) | collective-permute-done | bytes 262176 | tf_op jit(solution)/shard_map/ppermute | solution.py:466
  486.4 10.4 %collective-permute-done.62 = bf16[2,128,512]{2,1,0:T(8,128)(2,1)S(1)} collective-permute-done((bf16[2,128,512]{2,1,0:T(8,128)(2,1)S(1)}, bf16[2,128,512]{2,1,0:T(8,128)(2,1)S(1)}, u32[]{:S(2)}, u32[]{:S(2)}) %collective-permute-start.62) | collective-permute-done | bytes 262176 | tf_op jit(solution)/shard_map/ppermute | solution.py:466
  501.6 7.5 %grad_heads_keep.2 = (bf16[2,4,128,384]{3,2,1,0:T(8,128)(2,1)}, bf16[2,4,128,384]{3,2,1,0:T(8,128)(2,1)}) custom-call(s32[2]{0:T(128)} %pad_add_fusion.idx_ref, bf16[1024,1024]{1,0:T(8,128)(2,1)} %get-tuple-element.138.refs_0_.refs_1_.refs_2_.refs_3_, bf16[1024,1024]{1,0:T(8,128)(2,1)} %get-tuple-element.138.refs_0_.refs_1_.refs_2_.refs_3_, ...), custom_call_target="tpu_custom_call" | custom-call | flops 1610612736 | bytes 4026531 | tf_op jit(solution)/shard_map/grad_heads_keep/pallas_call | solution.py:605
  510.5 14.6 %input_backward.1 = (f32[1024,1024]{1,0:T(8,128)}, f32[8,1024]{1,0:T(8,128)}) custom-call(bf16[1024,512]{1,0:T(8,128)(2,1)} %get-tuple-element.137.refs_4_.refs_0_, bf16[1024,512]{1,0:T(8,128)(2,1)} %get-tuple-element.149.refs_4_.refs_1_, bf16[1024,512]{1,0:T(8,128)(2,1)} %get-tuple-element.139.refs_5_.refs_2_, ...), custom_call_target="tpu_custom_call" | custom-call | flops 6442450944 | bytes 20971520 | tf_op jit(solution)/shard_map/input_backward/pallas_call | solution.py:314
  532.1 7.4 %collective-permute-done.39 = bf16[2,4,128,384]{3,2,1,0:T(8,128)(2,1)} collective-permute-done((bf16[2,4,128,384]{3,2,1,0:T(8,128)(2,1)}, bf16[2,4,128,384]{3,2,1,0:T(8,128)(2,1)}, u32[]{:S(2)}, u32[]{:S(2)}) %collective-permute-start.39) | collective-permute-done | bytes 786464 | tf_op jit(solution)/shard_map/ppermute | solution.py:466
  542.9 9.3 %collective-permute-done.40 = bf16[4,128,384]{2,1,0:T(8,128)(2,1)S(1)} collective-permute-done((bf16[4,128,384]{2,1,0:T(8,128)(2,1)S(1)}, bf16[4,128,384]{2,1,0:T(8,128)(2,1)S(1)}, u32[]{:S(2)}, u32[]{:S(2)}) %collective-permute-start.40) | collective-permute-done | bytes 393248 | tf_op jit(solution)/shard_map/ppermute | solution.py:466
  553.3 8.0 %collective-permute-done.34 = bf16[1,128,640]{2,1,0:T(8,128)(2,1)S(1)} collective-permute-done((bf16[1,128,640]{2,1,0:T(8,128)(2,1)S(1)}, bf16[1,128,640]{2,1,0:T(8,128)(2,1)S(1)}, u32[]{:S(2)}, u32[]{:S(2)}) %collective-permute-start.34) | collective-permute-done | bytes 163872 | tf_op jit(solution)/shard_map/ppermute | solution.py:466
  561.4 6.8 %collective-permute-done.41 = bf16[2,1,128,384]{3,2,1,0:T(8,128)(2,1)S(1)} collective-permute-done((bf16[2,1,128,384]{3,2,1,0:T(8,128)(2,1)S(1)}, bf16[2,1,128,384]{3,2,1,0:T(8,128)(2,1)S(1)}, u32[]{:S(2)}, u32[]{:S(2)}) %collective-permute-start.41) | collective-permute-done | bytes 196640 | tf_op jit(solution)/shard_map/ppermute | solution.py:466
  569.4 4.1 collective-permute-done.35
  576.2 3.8 collective-permute-done.42
  582.2 6.5 %collective-permute-done.43 = bf16[1,128,384]{2,1,0:T(8,128)(2,1)S(1)} collective-permute-done((bf16[1,128,384]{2,1,0:T(8,128)(2,1)S(1)}, bf16[1,128,384]{2,1,0:T(8,128)(2,1)S(1)}, u32[]{:S(2)}, u32[]{:S(2)}) %collective-permute-start.43) | collective-permute-done | bytes 98336 | tf_op jit(solution)/shard_map/ppermute | solution.py:466
  589.9 3.6 collective-permute-done.49
  595.7 3.3 collective-permute-done.50
  601.1 3.8 finish_down.1
  605.0 3.8 finish_up.1
  614.2 4.1 finish_heads.1
  (308 shorter events, 104.2 us)
Async XLA Ops:
  6.4 14.1 %collective-permute-start.2 = (bf16[32,3200]{1,0:T(8,128)(2,1)S(1)}, bf16[32,3200]{1,0:T(8,128)(2,1)S(1)}, u32[]{:S(2)}, u32[]{:S(2)}) collective-permute-start(bf16[32,3200]{1,0:T(8,128)(2,1)S(1)} %pad_maximum_fusion.12), channel_id=1, source_target_pairs={{0,3},{1,2},{2,1},{3,0},{4,7},{5,6},{6,5},{7,4},{8,11},{9,10},{10,... | collective-permute-start | bytes 614408 | tf_op jit(solution)/shard_map/ppermute | solution.py:466
  11.5 17.4 %collective-permute-start.1 = (bf16[32,3200]{1,0:T(8,128)(2,1)S(1)}, bf16[32,3200]{1,0:T(8,128)(2,1)S(1)}, u32[]{:S(2)}, u32[]{:S(2)}) collective-permute-start(bf16[32,3200]{1,0:T(8,128)(2,1)S(1)} %pad_maximum_fusion.12), channel_id=1, source_target_pairs={{0,2},{1,3},{2,0},{3,1},{4,6},{5,7},{6,4},{7,5},{8,10},{9,11},{10,... | collective-permute-start | bytes 614408 | tf_op jit(solution)/shard_map/ppermute | solution.py:466
  11.5 17.4 %collective-permute-start = (bf16[32,3200]{1,0:T(8,128)(2,1)S(1)}, bf16[32,3200]{1,0:T(8,128)(2,1)S(1)}, u32[]{:S(2)}, u32[]{:S(2)}) collective-permute-start(bf16[32,3200]{1,0:T(8,128)(2,1)S(1)} %pad_maximum_fusion.12), channel_id=1, source_target_pairs={{0,1},{1,0},{2,3},{3,2},{4,5},{5,4},{6,7},{7,6},{8,9},{9,8},{10,11... | collective-permute-start | bytes 614408 | tf_op jit(solution)/shard_map/ppermute | solution.py:466
  31.6 26.8 %collective-permute-start.8 = (bf16[32,5120]{1,0:T(8,128)(2,1)S(1)}, bf16[32,5120]{1,0:T(8,128)(2,1)S(1)}, u32[]{:S(2)}, u32[]{:S(2)}) collective-permute-start(bf16[32,5120]{1,0:T(8,128)(2,1)S(1)} %pad_maximum_fusion.10), channel_id=1, source_target_pairs={{0,2},{1,3},{2,0},{3,1},{4,6},{5,7},{6,4},{7,5},{8,10},{9,11},{10,... | collective-permute-start | bytes 983048 | tf_op jit(solution)/shard_map/ppermute | solution.py:466
  31.6 26.8 %collective-permute-start.7 = (bf16[32,5120]{1,0:T(8,128)(2,1)S(1)}, bf16[32,5120]{1,0:T(8,128)(2,1)S(1)}, u32[]{:S(2)}, u32[]{:S(2)}) collective-permute-start(bf16[32,5120]{1,0:T(8,128)(2,1)S(1)} %pad_maximum_fusion.10), channel_id=1, source_target_pairs={{0,1},{1,0},{2,3},{3,2},{4,5},{5,4},{6,7},{7,6},{8,9},{9,8},{10,11... | collective-permute-start | bytes 983048 | tf_op jit(solution)/shard_map/ppermute | solution.py:466
  33.6 48.3 %collective-permute-start.3 = (bf16[3,32,3072]{2,1,0:T(8,128)(2,1)S(1)}, bf16[3,32,3072]{2,1,0:T(8,128)(2,1)}, u32[]{:S(2)}, u32[]{:S(2)}) collective-permute-start(bf16[3,32,3072]{2,1,0:T(8,128)(2,1)S(1)} %pad_maximum_fusion.7), channel_id=1, source_target_pairs={{0,16},{4,20},{8,24},{12,28},{16,0},{20,4},{24,8},{28,12},{1,17},{... | collective-permute-start | bytes 1769480 | tf_op jit(solution)/shard_map/ppermute | solution.py:466
  60.1 20.2 %collective-permute-start.15 = (bf16[128,1024]{1,0:T(8,128)(2,1)S(1)}, bf16[128,1024]{1,0:T(8,128)(2,1)S(1)}, u32[]{:S(2)}, u32[]{:S(2)}) collective-permute-start(bf16[128,1024]{1,0:T(8,128)(2,1)S(1)} %constant_dynamic-slice_fusion), channel_id=1, source_target_pairs={{0,2},{1,3},{2,0},{3,1},{4,6},{5,7},{6,4},{7,5},{8,10},{9,11},{10,... | collective-permute-start | bytes 786440 | tf_op jit(solution)/shard_map/ppermute | solution.py:466
  60.1 20.2 %collective-permute-start.14 = (bf16[128,1024]{1,0:T(8,128)(2,1)S(1)}, bf16[128,1024]{1,0:T(8,128)(2,1)S(1)}, u32[]{:S(2)}, u32[]{:S(2)}) collective-permute-start(bf16[128,1024]{1,0:T(8,128)(2,1)S(1)} %constant_dynamic-slice_fusion), channel_id=1, source_target_pairs={{0,1},{1,0},{2,3},{3,2},{4,5},{5,4},{6,7},{7,6},{8,9},{9,8},{10,11... | collective-permute-start | bytes 786440 | tf_op jit(solution)/shard_map/ppermute | solution.py:466
  63.9 20.4 %collective-permute-start.10 = (bf16[3,32,5120]{2,1,0:T(8,128)(2,1)}, bf16[3,32,5120]{2,1,0:T(8,128)(2,1)}, u32[]{:S(2)}, u32[]{:S(2)}) collective-permute-start(bf16[3,32,5120]{2,1,0:T(8,128)(2,1)} %pad_maximum_fusion.5), channel_id=1, source_target_pairs={{0,16},{4,20},{8,24},{12,28},{16,0},{20,4},{24,8},{28,12},{1,17},{... | collective-permute-start | bytes 2949128 | tf_op jit(solution)/shard_map/ppermute | solution.py:466
  80.4 20.5 %collective-permute-start.17 = (bf16[3,128,1024]{2,1,0:T(8,128)(2,1)S(1)}, bf16[3,128,1024]{2,1,0:T(8,128)(2,1)S(1)}, u32[]{:S(2)}, u32[]{:S(2)}) collective-permute-start(bf16[3,128,1024]{2,1,0:T(8,128)(2,1)S(1)} %pad_maximum_fusion.6), channel_id=1, source_target_pairs={{0,8},{4,12},{8,0},{12,4},{16,24},{20,28},{24,16},{28,20},{1,9},{5... | collective-permute-start | bytes 2359304 | tf_op jit(solution)/shard_map/ppermute | solution.py:466
  83.1 43.0 %collective-permute-start.4 = (bf16[6,32,3072]{2,1,0:T(8,128)(2,1)S(1)}, bf16[6,32,3072]{2,1,0:T(8,128)(2,1)S(1)}, u32[]{:S(2)}, u32[]{:S(2)}) collective-permute-start(bf16[6,32,3072]{2,1,0:T(8,128)(2,1)S(1)} %pad_maximum_fusion.4.refs_1_), channel_id=1, source_target_pairs={{0,8},{4,12},{8,0},{12,4},{16,24},{20,28},{24,16},{28,20},{1,9},{5... | collective-permute-start | bytes 3538952 | tf_op jit(solution)/shard_map/ppermute | solution.py:466
  85.8 79.2 %collective-permute-start.11 = (bf16[6,32,5120]{2,1,0:T(8,128)(2,1)S(1)}, bf16[6,32,5120]{2,1,0:T(8,128)(2,1)}, u32[]{:S(2)}, u32[]{:S(2)}) collective-permute-start(bf16[6,32,5120]{2,1,0:T(8,128)(2,1)S(1)} %pad_maximum_fusion.2.refs_2_), channel_id=1, source_target_pairs={{0,8},{4,12},{8,0},{12,4},{16,24},{20,28},{24,16},{28,20},{1,9},{5... | collective-permute-start | bytes 5898248 | tf_op jit(solution)/shard_map/ppermute | solution.py:466
  101.1 66.8 %collective-permute-start.18 = (bf16[6,128,1024]{2,1,0:T(8,128)(2,1)S(1)}, bf16[6,128,1024]{2,1,0:T(8,128)(2,1)}, u32[]{:S(2)}, u32[]{:S(2)}) collective-permute-start(bf16[6,128,1024]{2,1,0:T(8,128)(2,1)S(1)} %pad_maximum_fusion.3.refs_1_), channel_id=1, source_target_pairs={{0,16},{4,20},{8,24},{12,28},{16,0},{20,4},{24,8},{28,12},{1,17},{... | collective-permute-start | bytes 4718600 | tf_op jit(solution)/shard_map/ppermute | solution.py:466
  102.7 64.7 %collective-permute-start.5 = (bf16[6,32,3072]{2,1,0:T(8,128)(2,1)S(1)}, bf16[6,32,3072]{2,1,0:T(8,128)(2,1)S(1)}, u32[]{:S(2)}, u32[]{:S(2)}) collective-permute-start(bf16[6,32,3072]{2,1,0:T(8,128)(2,1)S(1)} %pad_maximum_fusion.4.refs_1_), channel_id=1, source_target_pairs={{0,4},{4,0},{8,12},{12,8},{16,20},{20,16},{24,28},{28,24},{1,5},{5... | collective-permute-start | bytes 3538952 | tf_op jit(solution)/shard_map/ppermute | solution.py:466
  126.2 44.0 %collective-permute-start.6 = (bf16[6,32,3072]{2,1,0:T(8,128)(2,1)S(1)}, bf16[6,32,3072]{2,1,0:T(8,128)(2,1)}, u32[]{:S(2)}, u32[]{:S(2)}) collective-permute-start(bf16[6,32,3072]{2,1,0:T(8,128)(2,1)S(1)} %collective-permute-done.4.refs_2_), channel_id=1, source_target_pairs={{0,4},{4,0},{8,12},{12,8},{16,20},{20,16},{24,28},{28,24},{1,5},{5... | collective-permute-start | bytes 3538952 | tf_op jit(solution)/shard_map/ppermute | solution.py:466
  126.9 90.2 %collective-permute-start.12 = (bf16[6,32,5120]{2,1,0:T(8,128)(2,1)S(1)}, bf16[6,32,5120]{2,1,0:T(8,128)(2,1)}, u32[]{:S(2)}, u32[]{:S(2)}) collective-permute-start(bf16[6,32,5120]{2,1,0:T(8,128)(2,1)S(1)} %pad_maximum_fusion.2.refs_2_), channel_id=1, source_target_pairs={{0,4},{4,0},{8,12},{12,8},{16,20},{20,16},{24,28},{28,24},{1,5},{5... | collective-permute-start | bytes 5898248 | tf_op jit(solution)/shard_map/ppermute | solution.py:466
  165.0 52.1 %collective-permute-start.13 = (bf16[6,32,5120]{2,1,0:T(8,128)(2,1)}, bf16[6,32,5120]{2,1,0:T(8,128)(2,1)}, u32[]{:S(2)}, u32[]{:S(2)}) collective-permute-start(bf16[6,32,5120]{2,1,0:T(8,128)(2,1)} %collective-permute-done.11.refs_3_), channel_id=1, source_target_pairs={{0,4},{4,0},{8,12},{12,8},{16,20},{20,16},{24,28},{28,24},{1,5},{5... | collective-permute-start | bytes 5898248 | tf_op jit(solution)/shard_map/ppermute | solution.py:466
  167.4 42.1 %collective-permute-start.19 = (bf16[6,128,1024]{2,1,0:T(8,128)(2,1)S(1)}, bf16[6,128,1024]{2,1,0:T(8,128)(2,1)}, u32[]{:S(2)}, u32[]{:S(2)}) collective-permute-start(bf16[6,128,1024]{2,1,0:T(8,128)(2,1)S(1)} %pad_maximum_fusion.3.refs_1_), channel_id=1, source_target_pairs={{0,4},{4,0},{8,12},{12,8},{16,20},{20,16},{24,28},{28,24},{1,5},{5... | collective-permute-start | bytes 4718600 | tf_op jit(solution)/shard_map/ppermute | solution.py:466
  167.9 41.6 %collective-permute-start.20 = (bf16[6,128,1024]{2,1,0:T(8,128)(2,1)}, bf16[6,128,1024]{2,1,0:T(8,128)(2,1)}, u32[]{:S(2)}, u32[]{:S(2)}) collective-permute-start(bf16[6,128,1024]{2,1,0:T(8,128)(2,1)} %collective-permute-done.18.refs_2_), channel_id=1, source_target_pairs={{0,4},{4,0},{8,12},{12,8},{16,20},{20,16},{24,28},{28,24},{1,5},{5... | collective-permute-start | bytes 4718600 | tf_op jit(solution)/shard_map/ppermute | solution.py:466
  283.4 17.1 %collective-permute-start.21 = (bf16[4,4,2,128,512]{4,3,2,1,0:T(8,128)(2,1)}, bf16[4,4,2,128,512]{4,3,2,1,0:T(8,128)(2,1)}, u32[]{:S(2)}, u32[]{:S(2)}) collective-permute-start(bf16[4,4,2,128,512]{4,3,2,1,0:T(8,128)(2,1)} %grad_down_send.1), channel_id=1, source_target_pairs={{0,4},{4,0},{8,12},{12,8},{16,20},{20,16},{24,28},{28,24},{1,5},{5... | collective-permute-start | bytes 12582920 | tf_op jit(solution)/shard_map/ppermute | solution.py:466
  320.7 35.4 %collective-permute-start.22 = (bf16[4,4,2,128,512]{4,3,2,1,0:T(8,128)(2,1)}, bf16[4,4,2,128,512]{4,3,2,1,0:T(8,128)(2,1)}, u32[]{:S(2)}, u32[]{:S(2)}) collective-permute-start(bf16[4,4,2,128,512]{4,3,2,1,0:T(8,128)(2,1)} %grad_up_send.1), channel_id=1, source_target_pairs={{0,4},{4,0},{8,12},{12,8},{16,20},{20,16},{24,28},{28,24},{1,5},{5... | collective-permute-start | bytes 12582920 | tf_op jit(solution)/shard_map/ppermute | solution.py:466
  322.8 27.7 %collective-permute-start.23 = (bf16[2,4,128,512]{3,2,1,0:T(8,128)(2,1)}, bf16[2,4,128,512]{3,2,1,0:T(8,128)(2,1)S(1)}, u32[]{:S(2)}, u32[]{:S(2)}) collective-permute-start(bf16[2,4,128,512]{3,2,1,0:T(8,128)(2,1)} %get-tuple-element.115), channel_id=1, source_target_pairs={{0,16},{4,20},{8,24},{12,28},{16,0},{20,4},{24,8},{28,12},{1,17},{... | collective-permute-start | bytes 3145736 | tf_op jit(solution)/shard_map/ppermute | solution.py:466
  324.4 26.2 %collective-permute-start.24 = (bf16[2,4,128,512]{3,2,1,0:T(8,128)(2,1)}, bf16[2,4,128,512]{3,2,1,0:T(8,128)(2,1)}, u32[]{:S(2)}, u32[]{:S(2)}) collective-permute-start(bf16[2,4,128,512]{3,2,1,0:T(8,128)(2,1)} %get-tuple-element.117), channel_id=1, source_target_pairs={{0,8},{4,12},{8,0},{12,4},{16,24},{20,28},{24,16},{28,20},{1,9},{5... | collective-permute-start | bytes 3145736 | tf_op jit(solution)/shard_map/ppermute | solution.py:466
  353.9 42.4 %collective-permute-start.29 = (bf16[4,128,512]{2,1,0:T(8,128)(2,1)}, bf16[4,128,512]{2,1,0:T(8,128)(2,1)S(1)}, u32[]{:S(2)}, u32[]{:S(2)}) collective-permute-start(bf16[4,128,512]{2,1,0:T(8,128)(2,1)} %get-tuple-element.180), channel_id=1, source_target_pairs={{0,16},{4,20},{8,24},{12,28},{16,0},{20,4},{24,8},{28,12},{1,17},{... | collective-permute-start | bytes 1572872 | tf_op jit(solution)/shard_map/ppermute | solution.py:466
  355.5 40.8 %collective-permute-start.28 = (bf16[4,128,512]{2,1,0:T(8,128)(2,1)}, bf16[4,128,512]{2,1,0:T(8,128)(2,1)}, u32[]{:S(2)}, u32[]{:S(2)}) collective-permute-start(bf16[4,128,512]{2,1,0:T(8,128)(2,1)} %get-tuple-element.182), channel_id=1, source_target_pairs={{0,8},{4,12},{8,0},{12,4},{16,24},{20,28},{24,16},{28,20},{1,9},{5... | collective-permute-start | bytes 1572872 | tf_op jit(solution)/shard_map/ppermute | solution.py:466
  366.9 29.5 %collective-permute-start.26 = (bf16[2,4,128,512]{3,2,1,0:T(8,128)(2,1)}, bf16[2,4,128,512]{3,2,1,0:T(8,128)(2,1)S(1)}, u32[]{:S(2)}, u32[]{:S(2)}) collective-permute-start(bf16[2,4,128,512]{3,2,1,0:T(8,128)(2,1)} %get-tuple-element.124), channel_id=1, source_target_pairs={{0,16},{4,20},{8,24},{12,28},{16,0},{20,4},{24,8},{28,12},{1,17},{... | collective-permute-start | bytes 3145736 | tf_op jit(solution)/shard_map/ppermute | solution.py:466
  368.4 28.0 %collective-permute-start.27 = (bf16[2,4,128,512]{3,2,1,0:T(8,128)(2,1)}, bf16[2,4,128,512]{3,2,1,0:T(8,128)(2,1)S(1)}, u32[]{:S(2)}, u32[]{:S(2)}) collective-permute-start(bf16[2,4,128,512]{3,2,1,0:T(8,128)(2,1)} %get-tuple-element.126), channel_id=1, source_target_pairs={{0,8},{4,12},{8,0},{12,4},{16,24},{20,28},{24,16},{28,20},{1,9},{5... | collective-permute-start | bytes 3145736 | tf_op jit(solution)/shard_map/ppermute | solution.py:466
  396.3 55.7 %collective-permute-start.25 = (bf16[4,4,1,128,640]{4,3,2,1,0:T(8,128)(2,1)}, bf16[4,4,1,128,640]{4,3,2,1,0:T(8,128)(2,1)}, u32[]{:S(2)}, u32[]{:S(2)}) collective-permute-start(bf16[4,4,1,128,640]{4,3,2,1,0:T(8,128)(2,1)} %grad_heads_send.2), channel_id=1, source_target_pairs={{0,4},{4,0},{8,12},{12,8},{16,20},{20,16},{24,28},{28,24},{1,5},{5... | collective-permute-start | bytes 7864328 | tf_op jit(solution)/shard_map/ppermute | solution.py:466
  417.7 14.4 %collective-permute-start.53 = (bf16[4,128,512]{2,1,0:T(8,128)(2,1)S(1)}, bf16[4,128,512]{2,1,0:T(8,128)(2,1)S(1)}, u32[]{:S(2)}, u32[]{:S(2)}) collective-permute-start(bf16[4,128,512]{2,1,0:T(8,128)(2,1)S(1)} %fusion.13), channel_id=1, source_target_pairs={{0,16},{4,20},{8,24},{12,28},{16,0},{20,4},{24,8},{28,12},{1,17},{... | collective-permute-start | bytes 1572872 | tf_op jit(solution)/shard_map/ppermute | solution.py:466
  418.4 14.1 %collective-permute-start.52 = (bf16[4,128,512]{2,1,0:T(8,128)(2,1)S(1)}, bf16[4,128,512]{2,1,0:T(8,128)(2,1)S(1)}, u32[]{:S(2)}, u32[]{:S(2)}) collective-permute-start(bf16[4,128,512]{2,1,0:T(8,128)(2,1)S(1)} %fusion.11), channel_id=1, source_target_pairs={{0,8},{4,12},{8,0},{12,4},{16,24},{20,28},{24,16},{28,20},{1,9},{5... | collective-permute-start | bytes 1572872 | tf_op jit(solution)/shard_map/ppermute | solution.py:466
  420.6 13.8 %collective-permute-start.60 = (bf16[2,2,128,512]{3,2,1,0:T(8,128)(2,1)S(1)}, bf16[2,2,128,512]{3,2,1,0:T(8,128)(2,1)S(1)}, u32[]{:S(2)}, u32[]{:S(2)}) collective-permute-start(bf16[2,2,128,512]{3,2,1,0:T(8,128)(2,1)S(1)} %slice.311), channel_id=1, source_target_pairs={{0,1},{1,0},{2,3},{3,2},{4,5},{5,4},{6,7},{7,6},{8,9},{9,8},{10,11... | collective-permute-start | bytes 1572872 | tf_op jit(solution)/shard_map/ppermute | solution.py:466
  432.8 19.0 %collective-permute-start.54 = (bf16[2,2,128,512]{3,2,1,0:T(8,128)(2,1)S(1)}, bf16[2,2,128,512]{3,2,1,0:T(8,128)(2,1)S(1)}, u32[]{:S(2)}, u32[]{:S(2)}) collective-permute-start(bf16[2,2,128,512]{3,2,1,0:T(8,128)(2,1)S(1)} %slice.306), channel_id=1, source_target_pairs={{0,1},{1,0},{2,3},{3,2},{4,5},{5,4},{6,7},{7,6},{8,9},{9,8},{10,11... | collective-permute-start | bytes 1572872 | tf_op jit(solution)/shard_map/ppermute | solution.py:466
  434.6 36.0 %collective-permute-start.61 = (bf16[2,128,512]{2,1,0:T(8,128)(2,1)S(1)}, bf16[2,128,512]{2,1,0:T(8,128)(2,1)S(1)}, u32[]{:S(2)}, u32[]{:S(2)}) collective-permute-start(bf16[2,128,512]{2,1,0:T(8,128)(2,1)S(1)} %fusion.24), channel_id=1, source_target_pairs={{0,2},{1,3},{2,0},{3,1},{4,6},{5,7},{6,4},{7,5},{8,10},{9,11},{10,... | collective-permute-start | bytes 786440 | tf_op jit(solution)/shard_map/ppermute | solution.py:466
  461.7 38.0 %collective-permute-start.31 = (bf16[2,4,128,640]{3,2,1,0:T(8,128)(2,1)}, bf16[2,4,128,640]{3,2,1,0:T(8,128)(2,1)S(1)}, u32[]{:S(2)}, u32[]{:S(2)}) collective-permute-start(bf16[2,4,128,640]{3,2,1,0:T(8,128)(2,1)} %get-tuple-element.154), channel_id=1, source_target_pairs={{0,16},{4,20},{8,24},{12,28},{16,0},{20,4},{24,8},{28,12},{1,17},{... | collective-permute-start | bytes 3932168 | tf_op jit(solution)/shard_map/ppermute | solution.py:466
  469.9 31.7 %collective-permute-start.30 = (bf16[4,4,1,128,384]{4,3,2,1,0:T(8,128)(2,1)}, bf16[4,4,1,128,384]{4,3,2,1,0:T(8,128)(2,1)}, u32[]{:S(2)}, u32[]{:S(2)}) collective-permute-start(bf16[4,4,1,128,384]{4,3,2,1,0:T(8,128)(2,1)} %grad_heads_send.3), channel_id=1, source_target_pairs={{0,4},{4,0},{8,12},{12,8},{16,20},{20,16},{24,28},{28,24},{1,5},{5... | collective-permute-start | bytes 4718600 | tf_op jit(solution)/shard_map/ppermute | solution.py:466
  469.9 14.3 %collective-permute-start.55 = (bf16[2,128,512]{2,1,0:T(8,128)(2,1)S(1)}, bf16[2,128,512]{2,1,0:T(8,128)(2,1)S(1)}, u32[]{:S(2)}, u32[]{:S(2)}) collective-permute-start(bf16[2,128,512]{2,1,0:T(8,128)(2,1)S(1)} %fusion.23), channel_id=1, source_target_pairs={{0,2},{1,3},{2,0},{3,1},{4,6},{5,7},{6,4},{7,5},{8,10},{9,11},{10,... | collective-permute-start | bytes 786440 | tf_op jit(solution)/shard_map/ppermute | solution.py:466
  470.6 26.2 %collective-permute-start.62 = (bf16[2,128,512]{2,1,0:T(8,128)(2,1)S(1)}, bf16[2,128,512]{2,1,0:T(8,128)(2,1)S(1)}, u32[]{:S(2)}, u32[]{:S(2)}) collective-permute-start(bf16[2,128,512]{2,1,0:T(8,128)(2,1)S(1)} %fusion.15), channel_id=1, source_target_pairs={{0,16},{4,20},{8,24},{12,28},{16,0},{20,4},{24,8},{28,12},{1,17},{... | collective-permute-start | bytes 786440 | tf_op jit(solution)/shard_map/ppermute | solution.py:466
  484.3 13.8 %collective-permute-start.56 = (bf16[2,128,512]{2,1,0:T(8,128)(2,1)S(1)}, bf16[2,128,512]{2,1,0:T(8,128)(2,1)S(1)}, u32[]{:S(2)}, u32[]{:S(2)}) collective-permute-start(bf16[2,128,512]{2,1,0:T(8,128)(2,1)S(1)} %fusion.17), channel_id=1, source_target_pairs={{0,8},{4,12},{8,0},{12,4},{16,24},{20,28},{24,16},{28,20},{1,9},{5... | collective-permute-start | bytes 786440 | tf_op jit(solution)/shard_map/ppermute | solution.py:466
  496.9 34.6 %collective-permute-start.63 = (bf16[2,2,128,512]{3,2,1,0:T(8,128)(2,1)S(1)}, bf16[2,2,128,512]{3,2,1,0:T(8,128)(2,1)}, u32[]{:S(2)}, u32[]{:S(2)}) collective-permute-start(bf16[2,2,128,512]{3,2,1,0:T(8,128)(2,1)S(1)} %pad_maximum_fusion.9.refs_0_), channel_id=1, source_target_pairs={{0,8},{4,12},{8,0},{12,4},{16,24},{20,28},{24,16},{28,20},{1,9},{5... | collective-permute-start | bytes 1572872 | tf_op jit(solution)/shard_map/ppermute | solution.py:466
  498.1 33.8 %collective-permute-start.57 = (bf16[2,2,128,512]{3,2,1,0:T(8,128)(2,1)S(1)}, bf16[2,2,128,512]{3,2,1,0:T(8,128)(2,1)}, u32[]{:S(2)}, u32[]{:S(2)}) collective-permute-start(bf16[2,2,128,512]{3,2,1,0:T(8,128)(2,1)S(1)} %pad_maximum_fusion.8.refs_0_), channel_id=1, source_target_pairs={{0,16},{4,20},{8,24},{12,28},{16,0},{20,4},{24,8},{28,12},{1,17},{... | collective-permute-start | bytes 1572872 | tf_op jit(solution)/shard_map/ppermute | solution.py:466
  500.9 25.7 %collective-permute-start.32 = (bf16[4,128,640]{2,1,0:T(8,128)(2,1)}, bf16[4,128,640]{2,1,0:T(8,128)(2,1)}, u32[]{:S(2)}, u32[]{:S(2)}) collective-permute-start(bf16[4,128,640]{2,1,0:T(8,128)(2,1)} %fusion.5), channel_id=1, source_target_pairs={{0,8},{4,12},{8,0},{12,4},{16,24},{20,28},{24,16},{28,20},{1,9},{5... | collective-permute-start | bytes 1966088 | tf_op jit(solution)/shard_map/ppermute | solution.py:466
  509.1 30.4 %collective-permute-start.39 = (bf16[2,4,128,384]{3,2,1,0:T(8,128)(2,1)}, bf16[2,4,128,384]{3,2,1,0:T(8,128)(2,1)}, u32[]{:S(2)}, u32[]{:S(2)}) collective-permute-start(bf16[2,4,128,384]{3,2,1,0:T(8,128)(2,1)} %get-tuple-element.147), channel_id=1, source_target_pairs={{0,8},{4,12},{8,0},{12,4},{16,24},{20,28},{24,16},{28,20},{1,9},{5... | collective-permute-start | bytes 2359304 | tf_op jit(solution)/shard_map/ppermute | solution.py:466
  531.3 43.6 %collective-permute-start.64 = (bf16[2,2,128,512]{3,2,1,0:T(8,128)(2,1)S(1)}, bf16[2,2,128,512]{3,2,1,0:T(8,128)(2,1)S(1)}, u32[]{:S(2)}, u32[]{:S(2)}) collective-permute-start(bf16[2,2,128,512]{3,2,1,0:T(8,128)(2,1)S(1)} %pad_maximum_fusion.9.refs_0_), channel_id=1, source_target_pairs={{0,4},{4,0},{8,12},{12,8},{16,20},{20,16},{24,28},{28,24},{1,5},{5... | collective-permute-start | bytes 1572872 | tf_op jit(solution)/shard_map/ppermute | solution.py:466
  531.5 63.2 %collective-permute-start.58 = (bf16[2,2,128,512]{3,2,1,0:T(8,128)(2,1)S(1)}, bf16[2,2,128,512]{3,2,1,0:T(8,128)(2,1)S(1)}, u32[]{:S(2)}, u32[]{:S(2)}) collective-permute-start(bf16[2,2,128,512]{3,2,1,0:T(8,128)(2,1)S(1)} %pad_maximum_fusion.8.refs_0_), channel_id=1, source_target_pairs={{0,4},{4,0},{8,12},{12,8},{16,20},{20,16},{24,28},{28,24},{1,5},{5... | collective-permute-start | bytes 1572872 | tf_op jit(solution)/shard_map/ppermute | solution.py:466
  531.9 67.7 %collective-permute-start.65 = (bf16[2,2,128,512]{3,2,1,0:T(8,128)(2,1)}, bf16[2,2,128,512]{3,2,1,0:T(8,128)(2,1)}, u32[]{:S(2)}, u32[]{:S(2)}) collective-permute-start(bf16[2,2,128,512]{3,2,1,0:T(8,128)(2,1)} %collective-permute-done.63.refs_1_), channel_id=1, source_target_pairs={{0,4},{4,0},{8,12},{12,8},{16,20},{20,16},{24,28},{28,24},{1,5},{5... | collective-permute-start | bytes 1572872 | tf_op jit(solution)/shard_map/ppermute | solution.py:466
  539.4 65.5 %collective-permute-start.59 = (bf16[2,2,128,512]{3,2,1,0:T(8,128)(2,1)}, bf16[2,2,128,512]{3,2,1,0:T(8,128)(2,1)}, u32[]{:S(2)}, u32[]{:S(2)}) collective-permute-start(bf16[2,2,128,512]{3,2,1,0:T(8,128)(2,1)} %collective-permute-done.57.refs_1_), channel_id=1, source_target_pairs={{0,4},{4,0},{8,12},{12,8},{16,20},{20,16},{24,28},{28,24},{1,5},{5... | collective-permute-start | bytes 1572872 | tf_op jit(solution)/shard_map/ppermute | solution.py:466
  580.1 18.9 %collective-permute-start.36 = (bf16[2,1,128,640]{3,2,1,0:T(8,128)(2,1)S(1)}, bf16[2,1,128,640]{3,2,1,0:T(8,128)(2,1)S(1)}, u32[]{:S(2)}, u32[]{:S(2)}) collective-permute-start(bf16[2,1,128,640]{3,2,1,0:T(8,128)(2,1)S(1)} %pad_maximum_fusion.11.refs_0_), channel_id=1, source_target_pairs={{0,8},{4,12},{8,0},{12,4},{16,24},{20,28},{24,16},{28,20},{1,9},{5... | collective-permute-start | bytes 983048 | tf_op jit(solution)/shard_map/ppermute | solution.py:466
  593.5 15.5 %collective-permute-start.44 = (bf16[2,1,128,384]{3,2,1,0:T(8,128)(2,1)S(1)}, bf16[2,1,128,384]{3,2,1,0:T(8,128)(2,1)S(1)}, u32[]{:S(2)}, u32[]{:S(2)}) collective-permute-start(bf16[2,1,128,384]{3,2,1,0:T(8,128)(2,1)S(1)} %pad_maximum_fusion.13.refs_4_), channel_id=1, source_target_pairs={{0,16},{4,20},{8,24},{12,28},{16,0},{20,4},{24,8},{28,12},{1,17},{... | collective-permute-start | bytes 589832 | tf_op jit(solution)/shard_map/ppermute | solution.py:466
  (54 other events, 772.9 us)

commit v2 on v1

v2 whole, which is shorter than its diff:
```python
import functools
import math

import jax
import jax.numpy as jnp
from jax import lax
from jax.experimental import pallas as pl
from jax.experimental.pallas import tpu as pltpu
from jax.sharding import PartitionSpec as P

F32 = jnp.float32
BF = jnp.bfloat16
SDS = jax.ShapeDtypeStruct
HEAD_DIM = 64
PAIR = 2 * HEAD_DIM
EPS = 1e-05
MASKED = -1e30
QUERY_SCALE = math.log2(math.e) / math.sqrt(HEAD_DIM)
GRAD_SCALE = 1.0 / math.sqrt(HEAD_DIM)
BLOCK = 256
GELU_A = math.sqrt(2.0 / math.pi)
GELU_B = 0.044715 * GELU_A


def params(**more):
    return pltpu.CompilerParams(vmem_limit_bytes=60 * 1024 * 1024, **more)


def cost(flops, nbytes, trans=0):
    return pl.CostEstimate(flops=int(flops) // 1, bytes_accessed=int(nbytes) // 1, transcendentals=int(trans))


def dot_nn(a, b):
    return lax.dot_general(a, b, (((1,), (0,)), ((), ())), preferred_element_type=F32)


def dot_nt(a, b):
    return lax.dot_general(a, b, (((1,), (1,)), ((), ())), preferred_element_type=F32)


def dot_tn(a, b):
    return lax.dot_general(a, b, (((0,), (0,)), ((), ())), preferred_element_type=F32)


def centred(values):
    centre = values - jnp.mean(values, axis=-1, keepdims=True)
    rstd = lax.rsqrt(jnp.mean(centre * centre, axis=-1, keepdims=True) + EPS)
    return centre * rstd, rstd


def norm_back(grad, vhat, rstd, gain):
    e = grad * gain
    mean_e = jnp.mean(e, axis=-1, keepdims=True)
    mean_ev = jnp.mean(e * vhat, axis=-1, keepdims=True)
    return (e - mean_e - vhat * mean_ev) * rstd


def col_sum(values):
    return jnp.sum(values, axis=0, keepdims=True)


def piece_copies(spec, idx_ref, own_refs, slot_refs, places, sems):
    own_spec, slot_spec = spec
    dp, z = idx_ref[0], idx_ref[1]
    copies = []

    def add(group, src, dst):
        copies.append((group, pltpu.make_async_copy(src, dst, sems.at[len(copies)])))

    for o, first, cols, group in own_spec:
        rows = own_refs[o].shape[0]
        dst = places[o].at[pl.ds(pl.multiple_of(z * rows, rows), rows), first : first + cols]
        add(group, own_refs[o].at[:, first : first + cols], dst)
    for (pair, parts), ref in zip(slot_spec, slot_refs):
        rows = ref.shape[1]
        others = ref.shape[0] // 2
        for which, mask in enumerate(pair):
            for k in range(1, others + 1):
                at = which * others + k - 1
                for o, there, here, cols, group in parts:
                    dst = pl.multiple_of((z ^ k) * own_refs[o].shape[0] + (dp ^ mask) * rows, rows)
                    add(
                        group,
                        ref.at[at, :, here : here + cols],
                        places[o].at[pl.ds(dst, rows), there : there + cols],
                    )
    return copies


def count_copies(spec, slots):
    own_spec, slot_spec = spec
    return len(own_spec) + sum(len(parts) * s.shape[0] for (_, parts), s in zip(slot_spec, slots))


def start_all(copies):
    for _, copy in copies:
        copy.start()


def wait_group(copies, group):
    for g, copy in copies:
        if g == group:
            copy.wait()


def whole_shapes(owns, shards):
    return [(o.shape[0] * shards, o.shape[1]) for o in owns]


ANY = pl.BlockSpec(memory_space=pl.ANY)
SMEM = pl.BlockSpec(memory_space=pltpu.SMEM)


def qkv_kernel(spec, n_slots, idx_ref, own_ref, *refs):
    slots = refs[:n_slots]
    x_ref, bias_ref, gain_ref, shift_ref, normed_ref, packed_ref, out_ref = refs[n_slots : n_slots + 7]
    weight, sems, out_sem = refs[n_slots + 7 :]
    step, steps = pl.program_id(0), pl.num_programs(0)
    copies = piece_copies(spec, idx_ref, [own_ref], slots, [weight], sems)
    bn = packed_ref.shape[1]

    @pl.when(step == 0)
    def _():
        start_all(copies)
        vhat, _ = centred(x_ref[...].astype(F32))
        normed_ref[...] = (vhat * gain_ref[...] + shift_ref[...]).astype(BF)
        wait_group(copies, 0)

    half = weight.shape[1] // 2

    @pl.when(step == half // bn)
    def _():
        wait_group(copies, 1)
        pltpu.make_async_copy(weight, out_ref, out_sem).start()

    block = weight[:, pl.ds(pl.multiple_of(step * bn, bn), bn)]
    out = dot_nn(normed_ref[...], block) + bias_ref[...]
    packed_ref[...] = (out * jnp.where(step < steps // 3, QUERY_SCALE, 1.0)).astype(BF)

    @pl.when(step == steps - 1)
    def _():
        pltpu.make_async_copy(weight, out_ref, out_sem).wait()


def qkv_forward(idx, own, spec, slots, shards, x, bias, gain, shift):
    tokens, width = x.shape
    ((rows, cols),) = whole_shapes([own], shards)
    bn = width // 2
    row = pl.BlockSpec((1, width), lambda j: (0, 0))
    full = pl.BlockSpec((tokens, width), lambda j: (0, 0))
    return pl.pallas_call(
        functools.partial(qkv_kernel, spec, len(slots)),
        grid=(cols // bn,),
        in_specs=[SMEM] + [ANY] * (1 + len(slots))
        + [full, pl.BlockSpec((1, bn), lambda j: (0, j)), row, row],
        out_specs=(full, pl.BlockSpec((tokens, bn), lambda j: (0, j)), ANY),
        out_shape=(SDS((tokens, width), BF), SDS((tokens, cols), BF), SDS((rows, cols), BF)),
        scratch_shapes=[
            pltpu.VMEM((rows, cols), BF),
            pltpu.SemaphoreType.DMA((count_copies(spec, slots),)),
            pltpu.SemaphoreType.DMA(()),
        ],
        compiler_params=params(),
        cost_estimate=cost(2 * tokens * width * cols, 2 * width * cols + 2 * tokens * cols),
        name="qkv_forward",
    )(idx, own, *slots, x, bias, gain, shift)


def gelu_and_slope(a):
    sq = a * a
    t = jnp.tanh(a * (sq * GELU_B + GELU_A))
    half = 0.5 * t + 0.5
    act = a * half
    slope = half + act * ((1.0 - half) * (sq * (6.0 * GELU_B) + 2.0 * GELU_A))
    return act.astype(BF), slope.astype(BF)


def up_kernel(spec, n_slots, first, idx_ref, own_out, own_up, *refs):
    slots = refs[:n_slots]
    att_ref, x_ref, outb_ref, upb_ref, gain_ref, shift_ref = refs[n_slots : n_slots + 6]
    mixed_ref, mid_ref, two_ref, act_ref, slope_ref, wout_ref, wup_ref = refs[n_slots + 6 : n_slots + 13]
    w_out, w_up, sems, out_sems = refs[n_slots + 13 :]
    step, steps = pl.program_id(0), pl.num_programs(0)
    copies = piece_copies(spec, idx_ref, [own_out, own_up], slots, [w_out, w_up], sems)
    saves = [
        pltpu.make_async_copy(w_out, wout_ref, out_sems.at[0]),
        pltpu.make_async_copy(w_up, wup_ref, out_sems.at[1]),
    ]

    @pl.when(step == 0)
    def _():
        start_all(copies)
        wait_group(copies, 0)
        saves[0].start()

    @pl.when(step == first)
    def _():
        wait_group(copies, 1)
        saves[1].start()

    @pl.when(step < first)
    def _():
        mixed = dot_nn(att_ref[...], w_out[...]) + outb_ref[...]
        mixed_ref[...] = mixed
        vhat, _ = centred(mixed)
        mid = x_ref[...].astype(F32) + vhat * gain_ref[1:2, :] + shift_ref[1:2, :]
        mid_ref[...] = mid
        vhat, _ = centred(mid)
        at = pl.ds(pl.multiple_of(step * BLOCK, BLOCK), BLOCK)
        two_ref[at, :] = (vhat * gain_ref[2:3, :] + shift_ref[2:3, :]).astype(BF)

    @pl.when(step >= first)
    def _():
        bn = act_ref.shape[1]
        at = pl.ds(pl.multiple_of((step - first) * bn, bn), bn)
        a = dot_nn(two_ref[...], w_up[:, at]) + upb_ref[...]
        act_ref[...], slope_ref[...] = gelu_and_slope(a)

    @pl.when(step == steps - 1)
    def _():
        saves[0].wait()
        saves[1].wait()


def up_forward(idx, owns, spec, slots, shards, attended, x, out_bias, up_bias, gain, shift):
    tokens, width = x.shape
    out_shape, up_shape = whole_shapes(owns, shards)
    cols = up_shape[1]
    bn = width // 2
    first = tokens // BLOCK
    tok = pl.BlockSpec((BLOCK, width), lambda i: (jnp.minimum(i, first - 1), 0))
    col = pl.BlockSpec((tokens, bn), lambda i: (0, jnp.maximum(i - first, 0)))

    def whole(arr):
        return pl.BlockSpec(arr.shape, lambda i: (0, 0))

    return pl.pallas_call(
        functools.partial(up_kernel, spec, len(slots), first),
        grid=(first + cols // bn,),
        in_specs=[SMEM] + [ANY] * (2 + len(slots))
        + [
            tok,
            tok,
            whole(out_bias),
            pl.BlockSpec((1, bn), lambda i: (0, jnp.maximum(i - first, 0))),
            whole(gain),
            whole(shift),
        ],
        out_specs=(tok, tok, pl.BlockSpec((tokens, width), lambda i: (0, 0)), col, col, ANY, ANY),
        out_shape=(
            SDS((tokens, width), F32),
            SDS((tokens, width), F32),
            SDS((tokens, width), BF),
            SDS((tokens, cols), BF),
            SDS((tokens, cols), BF),
            SDS(out_shape, BF),
            SDS(up_shape, BF),
        ),
        scratch_shapes=[
            pltpu.VMEM(out_shape, BF),
            pltpu.VMEM(up_shape, BF),
            pltpu.SemaphoreType.DMA((count_copies(spec, slots),)),
            pltpu.SemaphoreType.DMA((2,)),
        ],
        compiler_params=params(),
        cost_estimate=cost(2 * tokens * width * (cols + width), 2 * width * cols + 4 * tokens * cols),
        name="up_forward",
    )(idx, *owns, *slots, attended, x, out_bias, up_bias, gain, shift)


def down_kernel(spec, n_slots, first, idx_ref, own_ref, *refs):
    slots = refs[:n_slots]
    act_ref, slope_ref, bias_ref, mid_ref, cot_ref, live_ref, gain_ref, shift_ref = refs[n_slots : n_slots + 8]
    out_ref, grad_ref, sums_ref, hid_ref, hsum_ref, weight, sems = refs[n_slots + 8 :]
    step = pl.program_id(0)
    copies = piece_copies(spec, idx_ref, [own_ref], slots, [weight], sems)

    @pl.when(step == 0)
    def _():
        start_all(copies)
        sums_ref[...] = jnp.zeros_like(sums_ref)
        wait_group(copies, 0)

    @pl.when(step < first)
    def _():
        ffn = dot_nn(act_ref[...], weight[...]) + bias_ref[...]
        vhat, rstd = centred(ffn)
        gain = gain_ref[3:4, :]
        out_ref[...] = (mid_ref[...] + vhat * gain + shift_ref[3:4, :]).astype(BF)
        grad = cot_ref[...].astype(F32) * live_ref[...]
        low = norm_back(grad, vhat, rstd, gain).astype(BF)
        grad_ref[pl.ds(pl.multiple_of(step * BLOCK, BLOCK), BLOCK), :] = low
        sums_ref[0:1, :] += col_sum(grad * vhat)
        sums_ref[1:2, :] += col_sum(grad)
        sums_ref[2:3, :] += col_sum(low.astype(F32))

    @pl.when(step >= first)
    def _():
        bn = hid_ref.shape[1]
        at = pl.ds(pl.multiple_of((step - first) * bn, bn), bn)
        low = (dot_nt(grad_ref[...], weight[at, :]) * slope_ref[...].astype(F32)).astype(BF)
        hid_ref[...] = low
        hsum_ref[...] = col_sum(low.astype(F32))


def down_both(idx, own, spec, slots, shards, act, slope, bias, mid, cot, live, gain, shift):
    tokens, width = mid.shape
    (shape,) = whole_shapes([own], shards)
    cols = shape[0]
    bn = width // 2
    first = tokens // BLOCK

    def at(i):
        return jnp.minimum(i, first - 1)

    tok = pl.BlockSpec((BLOCK, width), lambda i: (at(i), 0))
    col = pl.BlockSpec((tokens, bn), lambda i: (0, jnp.maximum(i - first, 0)))

    def whole(arr):
        return pl.BlockSpec(arr.shape, lambda i: (0, 0))

    return pl.pallas_call(
        functools.partial(down_kernel, spec, len(slots), first),
        grid=(first + cols // bn,),
        in_specs=[SMEM] + [ANY] * (1 + len(slots))
        + [
            pl.BlockSpec((BLOCK, cols), lambda i: (at(i), 0)),
            col,
            whole(bias),
            tok,
            tok,
            pl.BlockSpec((BLOCK, 1), lambda i: (at(i), 0)),
            whole(gain),
            whole(shift),
        ],
        out_specs=(
            tok,
            pl.BlockSpec((tokens, width), lambda i: (0, 0)),
            pl.BlockSpec((8, width), lambda i: (0, 0)),
            col,
            pl.BlockSpec((1, bn), lambda i: (0, jnp.maximum(i - first, 0))),
        ),
        out_shape=(
            SDS((tokens, width), BF),
            SDS((tokens, width), BF),
            SDS((8, width), F32),
            SDS((tokens, cols), BF),
            SDS((1, cols), F32),
        ),
        scratch_shapes=[pltpu.VMEM(shape, BF), pltpu.SemaphoreType.DMA((count_copies(spec, slots),))],
        compiler_params=params(),
        cost_estimate=cost(4 * tokens * width * cols, 2 * width * cols + 6 * tokens * cols),
        name="down_both",
    )(idx, own, *slots, act, slope, bias, mid, cot, live, gain, shift)


def mid_kernel(
    gh_ref, up_ref, out_w_ref, mid_ref, mixed_ref, cot_ref, live_ref, gain_ref,
    gmid_ref, gmix_ref, gatt_ref, sums_ref,
):
    @pl.when(pl.program_id(0) == 0)
    def _():
        sums_ref[...] = jnp.zeros_like(sums_ref)

    grad = dot_nt(gh_ref[...], up_ref[...])
    vhat, rstd = centred(mid_ref[...])
    sums_ref[0:1, :] += col_sum(grad * vhat)
    sums_ref[1:2, :] += col_sum(grad)
    gmid = cot_ref[...].astype(F32) * live_ref[...] + norm_back(grad, vhat, rstd, gain_ref[2:3, :])
    gmid_ref[...] = gmid
    vhat, rstd = centred(mixed_ref[...])
    sums_ref[2:3, :] += col_sum(gmid * vhat)
    sums_ref[3:4, :] += col_sum(gmid)
    low = norm_back(gmid, vhat, rstd, gain_ref[1:2, :]).astype(BF)
    gmix_ref[...] = low
    sums_ref[4:5, :] += col_sum(low.astype(F32))
    gatt_ref[...] = dot_nt(low, out_w_ref[...]).astype(BF)


def mid_backward(gh, up, out_w, mid, mixed, cot, live, gain):
    tokens, width = mid.shape
    cols = gh.shape[1]
    tok = pl.BlockSpec((BLOCK, width), lambda i: (i, 0))

    def whole(arr):
        return pl.BlockSpec(arr.shape, lambda i: (0, 0))

    return pl.pallas_call(
        mid_kernel,
        grid=(tokens // BLOCK,),
        in_specs=[
            pl.BlockSpec((BLOCK, cols), lambda i: (i, 0)),
            whole(up),
            whole(out_w),
            tok,
            tok,
            tok,
            pl.BlockSpec((BLOCK, 1), lambda i: (i, 0)),
            whole(gain),
        ],
        out_specs=(tok, tok, tok, pl.BlockSpec((8, width), lambda i: (0, 0))),
        out_shape=(
            SDS((tokens, width), F32),
            SDS((tokens, width), BF),
            SDS((tokens, width), BF),
            SDS((8, width), F32),
        ),
        compiler_params=params(),
        cost_estimate=cost(2 * tokens * width * (cols + width), 2 * width * cols + 2 * tokens * cols),
        name="mid_backward",
    )(gh, up, out_w, mid, mixed, cot, live, gain)


def input_kernel(n_grads, n_into, *refs):
    grad_refs, (w_ref, x_ref, gmid_ref, gain_ref) = refs[:n_grads], refs[n_grads : n_grads + 4]
    out_ref, sums_ref = refs[n_grads + 4 + n_into :]

    @pl.when(pl.program_id(0) == 0)
    def _():
        sums_ref[...] = jnp.zeros_like(sums_ref)

    grads = jnp.concatenate([ref[...] for ref in grad_refs], axis=1)
    grad = dot_nt(grads, w_ref[...])
    vhat, rstd = centred(x_ref[...].astype(F32))
    sums_ref[0:1, :] += col_sum(grad * vhat)
    sums_ref[1:2, :] += col_sum(grad)
    out_ref[...] = gmid_ref[...] + norm_back(grad, vhat, rstd, gain_ref[0:1, :])


def input_backward(grads, weight, x, gmid, gain, first, count, into=None):
    tokens, width = x.shape
    tok = pl.BlockSpec((BLOCK, width), lambda i: (first + i, 0))

    def whole(arr):
        return pl.BlockSpec(arr.shape, lambda i: (0, 0))

    in_specs = [pl.BlockSpec((BLOCK, g.shape[1]), lambda i: (first + i, 0)) for g in grads]
    in_specs += [whole(weight), tok, tok, whole(gain)]
    args = [*grads, weight, x, gmid, gain]
    aliases = {}
    if into is not None:
        aliases = {len(args): 0}
        in_specs.append(pl.BlockSpec(memory_space=pl.ANY))
        args.append(into)
    return pl.pallas_call(
        functools.partial(input_kernel, len(grads), len(aliases)),
        grid=(count,),
        in_specs=in_specs,
        out_specs=(tok, pl.BlockSpec((8, width), lambda i: (0, 0))),
        out_shape=(SDS((tokens, width), F32), SDS((8, width), F32)),
        input_output_aliases=aliases,
        compiler_params=params(),
        cost_estimate=cost(6 * count * BLOCK * width * width, 6 * width * width),
        name="input_backward",
    )(*args)


def fill_bias(bias, start_ref):
    length = bias.shape[0]
    for j in range(length // BLOCK):
        key = lax.broadcasted_iota(jnp.int32, (BLOCK, length), 0) + j * BLOCK
        query = lax.broadcasted_iota(jnp.int32, (BLOCK, length), 1)
        allowed = (key <= query) & (key >= start_ref[...])
        bias[j * BLOCK : (j + 1) * BLOCK, :] = jnp.where(allowed, 0.0, MASKED)


def one_head(low, arr, head):
    zero = jnp.zeros_like(arr)
    return jnp.where(low, arr, zero) if head == 0 else jnp.where(low, zero, arr)


def attend_kernel(q_ref, k_ref, v_ref, start_ref, out_ref, lse_ref, bias):
    length = q_ref.shape[0]

    @pl.when(pl.program_id(0) == 0)
    def _():
        fill_bias(bias, start_ref)

    low = lax.broadcasted_iota(jnp.int32, (1, PAIR), 1) < HEAD_DIM
    low_rows = lax.broadcasted_iota(jnp.int32, (PAIR, 1), 0) < HEAD_DIM
    keys = k_ref[...]
    values = jnp.concatenate([v_ref[...], jnp.ones((length, PAIR), BF)], axis=1)
    for i in range(length // BLOCK):
        reach = (i + 1) * BLOCK
        sl = slice(i * BLOCK, reach)
        queries = q_ref[sl, :]
        parts = []
        for head in range(2):
            scores = dot_nt(keys[:reach], one_head(low, queries, head)) + bias[:reach, sl]
            top = jnp.max(scores, axis=0, keepdims=True)
            probs = jnp.exp2(scores - top).astype(BF)
            mixed = dot_tn(values[:reach], probs)
            total = mixed[PAIR : PAIR + 1]
            parts.append(mixed[:PAIR] / total)
            lse_ref[0, head : head + 1, sl] = top + jnp.log2(total)
        out_ref[sl, :] = jnp.where(low_rows, parts[0], parts[1]).T.astype(BF)


def attend(packed, start_row):
    length = packed.shape[0]
    pairs = packed.shape[1] // (3 * PAIR)

    def blk(offset):
        return pl.BlockSpec((length, PAIR), lambda h: (0, offset + h))

    return pl.pallas_call(
        attend_kernel,
        grid=(pairs,),
        in_specs=[blk(0), blk(pairs), blk(2 * pairs), pl.BlockSpec((1, length), lambda h: (0, 0))],
        out_specs=(blk(0), pl.BlockSpec((1, 2, length), lambda h: (h, 0, 0))),
        out_shape=(SDS((length, PAIR * pairs), BF), SDS((pairs, 2, length), F32)),
        scratch_shapes=[pltpu.VMEM((length, length), F32)],
        compiler_params=params(),
        cost_estimate=cost(8 * pairs * length * length * PAIR, 8 * length * pairs * PAIR),
        name="attend",
    )(packed, packed, packed, start_row)


def attend_back_kernel(
    q_ref, k_ref, v_ref, g_ref, o_ref, lse_ref, start_ref, gq_ref, gk_ref, gv_ref, sq_ref, sv_ref, bias, acc
):
    length = q_ref.shape[0]

    @pl.when(pl.program_id(0) == 0)
    def _():
        fill_bias(bias, start_ref)

    low = lax.broadcasted_iota(jnp.int32, (1, PAIR), 1) < HEAD_DIM
    queries, grads = q_ref[...], g_ref[...]
    q_of = [one_head(low, queries, head) for head in range(2)]
    g_of = [one_head(low, grads, head) for head in range(2)]
    inner = (grads.astype(F32) * o_ref[...].astype(F32)).T
    inner_of = [col_sum(inner[:HEAD_DIM]), col_sum(inner[HEAD_DIM:])]
    sum_v = jnp.zeros((1, PAIR), F32)
    for j in range(length // BLOCK):
        first = j * BLOCK
        sl = slice(first, first + BLOCK)
        keys, values = k_ref[sl, :], v_ref[sl, :]
        gk = gv = gq = 0.0
        for head in range(2):
            scores = dot_nt(keys, q_of[head][first:]) + bias[sl, first:]
            probs = jnp.exp2(scores - lse_ref[0, head : head + 1, first:])
            gprobs = dot_nt(values, g_of[head][first:])
            gscores = (probs * (gprobs - inner_of[head][:, first:]) * GRAD_SCALE).astype(BF)
            gv = gv + dot_nn(probs.astype(BF), g_of[head][first:])
            gk = gk + dot_nn(gscores, q_of[head][first:])
            gq = gq + dot_tn(gscores, one_head(low, keys, head))
        low_v = gv.astype(BF)
        gv_ref[sl, :] = low_v
        gk_ref[sl, :] = (gk * (1.0 / QUERY_SCALE)).astype(BF)
        sum_v = sum_v + col_sum(low_v.astype(F32))
        if j == 0:
            acc[...] = gq
        else:
            acc[first:, :] += gq
    low_q = acc[...].astype(BF)
    gq_ref[...] = low_q
    sq_ref[...] = col_sum(low_q.astype(F32))
    sv_ref[...] = sum_v


def attend_back(packed, grads, attended, lse, start_row, first, count, columns, into=None):
    length = packed.shape[0]
    total = packed.shape[1] // (3 * PAIR)

    def blk(offset):
        return pl.BlockSpec((length, PAIR), lambda h: (0, offset + h))

    row = pl.BlockSpec((1, PAIR), lambda h: (0, columns + h))
    out = blk(columns)
    grad = SDS((length, PAIR * total // 2), BF)
    sums = SDS((1, PAIR * total // 2), F32)
    in_specs = [
        blk(first),
        blk(total + first),
        blk(2 * total + first),
        blk(first),
        blk(first),
        pl.BlockSpec((1, 2, length), lambda h: (first + h, 0, 0)),
        pl.BlockSpec((1, length), lambda h: (0, 0)),
    ]
    args = [packed, packed, packed, grads, attended, lse, start_row]
    kernel, aliases = attend_back_kernel, {}
    if into is not None:
        in_specs = in_specs + [pl.BlockSpec(memory_space=pl.ANY)] * len(into)
        aliases = {len(args) + i: i for i in range(len(into))}
        args = args + list(into)

        def kernel(*refs):
            attend_back_kernel(*refs[:7], *refs[7 + len(into) :])

    return pl.pallas_call(
        kernel,
        grid=(count,),
        in_specs=in_specs,
        out_specs=(out, out, out, row, row),
        out_shape=(grad, grad, grad, sums, sums),
        input_output_aliases=aliases,
        scratch_shapes=[pltpu.VMEM((length, length), F32), pltpu.VMEM((length, PAIR), F32)],
        compiler_params=params(),
        cost_estimate=cost(20 * count * length * length * PAIR, 16 * length * count * PAIR),
        name="attend_back",
    )(*args)


def swap(arr, axis, mask):
    size = lax.axis_size(axis)
    return lax.ppermute(arr, axis, [(i, i ^ mask) for i in range(size)])


def after(first, then):
    return lax.optimization_barrier((first, then))


def shard_swaps(piece):
    return [swap(piece, "fsdp", k) for k in range(1, lax.axis_size("fsdp"))]


PLANE_MASKS = [
    (0, 4), (2, 6), (1, 5), (3, 7),
    (0, 2), (4, 6), (1, 3), (5, 7),
]


def plane_slots(two, four):
    return [a for t, f in zip(two, four) for a in (t, f, swap(t, "dp", 1), swap(f, "dp", 1))]


def plane_spec(parts):
    return [(pair, parts[i // 4]) for i, pair in enumerate(PLANE_MASKS)]


def split_down(wide, zz):
    rows, cols = wide.shape[0] // 4, wide.shape[1] // 2
    part = wide[zz * rows : (zz + 1) * rows]
    return part[:, :cols], part[:, cols:]


def split_up(wide, zz):
    rows = wide.shape[0] // 8
    return wide[2 * zz * rows : (2 * zz + 1) * rows], wide[(2 * zz + 1) * rows : (2 * zz + 2) * rows]


def side_by_side(refs):
    blocks = [r[...] for r in refs]
    return blocks[0] if len(blocks) == 1 else jnp.concatenate(blocks, axis=1)


def emit(keep, wide, split, z, chip, rest):
    if not keep:
        for zz in range(4):
            for f, part in enumerate(split(wide, zz)):
                rest[0][0, 0, zz ^ z, f] = part.astype(BF)
        return
    got_ref, outs = rest[0], rest[1:]
    for dst in range(4):

        @pl.when(chip == dst)
        def _():
            for zz in range(4):
                slot = zz ^ z
                for f, part in enumerate(split(wide, zz)):
                    bit = dst // 2 if f == 0 else dst % 2
                    low = (part + got_ref[0, 0, slot, f].astype(F32)).astype(BF)
                    outs[2 * f + bit][0, 0, slot] = low


def grad_kernel(keep, jobs, idx_ref, *refs):
    step, z = pl.program_id(0), idx_ref[1]
    at = 0
    n_in = sum(n for groups, _ in jobs for group in groups for n in group)
    rest = refs[n_in:]
    for number, (groups, split) in enumerate(jobs):
        blocks = []
        for n_left, n_right in groups:
            blocks.append((refs[at : at + n_left], refs[at + n_left : at + n_left + n_right]))
            at += n_left + n_right

        @pl.when(step // 4 == number)
        def _():
            dots = [dot_tn(side_by_side(left), side_by_side(right)) for left, right in blocks]
            wide = dots[0] if len(dots) == 1 else jnp.concatenate(dots, axis=1)
            emit(keep, wide, split, z, step % 4, rest)


def grad_call(name, idx, specs, args, jobs, piece, flops, got=None):
    keep = got is not None
    n_jobs = len(jobs)
    rows, cols = piece
    block = pl.BlockSpec((1, 1, 4, 2, rows, cols), lambda i, idx: (i % 4, i // 4, 0, 0, 0, 0))
    half = (1, 1, 4, rows, cols)
    if keep:
        along_y = (
            lambda i, idx: (jnp.minimum(i % 4, 1), i // 4, 0, 0, 0),
            lambda i, idx: (jnp.maximum(i % 4 - 2, 0), i // 4, 0, 0, 0),
        )
        along_x = (lambda i, idx: (i % 4 // 2, i // 4, 0, 0, 0),) * 2
        specs = specs + [block]
        args = args + [got]
        out_specs = tuple(pl.BlockSpec(half, m) for m in along_y + along_x)
        out_shape = (SDS((2, n_jobs, 4, rows, cols), BF),) * 4
    else:
        out_specs = block
        out_shape = SDS((4, n_jobs, 4, 2, rows, cols), BF)
    return pl.pallas_call(
        functools.partial(grad_kernel, keep, jobs),
        grid_spec=pltpu.PrefetchScalarGridSpec(
            num_scalar_prefetch=1, grid=(4 * n_jobs,), in_specs=specs, out_specs=out_specs
        ),
        out_shape=out_shape,
        compiler_params=params(),
        cost_estimate=cost(flops, flops // 400),
        name=name + ("_keep" if keep else "_send"),
    )(idx, *args)


def chip_of(i, idx):
    return (idx[0] // 2) ^ (3 - i)


def core_of(keep, idx):
    return idx[0] & 1 if keep else (idx[0] & 1) ^ 1


def grad_down(idx, act, gffn, got=None):
    tokens, width = gffn.shape
    keep = got is not None
    rows = act.shape[1] // 32

    def act_spec(zz):
        def at(i, idx):
            return (0, zz * 8 + chip_of(i, idx) * 2 + core_of(keep, idx))

        return pl.BlockSpec((tokens, rows), at)

    specs = [act_spec(0), act_spec(1), act_spec(2), act_spec(3)]
    specs += [pl.BlockSpec((tokens, width), lambda i, idx: (0, 0))]
    args = [act, act, act, act, gffn]
    flops = act.shape[1] * width * tokens
    jobs = [([(4, 1)], split_down)]
    return grad_call("grad_down", idx, specs, args, jobs, (rows, width // 2), flops, got)


def grad_up(idx, two, ghid, got=None):
    tokens, width = two.shape
    keep = got is not None
    cols = ghid.shape[1] // 8
    specs = [
        pl.BlockSpec((tokens, width), lambda i, idx: (0, 0)),
        pl.BlockSpec((tokens, cols), lambda i, idx: (0, chip_of(i, idx) * 2 + core_of(keep, idx))),
    ]
    flops = ghid.shape[1] * width * tokens
    jobs = [([(1, 1)], split_up)]
    return grad_call("grad_up", idx, specs, [two, ghid], jobs, (width // 8, cols), flops, got)


def grad_heads(idx, one, gq, gk, gv, att=None, gmix=None, got=None):
    tokens, width = one.shape
    keep = got is not None
    rows = width // 8

    def left(zz):
        return pl.BlockSpec((tokens, rows), lambda i, idx: (0, zz * 2 + core_of(keep, idx)))

    def right(cols):
        return pl.BlockSpec((tokens, cols), lambda i, idx: (0, chip_of(i, idx)))

    lefts = [left(0), left(1), left(2), left(3)]
    specs, args, groups = lefts + [right(PAIR)] * 3, [one] * 4 + [gq, gk, gv], [(4, 3)]
    cols = 3 * PAIR
    if att is not None:
        specs, args, groups = specs + lefts + [right(width // 4)], args + [att] * 4 + [gmix], groups + [(4, 1)]
        cols += width // 4
    flops = 4 * tokens * width * cols
    return grad_call("grad_heads", idx, specs, args, [(groups, split_up)], (rows // 2, cols), flops, got)


def add_low(a, b):
    return (a.astype(F32) + b.astype(F32)).astype(BF)


def add_wide(a, b):
    return a.astype(F32) + b.astype(F32)


def plane_first(parts):
    return [swap(parts[2 * f], "dp", mask) for f, mask in enumerate((4, 2))]


def plane_adds(parts, got):
    send = [add_low(parts[2 * f + 1][0], got[f][0]) for f in range(2)]
    keep = [add_low(parts[2 * f + 1][1], got[f][1]) for f in range(2)]
    return keep, send


def plane_second(parts, got):
    keep, send = plane_adds(parts, got)
    return keep, [swap(s, "dp", mask) for s, mask in zip(send, (2, 4))]


def across_first(keep, got):
    both = jnp.stack([add_wide(k, g) for k, g in zip(keep, got)], axis=2)
    return both[:, 0::2].astype(BF), swap(both[:, 1::2].astype(BF), "fsdp", 1)


def across_second(both, got):
    return add_low(both[:, 0], got[:, 0]), swap(add_low(both[:, 1], got[:, 1]), "fsdp", 2)


def spread_first(piece, first):
    return jnp.stack([piece, swap(piece, "dp", first)])


def spread_second(two, first):
    return swap(two, "dp", 6 - first)


def spread_core(two, four, first):
    second = 6 - first
    return [
        ((0, first), two),
        ((second, 6), four),
        ((1, 1 ^ first), swap(two, "dp", 1)),
        ((1 ^ second, 7), swap(four, "dp", 1)),
    ]


def place_down(dp, piece, outs):
    rows, cols = piece.shape[1], piece.shape[2]
    at = pl.ds(pl.multiple_of(dp * rows, rows), rows)
    outs[1][at, :cols] = piece[0].astype(F32)
    outs[1][at, cols:] = piece[1].astype(F32)


def place_up(dp, piece, outs):
    rows, cols = piece.shape[1], piece.shape[2]
    at = pl.ds(pl.multiple_of(dp * cols, cols), cols)
    outs[0][:rows, at] = piece[0].astype(F32)
    outs[0][rows:, at] = piece[1].astype(F32)


def place_heads(half, dp, piece, outs):
    rows = piece.shape[1]
    width = outs[0].shape[1] // 3
    chip, core = dp // 2, dp % 2
    for flow in range(2):
        at_rows = pl.ds(pl.multiple_of((core * 2 + flow) * rows, rows), rows)
        part_of = piece[flow].astype(F32)
        for part in range(3):
            at = pl.multiple_of(part * width + half * (width // 2) + chip * PAIR, PAIR)
            outs[0][at_rows, pl.ds(at, PAIR)] = part_of[:, part * PAIR : (part + 1) * PAIR]
        if half == 0:
            cols = width // 4
            at = pl.multiple_of(chip * cols, cols)
            outs[1][at_rows, pl.ds(at, cols)] = part_of[:, 3 * PAIR :]


def finish_kernel(placers, masks, idx_ref, *refs):
    ins, outs = list(refs[: sum(map(len, masks))]), refs[sum(map(len, masks)) :]
    for placer, pairs in zip(placers, masks):
        for pair in pairs:
            ref = ins.pop(0)
            for which, mask in enumerate(pair):
                placer(idx_ref[0] ^ mask, ref[which], outs)


def finish(name, idx, placers, flows, shapes):
    masks = [[m for m, _ in flow] for flow in flows]
    arrays = [a for flow in flows for _, a in flow]
    vmem = pl.BlockSpec(memory_space=pltpu.VMEM)
    return pl.pallas_call(
        functools.partial(finish_kernel, placers, masks),
        in_specs=[SMEM] + [vmem] * len(arrays),
        out_specs=(vmem,) * len(shapes),
        out_shape=tuple(SDS(s, F32) for s in shapes),
        compiler_params=params(),
        cost_estimate=cost(0, sum(6 * math.prod(s) for s in shapes)),
        name=name,
    )(idx, *arrays)


def segment_starts(lengths, length):
    ends = jnp.cumsum(lengths)
    positions = jnp.arange(length, dtype=jnp.int32)
    begun = jnp.where(ends[None, :] <= positions[:, None], ends[None, :], 0)
    return jnp.max(begun, axis=1).astype(jnp.int32), positions < ends[-1]


def eighth(shard):
    rows = shard.shape[0] // 8
    return lax.dynamic_slice_in_dim(shard, lax.axis_index("dp") * rows, rows, axis=0)


SMALL_ROWS = 16


def pack_small(qv_bias, out_bias, up_bias, down_bias, gain, shift):
    flat = [a.reshape(-1) for a in (qv_bias, out_bias, up_bias, down_bias, gain, shift)]
    return jnp.concatenate(flat)


def unpack_small(shards):
    count, total = shards.shape
    unit = total // SMALL_ROWS
    sizes = ((2, unit), (1, unit), (1, 4 * unit), (1, unit), (4, unit), (4, unit))
    out, at = [], 0
    for lead, cols in sizes:
        block = shards[:, at : at + lead * cols].reshape(count, lead, cols)
        out.append(jnp.swapaxes(block, 0, 1).reshape(lead, count * cols))
        at += lead * cols
    return out


def by_shard(rows, count):
    flat = []
    for arr in rows:
        lead, cols = arr.shape
        flat.append(
            jnp.swapaxes(arr.reshape(lead, count, cols // count), 0, 1).reshape(count, -1)
        )
    return jnp.concatenate(flat, axis=1)


def gather_small(own, got):
    z = lax.axis_index("fsdp")
    slots = jnp.stack([own] + got)
    low, high = z % 2, z // 2
    slots = jnp.where(low == 0, slots, slots[jnp.array([1, 0, 3, 2])])
    return jnp.where(high == 0, slots, slots[jnp.array([2, 3, 0, 1])])


def on_device(
    layer_input,
    qkv_weight,
    query_value_bias,
    out_weight,
    out_bias,
    up_weight,
    up_bias,
    down_weight,
    down_bias,
    norm_gain,
    norm_shift,
    doc_lengths,
    cotangent,
):
    _, tokens, width = layer_input.shape
    shards = lax.axis_size("fsdp")
    halves = shards == 4 and lax.axis_size("dp") == 8
    idx = jnp.stack([lax.axis_index("dp"), lax.axis_index("fsdp")]).astype(jnp.int32)
    x = layer_input[0]
    cot = cotangent[0]
    start, live = segment_starts(doc_lengths[0], tokens)
    start_row = start[None, :]
    live_col = live.astype(F32)[:, None]
    small_own = pack_small(query_value_bias, out_bias, up_bias, down_bias, norm_gain, norm_shift)
    tie = lax.optimization_barrier
    both = (4, 2)
    if halves:
        piece = eighth(qkv_weight)
        cols = piece.shape[1]
        extra = small_own.reshape(piece.shape[0], -1)
        got = shard_swaps(jnp.concatenate([piece, extra], axis=1))
        small = gather_small(small_own, [g[:, cols:].reshape(-1) for g in got])
        half_q = cols // 2
        q_own = [jnp.stack([g[:, :half_q] for g in got]), jnp.stack([g[:, half_q:cols] for g in got])]
        q_own, piece = after(q_own, jnp.concatenate([eighth(out_weight), eighth(up_weight)], axis=1))
        q_got = [swap(o, "dp", m) for o, m in zip(q_own, both)]
        got_u = shard_swaps(piece)
        q_two = [jnp.concatenate([o, g]) for o, g in zip(q_own, q_got)]
        q_four = [swap(t, "dp", 6 - m) for t, m in zip(q_two, both)]
        slots_q = plane_slots(q_two, q_four)
        q_four, got_u = after(q_four, got_u)
        half_u = piece.shape[1] // 2
        u_own = [jnp.stack([g[:, :half_u] for g in got_u]), jnp.stack([g[:, half_u:] for g in got_u])]
        u_own, piece = after(u_own, eighth(down_weight))
        u_got = [swap(o, "dp", m) for o, m in zip(u_own, both)]
        got_d = shard_swaps(piece)
        own_q, own_u, own_d, at, count = qkv_weight, [out_weight, up_weight], down_weight, idx, shards
    else:
        small = lax.all_gather(small_own, "fsdp", axis=0)
        own_q = lax.all_gather(qkv_weight, "fsdp", axis=0, tiled=True)
        own_u = [
            lax.all_gather(out_weight, "fsdp", axis=0, tiled=True),
            lax.all_gather(up_weight, "fsdp", axis=0, tiled=True),
        ]
        own_d = lax.all_gather(down_weight, "fsdp", axis=0, tiled=True)
        half_q, half_u, at, count = own_q.shape[1] // 2, 0, jnp.zeros_like(idx), 1
        slots_q = slots_u = slots_d = []
    qv_b, out_b, up_b, down_b, gain, shift = unpack_small(small.astype(F32))
    qkv_b = jnp.concatenate([qv_b[0:1], jnp.zeros((1, width), F32), qv_b[1:2]], axis=1)

    spec = (
        [(0, 0, half_q, 0), (0, half_q, half_q, 1)],
        plane_spec([[(0, 0, 0, half_q, 0)], [(0, half_q, 0, half_q, 1)]]) if halves else [],
    )
    normed_one, packed, w_qkv = qkv_forward(
        at, own_q, spec, slots_q, count, x, qkv_b, gain[0:1], shift[0:1]
    )
    if halves:
        packed, u_got, got_d = tie((packed, u_got, got_d))
        u_two = [jnp.concatenate([o, g]) for o, g in zip(u_own, u_got)]
        u_four = [swap(t, "dp", 6 - m) for t, m in zip(u_two, both)]
        half_d = width // 2
        d_own = [jnp.stack([g[:, :half_d] for g in got_d]), jnp.stack([g[:, half_d:] for g in got_d])]
        d_got = [swap(o, "dp", m) for o, m in zip(d_own, both)]
        u_two, d_own, packed = tie((u_two, d_own, packed))
    attended, lse = attend(packed, start_row)
    if halves:
        attended, u_four, d_got = tie((attended, u_four, d_got))
        slots_u = plane_slots(u_two, u_four)
        d_two = [jnp.concatenate([o, g]) for o, g in zip(d_own, d_got)]
        d_four = [swap(t, "dp", 6 - m) for t, m in zip(d_two, both)]
    up_cols = own_u[1].shape[1]
    rest = half_u - width
    spec = (
        [(0, 0, width, 0), (1, 0, up_cols, 1)],
        plane_spec([[(0, 0, 0, width, 0), (1, 0, width, rest, 1)], [(1, rest, 0, half_u, 1)]])
        if halves
        else [],
    )
    mixed, mid, two, act, slope, w_out, w_up = up_forward(
        at, own_u, spec, slots_u, count, attended, x, out_b, up_b, gain, shift
    )
    if halves:
        act, d_four = after(act, d_four)
        slots_d = plane_slots(d_two, d_four)
    half = width // 2
    spec = ([(0, 0, width, 0)], plane_spec([[(0, 0, 0, half, 0)], [(0, half, 0, half, 0)]]) if halves else [])
    layer_out, gffn, sums3, ghid, up_sum = down_both(
        at, own_d, spec, slots_d, count, act, slope, down_b, mid, cot, live_col, gain, shift
    )

    if halves:
        send = grad_down(idx, act, gffn)
        got_down = swap(send, "dp", 1)
        send, ghid = after(send, ghid)
        send = grad_up(idx, two, ghid)
        got_up = swap(send, "dp", 1)
        send, got_down, act = tie((send, got_down, act))
        down_parts = grad_down(idx, act, gffn, got_down)
        down_got = plane_first(down_parts)
        down_parts, ghid = after(down_parts, ghid)
    gmid, gmix, gatt, sums21 = mid_backward(ghid, w_up, w_out, mid, mixed, cot, live_col, gain)
    if halves:
        down_got, got_up, gmix = tie((down_got, got_up, gmix))
        down_keep, down_got = plane_second(down_parts, down_got)
        ghid, down_keep = after(ghid, down_keep)
        up_parts = grad_up(idx, two, ghid, got_up)
        up_got = plane_first(up_parts)
        up_parts, gatt = after(up_parts, gatt)
    pairs = width // PAIR
    back = functools.partial(attend_back, packed)
    gq0, gk0, gv0, sq0, sv0 = back(gatt, attended, lse, start_row, 0, pairs // 2, 0)
    if halves:
        gq0, gmix = after(gq0, gmix)
        send = grad_heads(idx, normed_one, gq0, gk0, gv0, attended, gmix)
        got_heads = swap(send, "dp", 1)
        up_got, send, gatt = tie((up_got, send, gatt))
        up_keep, up_got = plane_second(up_parts, up_got)
        up_keep, gatt = after(up_keep, gatt)
    gq1, gk1, gv1, sq1, sv1 = back(gatt, attended, lse, start_row, pairs // 2, pairs // 2, 0)
    if halves:
        down_got, up_got, gq1 = tie((down_got, up_got, gq1))
        keep = [jnp.concatenate(pair) for pair in zip(down_keep, up_keep)]
        got = [jnp.concatenate(pair) for pair in zip(down_got, up_got)]
        ffn_total, ffn_got = across_first(keep, got)
        ffn_total, gq1 = after(ffn_total, gq1)
        send = grad_heads(idx, normed_one, gq1, gk1, gv1)
        got_last = swap(send, "dp", 1)
        send, got_heads, gq0 = tie((send, got_heads, gq0))
        heads_parts = grad_heads(idx, normed_one, gq0, gk0, gv0, attended, gmix, got_heads)
        heads_got = plane_first(heads_parts)
        heads_parts, got_last, gq1, ffn_got = tie((heads_parts, got_last, gq1, ffn_got))
        ffn_total, ffn_got = across_second(ffn_total, ffn_got)
        ffn_total, gq1 = after(ffn_total, gq1)
        last_parts = grad_heads(idx, normed_one, gq1, gk1, gv1, got=got_last)
        last_got = plane_first(last_parts)
        last_parts, heads_got, gq1 = tie((last_parts, heads_got, gq1))
        heads_keep, heads_got = plane_second(heads_parts, heads_got)
        heads_keep, gq1 = after(heads_keep, gq1)
    grads = [gq0, gq1, gk0, gk1, gv0, gv1]
    blocks = tokens // BLOCK
    grad_input, sums0 = input_backward(grads, w_qkv, x, gmid, gain, 0, blocks // 2)
    if halves:
        sums0, heads_got, last_got, ffn_got = tie((sums0, heads_got, last_got, ffn_got))
        last_keep, last_got = plane_second(last_parts, last_got)
        heads_total, heads_got = across_first(heads_keep, heads_got)
        ffn_piece = add_low(ffn_total, ffn_got)
        last_keep, heads_total, ffn_piece, grad_input = tie((last_keep, heads_total, ffn_piece, grad_input))
    grad_input, sums0_rest = input_backward(
        grads, w_qkv, x, gmid, gain, blocks // 2, blocks // 2, grad_input
    )
    if halves:
        sums0_rest, last_got, heads_got = tie((sums0_rest, last_got, heads_got))
    sums0 = sums0 + sums0_rest
    small_grads = by_shard(
        [
            jnp.concatenate([jnp.concatenate([sq0, sq1], axis=1), jnp.concatenate([sv0, sv1], axis=1)]),
            sums21[4:5],
            up_sum,
            sums3[2:3],
            jnp.concatenate([sums0[0:1], sums21[2:3], sums21[0:1], sums3[0:1]]),
            jnp.concatenate([sums0[1:2], sums21[3:4], sums21[1:2], sums3[1:2]]),
        ],
        shards,
    )
    if halves:
        last_total, last_got = across_first(last_keep, last_got)
        heads_total, heads_got = across_second(heads_total, heads_got)
        ffn_piece, last_total = after(ffn_piece, last_total)
        down_two = spread_first(ffn_piece[0], 4)
        up_two = spread_first(ffn_piece[1], 2)
        tail = small_grads.reshape(-1, width // 8)
        tail_got = swap(tail, "dp", 1)

        last_total, last_got, heads_got, tail_got, down_two, up_two = tie(
            (last_total, last_got, heads_got, tail_got, down_two, up_two)
        )
        last_total, last_got = across_second(last_total, last_got)
        heads_two = spread_first(add_low(heads_total, heads_got)[0], 4)
        down_four = spread_second(down_two, 4)
        up_four = spread_second(up_two, 2)
        tail = tail + tail_got
        tail_got = swap(tail, "dp", 2)

        last_total, last_got, heads_two, tail_got = tie((last_total, last_got, heads_two, tail_got))
        last_two = spread_first(add_low(last_total, last_got)[0], 2)
        heads_four = spread_second(heads_two, 4)
        tail = tail + tail_got
        tail_got = swap(tail, "dp", 4)

        last_two, heads_four, tail_got, down_four, up_four = tie(
            (last_two, heads_four, tail_got, down_four, up_four)
        )
        last_four = spread_second(last_two, 2)
        tail = tail + tail_got
        tail_got = swap(tail, "fsdp", 1)
        heads_all = spread_core(heads_two, heads_four, 4)
        down_all = spread_core(down_two, down_four, 4)
        up_all = spread_core(up_two, up_four, 2)
        up_grad, down_grad = finish(
            "finish_ffn", idx, [place_down, place_up], [down_all, up_all], [up_weight.shape, down_weight.shape]
        )

        last_four, tail_got, up_grad = tie((last_four, tail_got, up_grad))
        tail = tail + tail_got
        tail_got = swap(tail, "fsdp", 2)
        last_all = spread_core(last_two, last_four, 2)
        tail = tail + tail_got
        small_sum = lax.dynamic_index_in_dim(
            tail.reshape(small_grads.shape), lax.axis_index("fsdp"), 0, keepdims=False
        )
        qkv_grad, out_grad = finish(
            "finish_heads",
            idx,
            [functools.partial(place_heads, 0), functools.partial(place_heads, 1)],
            [heads_all, last_all],
            [qkv_weight.shape, out_weight.shape],
        )
    else:
        gpacked = jnp.concatenate([gq0, gq1, gk0, gk1, gv0, gv1], axis=1)

        def reduced(left, right):
            grad = dot_tn(left, right)
            return lax.psum(lax.psum_scatter(grad, "fsdp", scatter_dimension=0, tiled=True), "dp")

        qkv_grad = reduced(normed_one, gpacked)
        out_grad = reduced(attended, gmix)
        up_grad = reduced(two, ghid)
        down_grad = reduced(act, gffn)
        small_sum = lax.dynamic_index_in_dim(
            lax.psum(small_grads, ("dp", "fsdp")), lax.axis_index("fsdp"), 0, keepdims=False
        )
    qv_g, outb_g, upb_g, downb_g, gain_g, shift_g = unpack_small(small_sum[None])
    return (
        layer_out[None],
        grad_input[None],
        qkv_grad,
        qv_g,
        out_grad,
        outb_g[0],
        up_grad,
        upb_g[0],
        down_grad,
        downb_g[0],
        gain_g,
        shift_g,
    )


def solution(mesh):
    rows = P(("dp", "fsdp"), None, None)
    split = P("fsdp", None)
    placed = (
        rows,
        split,
        P(None, "fsdp"),
        split,
        P("fsdp"),
        split,
        P("fsdp"),
        split,
        P("fsdp"),
        P(None, "fsdp"),
        P(None, "fsdp"),
        P(("dp", "fsdp"), None),
        rows,
    )
    return jax.shard_map(
        on_device,
        mesh=mesh,
        in_specs=placed,
        out_specs=(
            rows,
            rows,
            split,
            P(None, "fsdp"),
            split,
            P("fsdp"),
            split,
            P("fsdp"),
            split,
            P("fsdp"),
            P(None, "fsdp"),
            P(None, "fsdp"),
        ),
        check_vma=False,
    )
```

time: 628 us -> 496 us (0.79)
  waiting for transfers between devices: 226 us -> 89.6 us
  starting transfers between devices: 55.9 us -> 77.8 us
  Pallas kernels: 279 us -> 263 us
    ppermute x66 -> x80, waiting for transfers between devices: 226 us -> 89.6 us  [swap(): return lax.ppermute(arr, axis, [(i, i ^ mask) for i in range(size)])]
    ppermute x66 -> x80, starting transfers between devices: 55.9 us -> 77.8 us  [swap(): return lax.ppermute(arr, axis, [(i, i ^ mask) for i in range(size)])]
    pallas_call x19 -> x15, Pallas kernels: 223 us -> 209 us  [the longest x8 73.3 us: grad_call(): pl.pallas_call(functools.partial(grad_kernel, keep, jobs), grid_spec=pltp...]
    unnamed x104 -> x141, local copies, waits for them, and re-layouts: 16 us -> 17.6 us
  transfers between devices with their start and end apart: 66 -> 80, of which waited for: 25 -> 22; matrix products, arithmetic and copies ran while one was open for 7% -> 8% of each run, Pallas kernels for 30% -> 42%
where the time goes in v2:
time: 496 us; the launch traced here: 487 us
  Pallas kernels  263 us (53%)
  waiting for transfers between devices  89.6 us (18%)
  starting transfers between devices  77.8 us (16%)
  local copies, waits for them, and re-layouts  31.9 us (6%)
  other arithmetic  22.2 us (4%)
    ppermute x80, waiting for transfers between devices, swap(): return lax.ppermute(arr, axis, [(i, i ^ mask) for i in range(size)])  89.6 us
    ppermute x80, starting transfers between devices, swap(): return lax.ppermute(arr, axis, [(i, i ^ mask) for i in range(size)])  77.8 us
    pallas_call x8, Pallas kernels, grad_call(): pl.pallas_call(functools.partial(grad_kernel, keep, jobs), grid_spec=pltp...  73.3 us
    pallas_call x2, Pallas kernels, attend_back(): pl.pallas_call(kernel, grid=(count,), in_specs=in_specs, out_specs=(out,...  35.7 us
    pallas_call x1, Pallas kernels, down_both(): pl.pallas_call(functools.partial(down_kernel, spec, len(slots), first), g...  33.9 us
    pallas_call x1, Pallas kernels, up_forward(): pl.pallas_call(functools.partial(up_kernel, spec, len(slots), first), gri...  32.4 us
    pallas_call x1, Pallas kernels, mid_backward(): pl.pallas_call(mid_kernel, grid=(tokens // BLOCK,), in_specs=[pl.BlockSpe...  23.7 us
    pallas_call x1, Pallas kernels, attend(): pl.pallas_call(attend_kernel, grid=(pairs,), in_specs=[blk(0), blk(pairs)...  20.1 us
  transfers between devices with their start and end apart: 80, of which 22 were waited for; matrix products, arithmetic and copies ran while one was open for 8% of the time, Pallas kernels for 42%

profile of v2, /device:TPU:0, one launch (start us, length us, event | category | flops | bytes accessed | tf_op | source)
XLA Modules:
  0.0 487.1 jit_solution(1103674310222947072)
XLA Ops:
  6.5 5.1 %collective-permute-start.2 = (bf16[32,3200]{1,0:T(8,128)(2,1)S(1)}, bf16[32,3200]{1,0:T(8,128)(2,1)S(1)}, u32[]{:S(2)}, u32[]{:S(2)}) collective-permute-start(bf16[32,3200]{1,0:T(8,128)(2,1)S(1)} %pad_maximum_fusion.10), channel_id=1, source_target_pairs={{0,3},{1,2},{2,1},{3,0},{4,7},{5,6},{6,5},{7,4},{8,11},{9,10},{10,... | collective-permute-start | bytes 614408 | tf_op jit(solution)/shard_map/ppermute | solution.py:608
  18.6 6.2 %collective-permute-done = bf16[32,3200]{1,0:T(8,128)(2,1)S(1)} collective-permute-done((bf16[32,3200]{1,0:T(8,128)(2,1)S(1)}, bf16[32,3200]{1,0:T(8,128)(2,1)S(1)}, u32[]{:S(2)}, u32[]{:S(2)}) %collective-permute-start) | collective-permute-done | bytes 204832 | tf_op jit(solution)/shard_map/ppermute | solution.py:608
  24.8 4.2 collective-permute-done.1
  29.2 3.0 collective-permute-start.8
  38.8 3.5 collective-permute-done.5
  42.4 1.6 collective-permute-start.6
  46.8 8.1 %collective-permute-done.8 = bf16[32,5120]{1,0:T(8,128)(2,1)S(1)} collective-permute-done((bf16[32,5120]{1,0:T(8,128)(2,1)S(1)}, bf16[32,5120]{1,0:T(8,128)(2,1)S(1)}, u32[]{:S(2)}, u32[]{:S(2)}) %collective-permute-start.8) | collective-permute-done | bytes 327712 | tf_op jit(solution)/shard_map/ppermute | solution.py:608
  60.1 5.2 %collective-permute-start.16 = (bf16[128,1024]{1,0:T(8,128)(2,1)S(1)}, bf16[128,1024]{1,0:T(8,128)(2,1)S(1)}, u32[]{:S(2)}, u32[]{:S(2)}) collective-permute-start(bf16[128,1024]{1,0:T(8,128)(2,1)S(1)} %constant_dynamic-slice_fusion), channel_id=1, source_target_pairs={{0,1},{1,0},{2,3},{3,2},{4,5},{5,4},{6,7},{7,6},{8,9},{9,8},{10,11... | collective-permute-start | bytes 786440 | tf_op jit(solution)/shard_map/ppermute | solution.py:608
  67.8 14.5 %qkv_forward.1 = (bf16[1024,1024]{1,0:T(8,128)(2,1)}, bf16[1024,3072]{1,0:T(8,128)(2,1)}, bf16[1024,3072]{1,0:T(8,128)(2,1)}) custom-call(s32[2]{0:T(128)} %pad_add_fusion.idx_ref, bf16[256,3072]{1,0:T(8,128)(2,1)} %own_ref.2, bf16[6,32,1536]{2,1,0:T(8,128)(2,1)} %copy-done.24, bf16[6,32,1536]{2,1,0:T(8,128)(2,1)} %copy-done.46, ...), custom_call_target="tpu_custom_call" | custom-call | flops 6442450944 | bytes 12582912 | tf_op jit(solution)/shard_map/qkv_forward/pallas_call | solution.py:151
  82.3 4.4 collective-permute-done.17
  90.4 1.6 collective-permute-start.21
  92.0 20.1 %attend.1 = (bf16[1024,1024]{1,0:T(8,128)(2,1)}, f32[8,2,1024]{2,1,0:T(2,128)}) custom-call(bf16[1024,3072]{1,0:T(8,128)(2,1)} %get-tuple-element.195.q_ref.k_ref.v_ref, bf16[1024,3072]{1,0:T(8,128)(2,1)} %get-tuple-element.195.q_ref.k_ref.v_ref, bf16[1024,3072]{1,0:T(8,128)(2,1)} %get-tuple-element.195.q_ref.k_ref.v_ref, s32[1,1024]{1,0:T(1,128)} %bitcast.243), custom_call_target="tpu_custom_call" | custom-call | flops 8589934592 | bytes 8388608 | tf_op jit(solution)/shard_map/attend/pallas_call | solution.py:506
  112.1 4.8 collective-permute-done.22
  126.7 32.4 %up_forward.1 = (f32[1024,1024]{1,0:T(8,128)}, f32[1024,1024]{1,0:T(8,128)}, bf16[1024,1024]{1,0:T(8,128)(2,1)}, bf16[1024,4096]{1,0:T(8,128)(2,1)}, bf16[1024,4...) custom-call(s32[2]{0:T(128)} %pad_add_fusion.idx_ref, bf16[256,1024]{1,0:T(8,128)(2,1)} %own_out.1, ...), custom_call_target="tpu_custom_call" | custom-call | flops 10737418240 | bytes 25165824 | tf_op jit(solution)/shard_map/up_forward/pallas_call | solution.py:237
  164.3 33.9 %down_both.1 = (bf16[1024,1024]{1,0:T(8,128)(2,1)}, bf16[1024,1024]{1,0:T(8,128)(2,1)}, f32[8,1024]{1,0:T(8,128)}, bf16[1024,4096]{1,0:T(8,128)(2,1)}, f32[1,4096]{1,0:T(1,128)}) custom-call(s32[2]{0:T(128)} %pad_add_fusion.idx_ref, bf16[1024,1024]{1,0:T(8,128)(2,1)} %own_ref.3, bf16[6,128,512]{2,1,0:T(8,128)(2,1)} %constant_dynamic-update-slice_fusion.8.refs_0_, ...), custom_call_target="tpu_custom_call" | custom-call | flops 17179869184 | bytes 33554432 | tf_op jit(solution)/shard_map/down_both/pallas_call | solution.py:322
  198.2 9.3 %grad_down_send.1 = bf16[4,1,4,2,128,512]{5,4,3,2,1,0:T(8,128)(2,1)} custom-call(s32[2]{0:T(128)} %pad_add_fusion.idx_ref, bf16[1024,4096]{1,0:T(8,128)(2,1)} %get-tuple-element.217.refs_8_.refs_0_.refs_1_.refs_2_.refs_3_, bf16[1024,4096]{1,0:T(8,128)(2,1)} %get-tuple-element.217.refs_8_.refs_0_.refs_1_.refs_2_.refs_3_, ...), custom_call_target="tpu_custom_call" | custom-call | flops 4294967296 | bytes 10737418 | tf_op jit(solution)/shard_map/grad_down_send/pallas_call | solution.py:705
  207.7 9.2 %grad_up_send.1 = bf16[4,1,4,2,128,512]{5,4,3,2,1,0:T(8,128)(2,1)} custom-call(s32[2]{0:T(128)} %pad_add_fusion.idx_ref, bf16[1024,1024]{1,0:T(8,128)(2,1)} %get-tuple-element.213.refs_0_, bf16[1024,4096]{1,0:T(8,128)(2,1)} %get-tuple-element.233.refs_1_.gh_ref), custom_call_target="tpu_custom_call" | custom-call | flops 4294967296 | bytes 10737418 | tf_op jit(solution)/shard_map/grad_up_send/pallas_call | solution.py:705
  217.2 10.9 %grad_down_keep.1 = (bf16[2,1,4,128,512]{4,3,2,1,0:T(8,128)(2,1)}, bf16[2,1,4,128,512]{4,3,2,1,0:T(8,128)(2,1)}, bf16[2,1,4,128,512]{4,3,2,1,0:T(8,128)(2,1)}, bf16[2,1,4,128,512]{4,3,2,1,0:T(8,128)(2,1)}) custom-call(s32[2]{0:T(128)} %pad_add_fusion.idx_ref, bf16[1024,4096]{1,0:T(8,128)(2,1)} %get-tuple-element.217.refs_8_.refs_0_.refs_1_.refs_2_.refs_3_, ...), custom_call_target="tpu_custom_call" | custom-call | flops 4294967296 | bytes 10737418 | tf_op jit(solution)/shard_map/grad_down_keep/pallas_call | solution.py:705
  230.1 23.7 %mid_backward.1 = (f32[1024,1024]{1,0:T(8,128)}, bf16[1024,1024]{1,0:T(8,128)(2,1)}, bf16[1024,1024]{1,0:T(8,128)(2,1)}, f32[8,1024]{1,0:T(8,128)}) custom-call(bf16[1024,4096]{1,0:T(8,128)(2,1)} %get-tuple-element.233.refs_1_.gh_ref, bf16[1024,4096]{1,0:T(8,128)(2,1)} %get-tuple-element.225.up_ref, bf16[1024,1024]{1,0:T(8,128)(2,1)} %get-tuple-element.226.out_w_ref, ...), custom_call_target="tpu_custom_call" | custom-call | flops 10737418240 | bytes 16777216 | tf_op jit(solution)/shard_map/mid_backward/pallas_call | solution.py:388
  256.2 10.8 %grad_up_keep.1 = (bf16[2,1,4,128,512]{4,3,2,1,0:T(8,128)(2,1)}, bf16[2,1,4,128,512]{4,3,2,1,0:T(8,128)(2,1)}, bf16[2,1,4,128,512]{4,3,2,1,0:T(8,128)(2,1)}, bf16[2,1,4,128,512]{4,3,2,1,0:T(8,128)(2,1)}) custom-call(s32[2]{0:T(128)} %pad_add_fusion.idx_ref, bf16[1024,1024]{1,0:T(8,128)(2,1)} %get-tuple-element.213.refs_0_, ...), custom_call_target="tpu_custom_call" | custom-call | flops 4294967296 | bytes 10737418 | tf_op jit(solution)/shard_map/grad_up_keep/pallas_call | solution.py:705
  269.9 17.8 %attend_back.2 = (bf16[1024,512]{1,0:T(8,128)(2,1)}, bf16[1024,512]{1,0:T(8,128)(2,1)}, bf16[1024,512]{1,0:T(8,128)(2,1)}, f32[1,512]{1,0:T(1,128)}, f32[1,512]{1,0:T(1,128)}) custom-call(bf16[1024,3072]{1,0:T(8,128)(2,1)} %get-tuple-element.195.q_ref.k_ref.v_ref, bf16[1024,3072]{1,0:T(8,128)(2,1)} %get-tuple-element.195.q_ref.k_ref.v_ref, ...), custom_call_target="tpu_custom_call" | custom-call | flops 10737418240 | bytes 8388608 | tf_op jit(solution)/shard_map/attend_back/pallas_call | solution.py:592
  288.9 8.9 %grad_heads_send.2 = bf16[4,1,4,2,64,640]{5,4,3,2,1,0:T(8,128)(2,1)} custom-call(s32[2]{0:T(128)} %pad_add_fusion.idx_ref, bf16[1024,1024]{1,0:T(8,128)(2,1)} %get-tuple-element.212.refs_0_.refs_1_.refs_2_.refs_3_, bf16[1024,1024]{1,0:T(8,128)(2,1)} %get-tuple-element.212.refs_0_.refs_1_.refs_2_.refs_3_, ...), custom_call_target="tpu_custom_call" | custom-call | flops 2684354560 | bytes 6710886 | tf_op jit(solution)/shard_map/grad_heads_send/pallas_call | solution.py:705
  297.9 2.4 fusion.7
  304.4 17.9 %attend_back.3 = (bf16[1024,512]{1,0:T(8,128)(2,1)}, bf16[1024,512]{1,0:T(8,128)(2,1)}, bf16[1024,512]{1,0:T(8,128)(2,1)}, f32[1,512]{1,0:T(1,128)}, f32[1,512]{1,0:T(1,128)}) custom-call(bf16[1024,3072]{1,0:T(8,128)(2,1)} %get-tuple-element.195.q_ref.k_ref.v_ref, bf16[1024,3072]{1,0:T(8,128)(2,1)} %get-tuple-element.195.q_ref.k_ref.v_ref, ...), custom_call_target="tpu_custom_call" | custom-call | flops 10737418240 | bytes 8388608 | tf_op jit(solution)/shard_map/attend_back/pallas_call | solution.py:592
  326.4 6.9 %grad_heads_send.3 = bf16[4,1,4,2,64,384]{5,4,3,2,1,0:T(8,128)(2,1)} custom-call(s32[2]{0:T(128)} %pad_add_fusion.idx_ref, bf16[1024,1024]{1,0:T(8,128)(2,1)} %get-tuple-element.212.refs_0_.refs_1_.refs_2_.refs_3_, bf16[1024,1024]{1,0:T(8,128)(2,1)} %get-tuple-element.212.refs_0_.refs_1_.refs_2_.refs_3_, ...), custom_call_target="tpu_custom_call" | custom-call | flops 1610612736 | bytes 4026531 | tf_op jit(solution)/shard_map/grad_heads_send/pallas_call | solution.py:705
  334.5 6.3 %collective-permute-start.45 = (bf16[2,2,2,128,512]{4,3,2,0,1:T(8,128)(2,1)}, bf16[2,2,2,128,512]{4,3,2,0,1:T(8,128)(2,1)}, u32[]{:S(2)}, u32[]{:S(2)}) collective-permute-start(bf16[2,2,2,128,512]{4,3,2,0,1:T(8,128)(2,1)} %get-tuple-element.348), channel_id=1, source_target_pairs={{0,1},{1,0},{2,3},{3,2},{4,5},{5,4},{6,7},{7,6},{8,9},{9,8},{10,11... | collective-permute-start | bytes 3145736 | tf_op jit(solution)/shard_map/ppermute | solution.py:608
  341.9 9.8 %grad_heads_keep.2 = (bf16[2,1,4,64,640]{4,3,2,1,0:T(8,128)(2,1)}, bf16[2,1,4,64,640]{4,3,2,1,0:T(8,128)(2,1)}, bf16[2,1,4,64,640]{4,3,2,1,0:T(8,128)(2,1)}, bf16[2,1,4,64,640]{4,3,2,1,0:T(8,128)(2,1)}) custom-call(s32[2]{0:T(128)} %pad_add_fusion.idx_ref, bf16[1024,1024]{1,0:T(8,128)(2,1)} %get-tuple-element.212.refs_0_.refs_1_.refs_2_.refs_3_, ...), custom_call_target="tpu_custom_call" | custom-call | flops 2684354560 | bytes 6710886 | tf_op jit(solution)/shard_map/grad_heads_keep/pallas_call | solution.py:705
  352.9 12.1 %collective-permute-done.45 = bf16[2,2,2,128,512]{4,3,2,0,1:T(8,128)(2,1)} collective-permute-done((bf16[2,2,2,128,512]{4,3,2,0,1:T(8,128)(2,1)}, bf16[2,2,2,128,512]{4,3,2,0,1:T(8,128)(2,1)}, u32[]{:S(2)}, u32[]{:S(2)}) %collective-permute-start.45) | collective-permute-done | bytes 1048608 | tf_op jit(solution)/shard_map/ppermute | solution.py:608
  365.0 2.8 fusion.9
  367.8 7.6 %grad_heads_keep.3 = (bf16[2,1,4,64,384]{4,3,2,1,0:T(8,128)(2,1)}, bf16[2,1,4,64,384]{4,3,2,1,0:T(8,128)(2,1)}, bf16[2,1,4,64,384]{4,3,2,1,0:T(8,128)(2,1)}, bf16[2,1,4,64,384]{4,3,2,1,0:T(8,128)(2,1)}) custom-call(s32[2]{0:T(128)} %pad_add_fusion.idx_ref, bf16[1024,1024]{1,0:T(8,128)(2,1)} %get-tuple-element.212.refs_0_.refs_1_.refs_2_.refs_3_, ...), custom_call_target="tpu_custom_call" | custom-call | flops 1610612736 | bytes 4026531 | tf_op jit(solution)/shard_map/grad_heads_keep/pallas_call | solution.py:705
  376.6 2.6 collective-permute-start.52
  379.2 2.0 fusion.14
  385.0 9.9 %input_backward.2 = (f32[1024,1024]{1,0:T(8,128)}, f32[8,1024]{1,0:T(8,128)}) custom-call(bf16[1024,512]{1,0:T(8,128)(2,1)} %get-tuple-element.266.refs_4_.refs_0_, bf16[1024,512]{1,0:T(8,128)(2,1)} %get-tuple-element.286.refs_4_.refs_1_, bf16[1024,512]{1,0:T(8,128)(2,1)} %get-tuple-element.246.refs_5_.refs_2_, ...), custom_call_target="tpu_custom_call" | custom-call | flops 3221225472 | bytes 6291456 | tf_op jit(solution)/shard_map/input_backward/pallas_call | solution.py:445
  394.9 7.3 %collective-permute-done.52 = bf16[2,2,128,512]{3,2,1,0:T(8,128)(2,1)S(1)} collective-permute-done((bf16[2,2,128,512]{3,2,1,0:T(8,128)(2,1)}, bf16[2,2,128,512]{3,2,1,0:T(8,128)(2,1)S(1)}, u32[]{:S(2)}, u32[]{:S(2)}) %collective-permute-start.52) | collective-permute-done | bytes 524320 | tf_op jit(solution)/shard_map/ppermute | solution.py:608
  403.6 1.6 collective-permute-start.54
  406.6 9.6 %input_backward.3 = (f32[1024,1024]{1,0:T(8,128)}, f32[8,1024]{1,0:T(8,128)}) custom-call(bf16[1024,512]{1,0:T(8,128)(2,1)} %get-tuple-element.266.refs_4_.refs_0_, bf16[1024,512]{1,0:T(8,128)(2,1)} %get-tuple-element.286.refs_4_.refs_1_, bf16[1024,512]{1,0:T(8,128)(2,1)} %get-tuple-element.246.refs_5_.refs_2_, ...), custom_call_target="tpu_custom_call", output_to_operand_aliasing={{0}: (10, {})} | custom-call | flops 3221225472 | bytes 6291456 | tf_op jit(solution)/shard_map/input_backward/pallas_call | solution.py:445
  418.1 2.3 collective-permute-start.57
  421.0 2.2 collective-permute-done.60
  423.7 5.6 %collective-permute-done.57 = bf16[1,2,64,640]{3,2,1,0:T(8,128)(2,1)S(1)} collective-permute-done((bf16[1,2,64,640]{3,2,1,0:T(8,128)(2,1)S(1)}, bf16[1,2,64,640]{3,2,1,0:T(8,128)(2,1)S(1)}, u32[]{:S(2)}, u32[]{:S(2)}) %collective-permute-start.57) | collective-permute-done | bytes 163872 | tf_op jit(solution)/shard_map/ppermute | solution.py:608
  431.6 1.6 collective-permute-start.62
  435.7 1.9 collective-permute-done.62
  437.6 2.2 collective-permute-done.61
  442.0 14.4 %collective-permute-done.64 = bf16[2,64,384]{2,1,0:T(8,128)(2,1)S(1)} collective-permute-done((bf16[2,64,384]{2,1,0:T(8,128)(2,1)S(1)}, bf16[2,64,384]{2,1,0:T(8,128)(2,1)S(1)}, u32[]{:S(2)}, u32[]{:S(2)}) %collective-permute-start.64) | collective-permute-done | bytes 98336 | tf_op jit(solution)/shard_map/ppermute | solution.py:608
  457.0 3.7 collective-permute-done.66
  461.9 1.8 collective-permute-start.72
  465.1 6.1 %finish_ffn.1 = (f32[256,4096]{1,0:T(8,128)}, f32[1024,1024]{1,0:T(8,128)}) custom-call(s32[2]{0:T(128)} %pad_add_fusion.idx_ref, bf16[2,2,128,512]{3,2,1,0:T(8,128)(2,1)} %copy-done.1, bf16[2,2,128,512]{3,2,1,0:T(8,128)(2,1)} %copy-done.11, bf16[2,2,128,512]{3,2,1,0:T(8,128)(2,1)} %copy-done.13, bf16[2,2,128,512]{3,2,1,0:T(8,128)(2,1)} %copy-done.15, ...), custom_call_target="tpu_custom_call" | custom-call | bytes 12582912 | tf_op jit(solution)/shard_map/finish_ffn/pallas_call | solution.py:871
  472.9 5.0 %collective-permute-done.79 = f32[128,128]{1,0:T(8,128)S(1)} collective-permute-done((f32[128,128]{1,0:T(8,128)S(1)}, f32[128,128]{1,0:T(8,128)S(1)}, u32[]{:S(2)}, u32[]{:S(2)}) %collective-permute-start.79) | collective-permute-done | bytes 65568 | tf_op jit(solution)/shard_map/ppermute | solution.py:608
  482.6 4.0 finish_heads.1
  (377 shorter events, 96.1 us)
Async XLA Ops:
  6.5 22.5 %collective-permute-start.2 = (bf16[32,3200]{1,0:T(8,128)(2,1)S(1)}, bf16[32,3200]{1,0:T(8,128)(2,1)S(1)}, u32[]{:S(2)}, u32[]{:S(2)}) collective-permute-start(bf16[32,3200]{1,0:T(8,128)(2,1)S(1)} %pad_maximum_fusion.10), channel_id=1, source_target_pairs={{0,3},{1,2},{2,1},{3,0},{4,7},{5,6},{6,5},{7,4},{8,11},{9,10},{10,... | collective-permute-start | bytes 614408 | tf_op jit(solution)/shard_map/ppermute | solution.py:608
  11.6 17.4 %collective-permute-start.1 = (bf16[32,3200]{1,0:T(8,128)(2,1)S(1)}, bf16[32,3200]{1,0:T(8,128)(2,1)S(1)}, u32[]{:S(2)}, u32[]{:S(2)}) collective-permute-start(bf16[32,3200]{1,0:T(8,128)(2,1)S(1)} %pad_maximum_fusion.10), channel_id=1, source_target_pairs={{0,2},{1,3},{2,0},{3,1},{4,6},{5,7},{6,4},{7,5},{8,10},{9,11},{10,... | collective-permute-start | bytes 614408 | tf_op jit(solution)/shard_map/ppermute | solution.py:608
  11.6 13.2 %collective-permute-start = (bf16[32,3200]{1,0:T(8,128)(2,1)S(1)}, bf16[32,3200]{1,0:T(8,128)(2,1)S(1)}, u32[]{:S(2)}, u32[]{:S(2)}) collective-permute-start(bf16[32,3200]{1,0:T(8,128)(2,1)S(1)} %pad_maximum_fusion.10), channel_id=1, source_target_pairs={{0,1},{1,0},{2,3},{3,2},{4,5},{5,4},{6,7},{7,6},{8,9},{9,8},{10,11... | collective-permute-start | bytes 614408 | tf_op jit(solution)/shard_map/ppermute | solution.py:608
  29.1 17.7 %collective-permute-start.7 = (bf16[32,5120]{1,0:T(8,128)(2,1)S(1)}, bf16[32,5120]{1,0:T(8,128)(2,1)S(1)}, u32[]{:S(2)}, u32[]{:S(2)}) collective-permute-start(bf16[32,5120]{1,0:T(8,128)(2,1)S(1)} %pad_maximum_fusion.6), channel_id=1, source_target_pairs={{0,1},{1,0},{2,3},{3,2},{4,5},{5,4},{6,7},{7,6},{8,9},{9,8},{10,11... | collective-permute-start | bytes 983048 | tf_op jit(solution)/shard_map/ppermute | solution.py:608
  29.2 25.7 %collective-permute-start.8 = (bf16[32,5120]{1,0:T(8,128)(2,1)S(1)}, bf16[32,5120]{1,0:T(8,128)(2,1)S(1)}, u32[]{:S(2)}, u32[]{:S(2)}) collective-permute-start(bf16[32,5120]{1,0:T(8,128)(2,1)S(1)} %pad_maximum_fusion.6), channel_id=1, source_target_pairs={{0,2},{1,3},{2,0},{3,1},{4,6},{5,7},{6,4},{7,5},{8,10},{9,11},{10,... | collective-permute-start | bytes 983048 | tf_op jit(solution)/shard_map/ppermute | solution.py:608
  32.2 22.7 %collective-permute-start.9 = (bf16[32,5120]{1,0:T(8,128)(2,1)S(1)}, bf16[32,5120]{1,0:T(8,128)(2,1)S(1)}, u32[]{:S(2)}, u32[]{:S(2)}) collective-permute-start(bf16[32,5120]{1,0:T(8,128)(2,1)S(1)} %pad_maximum_fusion.6), channel_id=1, source_target_pairs={{0,3},{1,2},{2,1},{3,0},{4,7},{5,6},{6,5},{7,4},{8,11},{9,10},{10,... | collective-permute-start | bytes 983048 | tf_op jit(solution)/shard_map/ppermute | solution.py:608
  42.4 13.8 %collective-permute-start.6 = (bf16[6,32,1536]{2,1,0:T(8,128)(2,1)S(1)}, bf16[6,32,1536]{2,1,0:T(8,128)(2,1)S(1)}, u32[]{:S(2)}, u32[]{:S(2)}) collective-permute-start(bf16[6,32,1536]{2,1,0:T(8,128)(2,1)S(1)} %constant_dynamic-update-slice_fusion.2.refs_4_), channel_id=1, source_target_pairs={{0,16},{4,20},{8,24},{12,28},{16,0},{20,4},{24,8},{28,12},{1,17},{... | collective-permute-start | bytes 1769480 | tf_op jit(solution)/shard_map/ppermute | solution.py:608
  56.7 30.0 %collective-permute-start.14 = (bf16[3,32,2560]{2,1,0:T(8,128)(2,1)S(1)}, bf16[3,32,2560]{2,1,0:T(8,128)(2,1)S(1)}, u32[]{:S(2)}, u32[]{:S(2)}) collective-permute-start(bf16[3,32,2560]{2,1,0:T(8,128)(2,1)S(1)} %pad_maximum_fusion.2), channel_id=1, source_target_pairs={{0,16},{4,20},{8,24},{12,28},{16,0},{20,4},{24,8},{28,12},{1,17},{... | collective-permute-start | bytes 1474568 | tf_op jit(solution)/shard_map/ppermute | solution.py:608
  59.4 27.3 %collective-permute-start.15 = (bf16[3,32,2560]{2,1,0:T(8,128)(2,1)S(1)}, bf16[3,32,2560]{2,1,0:T(8,128)(2,1)S(1)}, u32[]{:S(2)}, u32[]{:S(2)}) collective-permute-start(bf16[3,32,2560]{2,1,0:T(8,128)(2,1)S(1)} %pad_maximum_fusion.3), channel_id=1, source_target_pairs={{0,8},{4,12},{8,0},{12,4},{16,24},{20,28},{24,16},{28,20},{1,9},{5... | collective-permute-start | bytes 1474568 | tf_op jit(solution)/shard_map/ppermute | solution.py:608
  60.1 22.1 %collective-permute-start.16 = (bf16[128,1024]{1,0:T(8,128)(2,1)S(1)}, bf16[128,1024]{1,0:T(8,128)(2,1)S(1)}, u32[]{:S(2)}, u32[]{:S(2)}) collective-permute-start(bf16[128,1024]{1,0:T(8,128)(2,1)S(1)} %constant_dynamic-slice_fusion), channel_id=1, source_target_pairs={{0,1},{1,0},{2,3},{3,2},{4,5},{5,4},{6,7},{7,6},{8,9},{9,8},{10,11... | collective-permute-start | bytes 786440 | tf_op jit(solution)/shard_map/ppermute | solution.py:608
  65.3 21.4 %collective-permute-start.17 = (bf16[128,1024]{1,0:T(8,128)(2,1)S(1)}, bf16[128,1024]{1,0:T(8,128)(2,1)S(1)}, u32[]{:S(2)}, u32[]{:S(2)}) collective-permute-start(bf16[128,1024]{1,0:T(8,128)(2,1)S(1)} %constant_dynamic-slice_fusion), channel_id=1, source_target_pairs={{0,2},{1,3},{2,0},{3,1},{4,6},{5,7},{6,4},{7,5},{8,10},{9,11},{10,... | collective-permute-start | bytes 786440 | tf_op jit(solution)/shard_map/ppermute | solution.py:608
  66.2 20.5 %collective-permute-start.18 = (bf16[128,1024]{1,0:T(8,128)(2,1)S(1)}, bf16[128,1024]{1,0:T(8,128)(2,1)S(1)}, u32[]{:S(2)}, u32[]{:S(2)}) collective-permute-start(bf16[128,1024]{1,0:T(8,128)(2,1)S(1)} %constant_dynamic-slice_fusion), channel_id=1, source_target_pairs={{0,3},{1,2},{2,1},{3,0},{4,7},{5,6},{6,5},{7,4},{8,11},{9,10},{10,... | collective-permute-start | bytes 786440 | tf_op jit(solution)/shard_map/ppermute | solution.py:608
  87.6 29.4 %collective-permute-start.20 = (bf16[6,32,2560]{2,1,0:T(8,128)(2,1)}, bf16[6,32,2560]{2,1,0:T(8,128)(2,1)}, u32[]{:S(2)}, u32[]{:S(2)}) collective-permute-start(bf16[6,32,2560]{2,1,0:T(8,128)(2,1)} %constant_dynamic-update-slice_fusion.6.refs_4_), channel_id=1, source_target_pairs={{0,16},{4,20},{8,24},{12,28},{16,0},{20,4},{24,8},{28,12},{1,17},{... | collective-permute-start | bytes 2949128 | tf_op jit(solution)/shard_map/ppermute | solution.py:608
  88.2 28.8 %collective-permute-start.19 = (bf16[6,32,2560]{2,1,0:T(8,128)(2,1)S(1)}, bf16[6,32,2560]{2,1,0:T(8,128)(2,1)}, u32[]{:S(2)}, u32[]{:S(2)}) collective-permute-start(bf16[6,32,2560]{2,1,0:T(8,128)(2,1)S(1)} %constant_dynamic-update-slice_fusion.4.refs_0_), channel_id=1, source_target_pairs={{0,8},{4,12},{8,0},{12,4},{16,24},{20,28},{24,16},{28,20},{1,9},{5... | collective-permute-start | bytes 2949128 | tf_op jit(solution)/shard_map/ppermute | solution.py:608
  88.8 28.1 %collective-permute-start.22 = (bf16[3,128,512]{2,1,0:T(8,128)(2,1)S(1)}, bf16[3,128,512]{2,1,0:T(8,128)(2,1)S(1)}, u32[]{:S(2)}, u32[]{:S(2)}) collective-permute-start(bf16[3,128,512]{2,1,0:T(8,128)(2,1)S(1)} %pad_maximum_fusion.5), channel_id=1, source_target_pairs={{0,8},{4,12},{8,0},{12,4},{16,24},{20,28},{24,16},{28,20},{1,9},{5... | collective-permute-start | bytes 1179656 | tf_op jit(solution)/shard_map/ppermute | solution.py:608
  90.4 26.5 %collective-permute-start.21 = (bf16[3,128,512]{2,1,0:T(8,128)(2,1)S(1)}, bf16[3,128,512]{2,1,0:T(8,128)(2,1)S(1)}, u32[]{:S(2)}, u32[]{:S(2)}) collective-permute-start(bf16[3,128,512]{2,1,0:T(8,128)(2,1)S(1)} %pad_maximum_fusion.4), channel_id=1, source_target_pairs={{0,16},{4,20},{8,24},{12,28},{16,0},{20,4},{24,8},{28,12},{1,17},{... | collective-permute-start | bytes 1179656 | tf_op jit(solution)/shard_map/ppermute | solution.py:608
  92.0 32.7 %collective-permute-start.23 = (bf16[6,32,2560]{2,1,0:T(8,128)(2,1)S(1)}, bf16[6,32,2560]{2,1,0:T(8,128)(2,1)}, u32[]{:S(2)}, u32[]{:S(2)}) collective-permute-start(bf16[6,32,2560]{2,1,0:T(8,128)(2,1)S(1)} %constant_dynamic-update-slice_fusion.4.refs_0_), channel_id=1, source_target_pairs={{0,4},{4,0},{8,12},{12,8},{16,20},{20,16},{24,28},{28,24},{1,5},{5... | collective-permute-start | bytes 2949128 | tf_op jit(solution)/shard_map/ppermute | solution.py:608
  122.4 36.7 %collective-permute-start.28 = (bf16[6,128,512]{2,1,0:T(8,128)(2,1)}, bf16[6,128,512]{2,1,0:T(8,128)(2,1)S(1)}, u32[]{:S(2)}, u32[]{:S(2)}) collective-permute-start(bf16[6,128,512]{2,1,0:T(8,128)(2,1)} %constant_dynamic-update-slice_fusion.10.refs_4_), channel_id=1, source_target_pairs={{0,16},{4,20},{8,24},{12,28},{16,0},{20,4},{24,8},{28,12},{1,17},{... | collective-permute-start | bytes 2359304 | tf_op jit(solution)/shard_map/ppermute | solution.py:608
  124.7 37.7 %collective-permute-start.31 = (bf16[6,128,512]{2,1,0:T(8,128)(2,1)}, bf16[6,128,512]{2,1,0:T(8,128)(2,1)S(1)}, u32[]{:S(2)}, u32[]{:S(2)}) collective-permute-start(bf16[6,128,512]{2,1,0:T(8,128)(2,1)} %constant_dynamic-update-slice_fusion.10.refs_4_), channel_id=1, source_target_pairs={{0,4},{4,0},{8,12},{12,8},{16,20},{20,16},{24,28},{28,24},{1,5},{5... | collective-permute-start | bytes 2359304 | tf_op jit(solution)/shard_map/ppermute | solution.py:608
  124.9 34.3 %collective-permute-start.27 = (bf16[6,128,512]{2,1,0:T(8,128)(2,1)}, bf16[6,128,512]{2,1,0:T(8,128)(2,1)S(1)}, u32[]{:S(2)}, u32[]{:S(2)}) collective-permute-start(bf16[6,128,512]{2,1,0:T(8,128)(2,1)} %constant_dynamic-update-slice_fusion.8.refs_0_), channel_id=1, source_target_pairs={{0,8},{4,12},{8,0},{12,4},{16,24},{20,28},{24,16},{28,20},{1,9},{5... | collective-permute-start | bytes 2359304 | tf_op jit(solution)/shard_map/ppermute | solution.py:608
  125.4 37.0 %collective-permute-start.29 = (bf16[6,128,512]{2,1,0:T(8,128)(2,1)}, bf16[6,128,512]{2,1,0:T(8,128)(2,1)S(1)}, u32[]{:S(2)}, u32[]{:S(2)}) collective-permute-start(bf16[6,128,512]{2,1,0:T(8,128)(2,1)} %constant_dynamic-update-slice_fusion.8.refs_0_), channel_id=1, source_target_pairs={{0,4},{4,0},{8,12},{12,8},{16,20},{20,16},{24,28},{28,24},{1,5},{5... | collective-permute-start | bytes 2359304 | tf_op jit(solution)/shard_map/ppermute | solution.py:608
  216.9 36.9 %collective-permute-start.36 = (bf16[4,1,4,2,128,512]{5,4,3,2,1,0:T(8,128)(2,1)}, bf16[4,1,4,2,128,512]{5,4,3,2,1,0:T(8,128)(2,1)}, u32[]{:S(2)}, u32[]{:S(2)}) collective-permute-start(bf16[4,1,4,2,128,512]{5,4,3,2,1,0:T(8,128)(2,1)} %grad_up_send.1), channel_id=1, source_target_pairs={{0,4},{4,0},{8,12},{12,8},{16,20},{20,16},{24,28},{28,24},{1,5},{5... | collective-permute-start | bytes 12582920 | tf_op jit(solution)/shard_map/ppermute | solution.py:608
  228.1 25.7 %collective-permute-start.34 = (bf16[2,1,4,128,512]{4,3,2,1,0:T(8,128)(2,1)}, bf16[2,1,4,128,512]{4,3,2,1,0:T(8,128)(2,1)S(1)}, u32[]{:S(2)}, u32[]{:S(2)}) collective-permute-start(bf16[2,1,4,128,512]{4,3,2,1,0:T(8,128)(2,1)} %get-tuple-element.219), channel_id=1, source_target_pairs={{0,16},{4,20},{8,24},{12,28},{16,0},{20,4},{24,8},{28,12},{1,17},{... | collective-permute-start | bytes 3145736 | tf_op jit(solution)/shard_map/ppermute | solution.py:608
  228.6 25.2 %collective-permute-start.35 = (bf16[2,1,4,128,512]{4,3,2,1,0:T(8,128)(2,1)}, bf16[2,1,4,128,512]{4,3,2,1,0:T(8,128)(2,1)S(1)}, u32[]{:S(2)}, u32[]{:S(2)}) collective-permute-start(bf16[2,1,4,128,512]{4,3,2,1,0:T(8,128)(2,1)} %get-tuple-element.221), channel_id=1, source_target_pairs={{0,8},{4,12},{8,0},{12,4},{16,24},{20,28},{24,16},{28,20},{1,9},{5... | collective-permute-start | bytes 3145736 | tf_op jit(solution)/shard_map/ppermute | solution.py:608
  267.0 30.9 %collective-permute-start.37 = (bf16[2,1,4,128,512]{4,3,2,1,0:T(8,128)(2,1)}, bf16[2,1,4,128,512]{4,3,2,1,0:T(8,128)(2,1)S(1)}, u32[]{:S(2)}, u32[]{:S(2)}) collective-permute-start(bf16[2,1,4,128,512]{4,3,2,1,0:T(8,128)(2,1)} %get-tuple-element.235), channel_id=1, source_target_pairs={{0,16},{4,20},{8,24},{12,28},{16,0},{20,4},{24,8},{28,12},{1,17},{... | collective-permute-start | bytes 3145736 | tf_op jit(solution)/shard_map/ppermute | solution.py:608
  268.5 29.4 %collective-permute-start.38 = (bf16[2,1,4,128,512]{4,3,2,1,0:T(8,128)(2,1)}, bf16[2,1,4,128,512]{4,3,2,1,0:T(8,128)(2,1)}, u32[]{:S(2)}, u32[]{:S(2)}) collective-permute-start(bf16[2,1,4,128,512]{4,3,2,1,0:T(8,128)(2,1)} %get-tuple-element.237), channel_id=1, source_target_pairs={{0,8},{4,12},{8,0},{12,4},{16,24},{20,28},{24,16},{28,20},{1,9},{5... | collective-permute-start | bytes 3145736 | tf_op jit(solution)/shard_map/ppermute | solution.py:608
  287.8 34.5 %collective-permute-start.40 = (bf16[1,4,128,512]{3,2,1,0:T(8,128)(2,1)}, bf16[1,4,128,512]{3,2,1,0:T(8,128)(2,1)}, u32[]{:S(2)}, u32[]{:S(2)}) collective-permute-start(bf16[1,4,128,512]{3,2,1,0:T(8,128)(2,1)} %get-tuple-element.354), channel_id=1, source_target_pairs={{0,16},{4,20},{8,24},{12,28},{16,0},{20,4},{24,8},{28,12},{1,17},{... | collective-permute-start | bytes 1572872 | tf_op jit(solution)/shard_map/ppermute | solution.py:608
  288.3 34.0 %collective-permute-start.39 = (bf16[1,4,128,512]{3,2,1,0:T(8,128)(2,1)}, bf16[1,4,128,512]{3,2,1,0:T(8,128)(2,1)}, u32[]{:S(2)}, u32[]{:S(2)}) collective-permute-start(bf16[1,4,128,512]{3,2,1,0:T(8,128)(2,1)} %get-tuple-element.356), channel_id=1, source_target_pairs={{0,8},{4,12},{8,0},{12,4},{16,24},{20,28},{24,16},{28,20},{1,9},{5... | collective-permute-start | bytes 1572872 | tf_op jit(solution)/shard_map/ppermute | solution.py:608
  297.8 44.1 %collective-permute-start.43 = (bf16[4,1,4,2,64,640]{5,4,3,2,1,0:T(8,128)(2,1)}, bf16[4,1,4,2,64,640]{5,4,3,2,1,0:T(8,128)(2,1)}, u32[]{:S(2)}, u32[]{:S(2)}) collective-permute-start(bf16[4,1,4,2,64,640]{5,4,3,2,1,0:T(8,128)(2,1)} %grad_heads_send.2), channel_id=1, source_target_pairs={{0,4},{4,0},{8,12},{12,8},{16,20},{20,16},{24,28},{28,24},{1,5},{5... | collective-permute-start | bytes 7864328 | tf_op jit(solution)/shard_map/ppermute | solution.py:608
  301.4 20.9 %collective-permute-start.42 = (bf16[1,4,128,512]{3,2,1,0:T(8,128)(2,1)}, bf16[1,4,128,512]{3,2,1,0:T(8,128)(2,1)S(1)}, u32[]{:S(2)}, u32[]{:S(2)}) collective-permute-start(bf16[1,4,128,512]{3,2,1,0:T(8,128)(2,1)} %get-tuple-element.350), channel_id=1, source_target_pairs={{0,16},{4,20},{8,24},{12,28},{16,0},{20,4},{24,8},{28,12},{1,17},{... | collective-permute-start | bytes 1572872 | tf_op jit(solution)/shard_map/ppermute | solution.py:608
  302.9 19.4 %collective-permute-start.41 = (bf16[1,4,128,512]{3,2,1,0:T(8,128)(2,1)}, bf16[1,4,128,512]{3,2,1,0:T(8,128)(2,1)S(1)}, u32[]{:S(2)}, u32[]{:S(2)}) collective-permute-start(bf16[1,4,128,512]{3,2,1,0:T(8,128)(2,1)} %get-tuple-element.352), channel_id=1, source_target_pairs={{0,8},{4,12},{8,0},{12,4},{16,24},{20,28},{24,16},{28,20},{1,9},{5... | collective-permute-start | bytes 1572872 | tf_op jit(solution)/shard_map/ppermute | solution.py:608
  333.3 31.7 %collective-permute-start.44 = (bf16[4,1,4,2,64,384]{5,4,3,2,1,0:T(8,128)(2,1)}, bf16[4,1,4,2,64,384]{5,4,3,2,1,0:T(8,128)(2,1)S(1)}, u32[]{:S(2)}, u32[]{:S(2)}) collective-permute-start(bf16[4,1,4,2,64,384]{5,4,3,2,1,0:T(8,128)(2,1)} %grad_heads_send.3), channel_id=1, source_target_pairs={{0,4},{4,0},{8,12},{12,8},{16,20},{20,16},{24,28},{28,24},{1,5},{5... | collective-permute-start | bytes 4718600 | tf_op jit(solution)/shard_map/ppermute | solution.py:608
  334.5 30.5 %collective-permute-start.45 = (bf16[2,2,2,128,512]{4,3,2,0,1:T(8,128)(2,1)}, bf16[2,2,2,128,512]{4,3,2,0,1:T(8,128)(2,1)}, u32[]{:S(2)}, u32[]{:S(2)}) collective-permute-start(bf16[2,2,2,128,512]{4,3,2,0,1:T(8,128)(2,1)} %get-tuple-element.348), channel_id=1, source_target_pairs={{0,1},{1,0},{2,3},{3,2},{4,5},{5,4},{6,7},{7,6},{8,9},{9,8},{10,11... | collective-permute-start | bytes 3145736 | tf_op jit(solution)/shard_map/ppermute | solution.py:608
  351.7 27.5 %collective-permute-start.46 = (bf16[2,1,4,64,640]{4,3,2,1,0:T(8,128)(2,1)}, bf16[2,1,4,64,640]{4,3,2,1,0:T(8,128)(2,1)S(1)}, u32[]{:S(2)}, u32[]{:S(2)}) collective-permute-start(bf16[2,1,4,64,640]{4,3,2,1,0:T(8,128)(2,1)} %get-tuple-element.268), channel_id=1, source_target_pairs={{0,16},{4,20},{8,24},{12,28},{16,0},{20,4},{24,8},{28,12},{1,17},{... | collective-permute-start | bytes 1966088 | tf_op jit(solution)/shard_map/ppermute | solution.py:608
  352.3 26.9 %collective-permute-start.47 = (bf16[2,1,4,64,640]{4,3,2,1,0:T(8,128)(2,1)}, bf16[2,1,4,64,640]{4,3,2,1,0:T(8,128)(2,1)}, u32[]{:S(2)}, u32[]{:S(2)}) collective-permute-start(bf16[2,1,4,64,640]{4,3,2,1,0:T(8,128)(2,1)} %get-tuple-element.270), channel_id=1, source_target_pairs={{0,8},{4,12},{8,0},{12,4},{16,24},{20,28},{24,16},{28,20},{1,9},{5... | collective-permute-start | bytes 1966088 | tf_op jit(solution)/shard_map/ppermute | solution.py:608
  375.4 19.4 %collective-permute-start.50 = (bf16[2,1,4,64,384]{4,3,2,1,0:T(8,128)(2,1)}, bf16[2,1,4,64,384]{4,3,2,1,0:T(8,128)(2,1)S(1)}, u32[]{:S(2)}, u32[]{:S(2)}) collective-permute-start(bf16[2,1,4,64,384]{4,3,2,1,0:T(8,128)(2,1)} %get-tuple-element.278), channel_id=1, source_target_pairs={{0,16},{4,20},{8,24},{12,28},{16,0},{20,4},{24,8},{28,12},{1,17},{... | collective-permute-start | bytes 1179656 | tf_op jit(solution)/shard_map/ppermute | solution.py:608
  376.0 18.8 %collective-permute-start.51 = (bf16[2,1,4,64,384]{4,3,2,1,0:T(8,128)(2,1)}, bf16[2,1,4,64,384]{4,3,2,1,0:T(8,128)(2,1)S(1)}, u32[]{:S(2)}, u32[]{:S(2)}) collective-permute-start(bf16[2,1,4,64,384]{4,3,2,1,0:T(8,128)(2,1)} %get-tuple-element.280), channel_id=1, source_target_pairs={{0,8},{4,12},{8,0},{12,4},{16,24},{20,28},{24,16},{28,20},{1,9},{5... | collective-permute-start | bytes 1179656 | tf_op jit(solution)/shard_map/ppermute | solution.py:608
  376.6 25.5 %collective-permute-start.52 = (bf16[2,2,128,512]{3,2,1,0:T(8,128)(2,1)}, bf16[2,2,128,512]{3,2,1,0:T(8,128)(2,1)S(1)}, u32[]{:S(2)}, u32[]{:S(2)}) collective-permute-start(bf16[2,2,128,512]{3,2,1,0:T(8,128)(2,1)} %get-tuple-element.346), channel_id=1, source_target_pairs={{0,2},{1,3},{2,0},{3,1},{4,6},{5,7},{6,4},{7,5},{8,10},{9,11},{10,... | collective-permute-start | bytes 1572872 | tf_op jit(solution)/shard_map/ppermute | solution.py:608
  381.2 13.7 %collective-permute-start.49 = (bf16[1,4,64,640]{3,2,1,0:T(8,128)(2,1)}, bf16[1,4,64,640]{3,2,1,0:T(8,128)(2,1)S(1)}, u32[]{:S(2)}, u32[]{:S(2)}) collective-permute-start(bf16[1,4,64,640]{3,2,1,0:T(8,128)(2,1)} %get-tuple-element.358), channel_id=1, source_target_pairs={{0,16},{4,20},{8,24},{12,28},{16,0},{20,4},{24,8},{28,12},{1,17},{... | collective-permute-start | bytes 983048 | tf_op jit(solution)/shard_map/ppermute | solution.py:608
  402.5 13.7 %collective-permute-start.55 = (bf16[1,2,2,64,640]{4,3,2,1,0:T(8,128)(2,1)S(1)}, bf16[1,2,2,64,640]{4,3,2,1,0:T(8,128)(2,1)S(1)}, u32[]{:S(2)}, u32[]{:S(2)}) collective-permute-start(bf16[1,2,2,64,640]{4,3,2,1,0:T(8,128)(2,1)S(1)} %get-tuple-element.366), channel_id=1, source_target_pairs={{0,1},{1,0},{2,3},{3,2},{4,5},{5,4},{6,7},{7,6},{8,9},{9,8},{10,11... | collective-permute-start | bytes 983048 | tf_op jit(solution)/shard_map/ppermute | solution.py:608
  403.6 12.6 %collective-permute-start.54 = (bf16[1,4,64,384]{3,2,1,0:T(8,128)(2,1)S(1)}, bf16[1,4,64,384]{3,2,1,0:T(8,128)(2,1)S(1)}, u32[]{:S(2)}, u32[]{:S(2)}) collective-permute-start(bf16[1,4,64,384]{3,2,1,0:T(8,128)(2,1)S(1)} %get-tuple-element.362), channel_id=1, source_target_pairs={{0,16},{4,20},{8,24},{12,28},{16,0},{20,4},{24,8},{28,12},{1,17},{... | collective-permute-start | bytes 589832 | tf_op jit(solution)/shard_map/ppermute | solution.py:608
  434.6 26.1 %collective-permute-start.67 = (bf16[2,2,128,512]{3,2,1,0:T(8,128)(2,1)S(1)}, bf16[2,2,128,512]{3,2,1,0:T(8,128)(2,1)S(1)}, u32[]{:S(2)}, u32[]{:S(2)}) collective-permute-start(bf16[2,2,128,512]{3,2,1,0:T(8,128)(2,1)S(1)} %pad_maximum_fusion.refs_0_), channel_id=1, source_target_pairs={{0,8},{4,12},{8,0},{12,4},{16,24},{20,28},{24,16},{28,20},{1,9},{5... | collective-permute-start | bytes 1572872 | tf_op jit(solution)/shard_map/ppermute | solution.py:608
  435.2 25.5 %collective-permute-start.68 = (bf16[2,2,128,512]{3,2,1,0:T(8,128)(2,1)S(1)}, bf16[2,2,128,512]{3,2,1,0:T(8,128)(2,1)S(1)}, u32[]{:S(2)}, u32[]{:S(2)}) collective-permute-start(bf16[2,2,128,512]{3,2,1,0:T(8,128)(2,1)S(1)} %pad_maximum_fusion.1.refs_4_), channel_id=1, source_target_pairs={{0,16},{4,20},{8,24},{12,28},{16,0},{20,4},{24,8},{28,12},{1,17},{... | collective-permute-start | bytes 1572872 | tf_op jit(solution)/shard_map/ppermute | solution.py:608
  439.8 20.9 %collective-permute-start.65 = (bf16[2,2,64,640]{3,2,1,0:T(8,128)(2,1)S(1)}, bf16[2,2,64,640]{3,2,1,0:T(8,128)(2,1)S(1)}, u32[]{:S(2)}, u32[]{:S(2)}) collective-permute-start(bf16[2,2,64,640]{3,2,1,0:T(8,128)(2,1)S(1)} %pad_maximum_fusion.7.refs_0_), channel_id=1, source_target_pairs={{0,8},{4,12},{8,0},{12,4},{16,24},{20,28},{24,16},{28,20},{1,9},{5... | collective-permute-start | bytes 983048 | tf_op jit(solution)/shard_map/ppermute | solution.py:608
  440.5 15.9 %collective-permute-start.64 = (bf16[2,64,384]{2,1,0:T(8,128)(2,1)S(1)}, bf16[2,64,384]{2,1,0:T(8,128)(2,1)S(1)}, u32[]{:S(2)}, u32[]{:S(2)}) collective-permute-start(bf16[2,64,384]{2,1,0:T(8,128)(2,1)S(1)} %bitcast.210), channel_id=1, source_target_pairs={{0,8},{4,12},{8,0},{12,4},{16,24},{20,28},{24,16},{28,20},{1,9},{5... | collective-permute-start | bytes 294920 | tf_op jit(solution)/shard_map/ppermute | solution.py:608
  442.0 20.0 %collective-permute-start.73 = (bf16[2,2,128,512]{3,2,1,0:T(8,128)(2,1)S(1)}, bf16[2,2,128,512]{3,2,1,0:T(8,128)(2,1)S(1)}, u32[]{:S(2)}, u32[]{:S(2)}) collective-permute-start(bf16[2,2,128,512]{3,2,1,0:T(8,128)(2,1)S(1)} %pad_maximum_fusion.refs_0_), channel_id=1, source_target_pairs={{0,4},{4,0},{8,12},{12,8},{16,20},{20,16},{24,28},{28,24},{1,5},{5... | collective-permute-start | bytes 1572872 | tf_op jit(solution)/shard_map/ppermute | solution.py:608
  463.7 17.4 %collective-permute-start.69 = (bf16[2,2,64,640]{3,2,1,0:T(8,128)(2,1)S(1)}, bf16[2,2,64,640]{3,2,1,0:T(8,128)(2,1)S(1)}, u32[]{:S(2)}, u32[]{:S(2)}) collective-permute-start(bf16[2,2,64,640]{3,2,1,0:T(8,128)(2,1)S(1)} %pad_maximum_fusion.7.refs_0_), channel_id=1, source_target_pairs={{0,4},{4,0},{8,12},{12,8},{16,20},{20,16},{24,28},{28,24},{1,5},{5... | collective-permute-start | bytes 983048 | tf_op jit(solution)/shard_map/ppermute | solution.py:608
  464.9 16.2 %collective-permute-start.70 = (bf16[2,2,64,640]{3,2,1,0:T(8,128)(2,1)S(1)}, bf16[2,2,64,640]{3,2,1,0:T(8,128)(2,1)}, u32[]{:S(2)}, u32[]{:S(2)}) collective-permute-start(bf16[2,2,64,640]{3,2,1,0:T(8,128)(2,1)S(1)} %collective-permute-done.65.refs_1_), channel_id=1, source_target_pairs={{0,4},{4,0},{8,12},{12,8},{16,20},{20,16},{24,28},{28,24},{1,5},{5... | collective-permute-start | bytes 983048 | tf_op jit(solution)/shard_map/ppermute | solution.py:608
  (83 other events, 708.3 us)
